TPU v7x, 32 devices: a whole 2x2x4 slice. The times are simulated.
32 devices in a mesh: blk: 4 (over x, core), wide: 8 (over z, y).
Axes of the slice: x: 2, y: 2, z: 4, core: 2. Of those that a mesh axis runs over, the one named last changes fastest.
Arguments:
- observed: bfloat16 [8192, 5120], P(('blk', 'wide')), may hold values from -8 to 8
- mask_bits: int32 [8192, 640], P(('blk', 'wide')), may hold values from 0 to 255, as said below
- frame_factors: float32 [8192, 256], P(('blk', 'wide')), may hold values from -2 to 2
- pixel_factors: bfloat16 [32768, 256], P(('blk', 'wide')), may hold values from -2 to 2
Outputs:
- frames_out: float32 [8192, 256], P(('blk', 'wide'))
- pixels_out: bfloat16 [32768, 256], P(('blk', 'wide'))
Inputs may be any that keep to these rules, and one draw needn't show every extreme that they name: `mask_bits`: each word holds 8 independent flags, each set with probability one half.
All inputs are finite; a program needn't handle non-finite values.
Results may differ from a plain program's by a relative error of at most 0.0071.
Values may be sent and summed in bfloat16 or wider, within the bound.
No kernel may reach another device: no remote copies, remote signals or barrier semaphores. Data moves between devices by JAX's collectives and lax.ppermute only.
A program may use at most 64 MiB of HBM per device.

v0:
```python
import jax
import jax.numpy as jnp
from jax import lax
from jax.sharding import PartitionSpec as P

VISITS = 5


clip_level = 1.0
step_frames = 0.01
step_pixels = 0.02
decay_weight = 0.1


def shifted(value, axis, steps):
    count = lax.axis_size(axis)
    pairs = [(source, (source + steps) % count) for source in range(count)]
    return lax.ppermute(value, axis, pairs)


def unpack_mask(packed):
    shifts = jnp.arange(8, dtype=jnp.int32)
    expanded = jnp.bitwise_and(jnp.right_shift(packed[..., None, :], shifts[:, None]), 1)
    return expanded.reshape(packed.shape[:-1] + (8 * packed.shape[-1],)).astype(jnp.float32)


def send_block(block, visit_index):
    if visit_index == VISITS - 2:
        return shifted(block, "wide", 1)
    return block


def body(observed, mask_bits, frame_factors, pixel_factors):
    visible_all = unpack_mask(mask_bits).astype(jnp.bfloat16)
    frames = frame_factors
    pixels = pixel_factors
    width = pixels.shape[0]
    middle = width // 2
    for visit_index in range(VISITS):
        lower = visit_index * width
        wanted = observed[:, lower : lower + width].astype(jnp.float32)
        visible = visible_all[:, lower : lower + width].astype(jnp.float32)
        frames_low = frames.astype(jnp.bfloat16)
        predicted = jnp.dot(frames_low, pixels.T, preferred_element_type=jnp.float32)
        errors = visible * (wanted - predicted)
        weights = clip_level / jnp.maximum(jnp.abs(errors), clip_level)
        scaled = (weights * errors).astype(jnp.bfloat16)

        def pixel_update(first_row, end_row):
            grad = lax.dot_general(
                scaled[:, first_row:end_row],
                frames_low,
                (((0,), (0,)), ((), ())),
                preferred_element_type=jnp.float32,
            )
            current = pixels[first_row:end_row].astype(jnp.float32)
            return (current + step_pixels * (grad - decay_weight * current)).astype(jnp.bfloat16)

        def frame_update():
            grad = jnp.dot(scaled, pixels, preferred_element_type=jnp.float32)
            return frames + step_frames * (grad - decay_weight * frames)

        if visit_index < VISITS - 2:
            upper_half = shifted(pixel_update(0, middle), "blk", 1)
            lower_half = shifted(pixel_update(middle, width), "blk", 1)
            frames = frame_update()
            pixels = jnp.concatenate((upper_half, lower_half), axis=0)
        else:
            new_frames = frame_update()
            moved = send_block(pixel_update(0, width), visit_index)
            frames = new_frames
            pixels = moved
    return (frames, pixels)


def solution(mesh):
    in_specs = (
        P(("blk", "wide"), None),
        P(("blk", "wide"), None),
        P(("blk", "wide"), None),
        P(("blk", "wide"), None),
    )
    out_specs = (P(("blk", "wide"), None), P(("blk", "wide"), None))
    return jax.shard_map(body, mesh=mesh, in_specs=in_specs, out_specs=out_specs, check_vma=False)
```

profile of v0, /device:TPU:0, one launch (start us, length us, event | category | flops | bytes accessed | tf_op | source)
XLA Modules:
  0.0 58.3 jit_solution(18218826369957024551)
XLA Ops:
  0.6 1.4 %shift_right_arithmetic.20 = s32[256,8,640]{2,1,0:T(8,128)S(1)} broadcast(s32[256,640]{1,0:T(8,128)} %param.5), dimensions={0,2} | broadcast | bytes 5898240 | tf_op jit(solution)/shard_map/shift_right_arithmetic | solution.py:23
  2.1 3.2 %copy.6 = s32[32,8,8,640]{3,1,2,0:T(8,128)} copy(s32[32,8,8,640]{3,2,1,0:T(8,128)S(1)} %bitcast.20) | data formatting | bytes 10485760
  5.3 3.3 %convert_convert_fusion = bf16[256,5120]{1,0:T(8,128)(2,1)S(1)} fusion(s32[256,5120]{1,0:T(8,128)} %bitcast.19, s32[5120]{0:T(1024)S(1)} %shift_right_arithmetic.23), kind=kLoop, calls=%fused_computation | loop fusion | flops 5242880 | bytes 7884800 | tf_op jit(solution)/shard_map/convert_element_type | solution.py:34
  8.7 0.2 copy-done.2
  8.8 0.5 multiply_convert_fusion.4
  9.3 0.3 fusion.9
  9.6 0.5 collective-permute-start
  10.1 0.3 fusion.10
  10.4 2.7 %collective-permute-start.1 = (bf16[512,256]{1,0:T(8,128)(2,1)S(1)}, bf16[512,256]{1,0:T(8,128)(2,1)S(1)}, u32[]{:S(2)}, u32[]{:S(2)}) collective-permute-start(bf16[512,256]{1,0:T(8,128)(2,1)S(1)} %fusion.10), channel_id=1, source_target_pairs={{0,8},{8,16},{16,24},{24,0},{1,9},{9,17},{17,25},{25,1},{2,10},{10... | collective-permute-start | bytes 786440 | tf_op jit(solution)/shard_map/ppermute | solution.py:18
  13.1 0.3 fusion.12
  13.4 2.7 %collective-permute-done = bf16[512,256]{1,0:T(8,128)(2,1)S(1)} collective-permute-done((bf16[512,256]{1,0:T(8,128)(2,1)S(1)}, bf16[512,256]{1,0:T(8,128)(2,1)S(1)}, u32[]{:S(2)}, u32[]{:S(2)}) %collective-permute-start) | collective-permute-done | bytes 262176 | tf_op jit(solution)/shard_map/ppermute | solution.py:18
  16.1 2.8 %collective-permute-done.1 = bf16[512,256]{1,0:T(8,128)(2,1)S(1)} collective-permute-done((bf16[512,256]{1,0:T(8,128)(2,1)S(1)}, bf16[512,256]{1,0:T(8,128)(2,1)S(1)}, u32[]{:S(2)}, u32[]{:S(2)}) %collective-permute-start.1) | collective-permute-done | bytes 262176 | tf_op jit(solution)/shard_map/ppermute | solution.py:18
  19.0 0.5 multiply_convert_fusion.3
  19.5 0.3 fusion.32
  19.8 0.3 fusion.29
  20.1 2.5 %collective-permute-start.2 = (bf16[512,256]{1,0:T(8,128)(2,1)S(1)}, bf16[512,256]{1,0:T(8,128)(2,1)S(1)}, u32[]{:S(2)}, u32[]{:S(2)}) collective-permute-start(bf16[512,256]{1,0:T(8,128)(2,1)S(1)} %fusion.29), channel_id=1, source_target_pairs={{0,8},{8,16},{16,24},{24,0},{1,9},{9,17},{17,25},{25,1},{2,10},{10... | collective-permute-start | bytes 786440 | tf_op jit(solution)/shard_map/ppermute | solution.py:18
  22.6 0.3 fusion.14
  22.9 5.5 %collective-permute-done.2 = bf16[512,256]{1,0:T(8,128)(2,1)S(1)} collective-permute-done((bf16[512,256]{1,0:T(8,128)(2,1)S(1)}, bf16[512,256]{1,0:T(8,128)(2,1)S(1)}, u32[]{:S(2)}, u32[]{:S(2)}) %collective-permute-start.2) | collective-permute-done | bytes 262176 | tf_op jit(solution)/shard_map/ppermute | solution.py:18
  28.5 0.5 multiply_convert_fusion.2
  29.0 0.3 fusion.38
  29.3 0.3 fusion.35
  29.6 2.5 %collective-permute-start.4 = (bf16[512,256]{1,0:T(8,128)(2,1)S(1)}, bf16[512,256]{1,0:T(8,128)(2,1)S(1)}, u32[]{:S(2)}, u32[]{:S(2)}) collective-permute-start(bf16[512,256]{1,0:T(8,128)(2,1)S(1)} %fusion.35), channel_id=1, source_target_pairs={{0,8},{8,16},{16,24},{24,0},{1,9},{9,17},{17,25},{25,1},{2,10},{10... | collective-permute-start | bytes 786440 | tf_op jit(solution)/shard_map/ppermute | solution.py:18
  32.1 0.3 fusion.16
  32.4 5.5 %collective-permute-done.4 = bf16[512,256]{1,0:T(8,128)(2,1)S(1)} collective-permute-done((bf16[512,256]{1,0:T(8,128)(2,1)S(1)}, bf16[512,256]{1,0:T(8,128)(2,1)S(1)}, u32[]{:S(2)}, u32[]{:S(2)}) %collective-permute-start.4) | collective-permute-done | bytes 262176 | tf_op jit(solution)/shard_map/ppermute | solution.py:18
  38.0 0.5 multiply_convert_fusion.1
  38.5 0.4 fusion.23
  38.9 2.4 %collective-permute-start.6 = (bf16[1024,256]{1,0:T(8,128)(2,1)S(1)}, bf16[1024,256]{1,0:T(8,128)(2,1)S(1)}, u32[]{:S(2)}, u32[]{:S(2)}) collective-permute-start(bf16[1024,256]{1,0:T(8,128)(2,1)S(1)} %fusion.23), channel_id=1, source_target_pairs={{0,1},{1,2},{2,3},{3,4},{4,5},{5,6},{6,7},{7,0},{8,9},{9,10},{10,1... | collective-permute-start | bytes 1572872 | tf_op jit(solution)/shard_map/ppermute | solution.py:18
  41.3 0.3 fusion.18
  41.6 13.9 %collective-permute-done.6 = bf16[1024,256]{1,0:T(8,128)(2,1)S(1)} collective-permute-done((bf16[1024,256]{1,0:T(8,128)(2,1)S(1)}, bf16[1024,256]{1,0:T(8,128)(2,1)S(1)}, u32[]{:S(2)}, u32[]{:S(2)}) %collective-permute-start.6) | collective-permute-done | bytes 524320 | tf_op jit(solution)/shard_map/ppermute | solution.py:18
  55.5 0.5 multiply_convert_fusion
  56.0 1.2 %fusion.26 = bf16[1024,256]{1,0:T(8,128)(2,1)} fusion(bf16[1024,256]{1,0:T(8,128)(2,1)S(1)} %collective-permute-done.6, bf16[256,1024]{1,0:T(8,128)(2,1)S(1)} %multiply_convert_fusion, f32[256,256]{1,0:T(8,128)S(1)} %fusion.18), kind=kOutput, calls=%fused_computation.43 | convolution fusion | flops 135856128 | bytes 1835008 | tf_op jit(solution)/shard_map/dot_general | solution.py:50
  57.3 1.0 %fusion.20 = f32[256,256]{1,0:T(8,128)} fusion(f32[256,256]{1,0:T(8,128)S(1)} %fusion.18, bf16[256,1024]{1,0:T(8,128)(2,1)S(1)} %multiply_convert_fusion, bf16[1024,256]{1,0:T(8,128)(2,1)S(1)} %collective-permute-done.6), kind=kOutput, calls=%fused_computation.37 | convolution fusion | flops 134479872 | bytes 1572864 | tf_op jit(solution)/shard_map/dot_general | solution.py:60
  (17 shorter events, 0.3 us)
Async XLA Ops:
  5.3 3.4 %copy-start = (bf16[1024,256]{1,0:T(8,128)(2,1)S(1)}, bf16[1024,256]{1,0:T(8,128)(2,1)}, u32[]{:S(2)}) copy-start(bf16[1024,256]{1,0:T(8,128)(2,1)} %param.7) | copy-start | bytes 1572868
  5.3 3.4 %copy-start.1 = (f32[256,256]{1,0:T(8,128)S(1)}, f32[256,256]{1,0:T(8,128)}, u32[]{:S(2)}) copy-start(f32[256,256]{1,0:T(8,128)} %param.6) | copy-start | bytes 786436
  5.3 3.5 %copy-start.2 = (bf16[256,5120]{1,0:T(8,128)(2,1)S(1)}, bf16[256,5120]{1,0:T(8,128)(2,1)}, u32[]{:S(2)}) copy-start(bf16[256,5120]{1,0:T(8,128)(2,1)} %param.4) | copy-start | bytes 7864324
  9.6 6.5 %collective-permute-start = (bf16[512,256]{1,0:T(8,128)(2,1)S(1)}, bf16[512,256]{1,0:T(8,128)(2,1)S(1)}, u32[]{:S(2)}, u32[]{:S(2)}) collective-permute-start(bf16[512,256]{1,0:T(8,128)(2,1)S(1)} %fusion.9), channel_id=1, source_target_pairs={{0,8},{8,16},{16,24},{24,0},{1,9},{9,17},{17,25},{25,1},{2,10},{10... | collective-permute-start | bytes 786440 | tf_op jit(solution)/shard_map/ppermute | solution.py:18
  10.4 8.5 %collective-permute-start.1 = (bf16[512,256]{1,0:T(8,128)(2,1)S(1)}, bf16[512,256]{1,0:T(8,128)(2,1)S(1)}, u32[]{:S(2)}, u32[]{:S(2)}) collective-permute-start(bf16[512,256]{1,0:T(8,128)(2,1)S(1)} %fusion.10), channel_id=1, source_target_pairs={{0,8},{8,16},{16,24},{24,0},{1,9},{9,17},{17,25},{25,1},{2,10},{10... | collective-permute-start | bytes 786440 | tf_op jit(solution)/shard_map/ppermute | solution.py:18
  19.7 8.7 %collective-permute-start.3 = (bf16[512,256]{1,0:T(8,128)(2,1)S(1)}, bf16[512,256]{1,0:T(8,128)(2,1)S(1)}, u32[]{:S(2)}, u32[]{:S(2)}) collective-permute-start(bf16[512,256]{1,0:T(8,128)(2,1)S(1)} %fusion.32), channel_id=1, source_target_pairs={{0,8},{8,16},{16,24},{24,0},{1,9},{9,17},{17,25},{25,1},{2,10},{10... | collective-permute-start | bytes 786440 | tf_op jit(solution)/shard_map/ppermute | solution.py:18
  20.1 8.3 %collective-permute-start.2 = (bf16[512,256]{1,0:T(8,128)(2,1)S(1)}, bf16[512,256]{1,0:T(8,128)(2,1)S(1)}, u32[]{:S(2)}, u32[]{:S(2)}) collective-permute-start(bf16[512,256]{1,0:T(8,128)(2,1)S(1)} %fusion.29), channel_id=1, source_target_pairs={{0,8},{8,16},{16,24},{24,0},{1,9},{9,17},{17,25},{25,1},{2,10},{10... | collective-permute-start | bytes 786440 | tf_op jit(solution)/shard_map/ppermute | solution.py:18
  29.3 8.7 %collective-permute-start.5 = (bf16[512,256]{1,0:T(8,128)(2,1)S(1)}, bf16[512,256]{1,0:T(8,128)(2,1)S(1)}, u32[]{:S(2)}, u32[]{:S(2)}) collective-permute-start(bf16[512,256]{1,0:T(8,128)(2,1)S(1)} %fusion.38), channel_id=1, source_target_pairs={{0,8},{8,16},{16,24},{24,0},{1,9},{9,17},{17,25},{25,1},{2,10},{10... | collective-permute-start | bytes 786440 | tf_op jit(solution)/shard_map/ppermute | solution.py:18
  29.6 8.3 %collective-permute-start.4 = (bf16[512,256]{1,0:T(8,128)(2,1)S(1)}, bf16[512,256]{1,0:T(8,128)(2,1)S(1)}, u32[]{:S(2)}, u32[]{:S(2)}) collective-permute-start(bf16[512,256]{1,0:T(8,128)(2,1)S(1)} %fusion.35), channel_id=1, source_target_pairs={{0,8},{8,16},{16,24},{24,0},{1,9},{9,17},{17,25},{25,1},{2,10},{10... | collective-permute-start | bytes 786440 | tf_op jit(solution)/shard_map/ppermute | solution.py:18
  38.9 16.6 %collective-permute-start.6 = (bf16[1024,256]{1,0:T(8,128)(2,1)S(1)}, bf16[1024,256]{1,0:T(8,128)(2,1)S(1)}, u32[]{:S(2)}, u32[]{:S(2)}) collective-permute-start(bf16[1024,256]{1,0:T(8,128)(2,1)S(1)} %fusion.23), channel_id=1, source_target_pairs={{0,1},{1,2},{2,3},{3,4},{4,5},{5,6},{6,7},{7,0},{8,9},{9,10},{10,1... | collective-permute-start | bytes 1572872 | tf_op jit(solution)/shard_map/ppermute | solution.py:18
where the time goes:
time: 58.4 us; the launch traced here: 58.3 us
  waiting for transfers between devices  30.5 us (52%)
  starting transfers between devices  10.6 us (18%)
  matrix products  8.04 us (14%)
  local copies, waits for them, and re-layouts  4.94 us (8%)
  other arithmetic  3.32 us (6%)
  between operations  0.87 us (1%)
    ppermute x7, waiting for transfers between devices, shifted(): return lax.ppermute(value, axis, pairs)  30.5 us
    ppermute x7, starting transfers between devices, shifted(): return lax.ppermute(value, axis, pairs)  10.6 us
    unnamed x10, local copies, waits for them, and re-layouts  3.45 us
    dot_general x8, matrix products, pixel_update(): lax.dot_general(scaled[:, first_row:end_row], frames_low, (((0,), (0,)),...  3.33 us
    convert_element_type x1, other arithmetic, body(): visible_all = unpack_mask(mask_bits).astype(jnp.bfloat16)  3.32 us
    dot_general x5, matrix products, body(): jnp.dot(frames_low, pixels.T, preferred_element_type=jnp.float32)  2.49 us
    dot_general x5, matrix products, frame_update(): grad = jnp.dot(scaled, pixels, preferred_element_type=jnp.float32)  2.21 us
    shift_right_arithmetic x3, local copies, waits for them, and re-layouts, unpack_mask(): jnp.right_shift(packed[..., None, :], shifts[:, None])  1.44 us
  transfers between devices with their start and end apart: 7, of which 5 were waited for; matrix products, arithmetic and copies ran while one was open for 4% of the time, Pallas kernels for 0%

commit v1 on v0

v1 whole, which is shorter than its diff:
```python
import jax
import jax.numpy as jnp
from jax import lax
from jax.experimental import pallas as pl
from jax.experimental.pallas import tpu as pltpu
from jax.sharding import PartitionSpec as P

CHUNKS = 4

step_frames = 0.01
step_pixels = 0.02
decay_weight = 0.1

VMEM = pl.BlockSpec(memory_space=pltpu.VMEM)
HBM = pl.BlockSpec(memory_space=pltpu.HBM)


def shifted(value, axis):
    count = lax.axis_size(axis)
    return lax.ppermute(value, axis, [(s, (s + 1) % count) for s in range(count)])


def flags(bits, lower, count):
    words = bits.shape[1]
    pieces = []
    at = lower
    while at < lower + count:
        flag, word = divmod(at, words)
        size = min(words - word, lower + count - at)
        pieces.append(lax.shift_right_logical(bits[:, word : word + size], flag) & 1)
        at += size
    return pieces[0] if len(pieces) == 1 else jnp.concatenate(pieces, axis=1)


def tile(lower, first, frames, done, observed, bits, block):
    count = block.shape[0]
    frames_low = frames.astype(jnp.bfloat16)
    predicted = lax.dot_general(
        frames_low, block, (((1,), (1,)), ((), ())), preferred_element_type=jnp.float32
    )
    errors = observed[:, lower : lower + count].astype(jnp.float32) - predicted
    clipped = jnp.clip(errors, -1.0, 1.0)
    scaled = jnp.where(flags(bits, lower, count) != 0, clipped, 0.0).astype(jnp.bfloat16)
    grad_pixels = lax.dot_general(
        scaled, frames_low, (((0,), (0,)), ((), ())), preferred_element_type=jnp.float32
    )
    current = block.astype(jnp.float32)
    new = (current + step_pixels * (grad_pixels - decay_weight * current)).astype(jnp.bfloat16)
    grad_frames = jnp.dot(scaled, block, preferred_element_type=jnp.float32)
    if first:
        return new, frames + step_frames * (grad_frames - decay_weight * frames)
    return new, done + step_frames * grad_frames


def cost(observed, count, rank):
    return pl.CostEstimate(flops=0, bytes_accessed=0, transcendentals=0)


def params():
    return pltpu.CompilerParams(vmem_limit_bytes=24 * 1024 * 1024)


def load_kernel(width, size, observed, mask_bits, frames, pixels, observed_v, bits_v, pixels_v, state, new, sems):
    copies = [
        pltpu.make_async_copy(frames, state.at[0], sems.at[0]),
        pltpu.make_async_copy(pixels, pixels_v, sems.at[1]),
        pltpu.make_async_copy(mask_bits, bits_v, sems.at[2]),
        pltpu.make_async_copy(observed.at[:, :width], observed_v.at[:, :width], sems.at[3]),
    ]
    for copy in copies:
        copy.start()
    for copy in copies:
        copy.wait()
    new[...], state[1] = tile(0, True, state[0], None, observed_v, bits_v, pixels_v[:size])


def rest_kernel(width, chunk, size, observed, bits, pixels, state, observed_in, new, state_out, observed_v, sem):
    del observed_in
    copy = pltpu.make_async_copy(observed.at[:, width:], observed_v.at[:, width:], sem)
    copy.start()
    rows = slice(chunk * size, (chunk + 1) * size)
    new[...], state_out[1] = tile(
        chunk * size, False, state[0], state[1], observed_v, bits, pixels[rows]
    )
    copy.wait()


def step_kernel(lower, first, old, rows, observed, bits, block, state, new, state_out):
    new[...], state_out[1 - old] = tile(
        lower, first, state[old], None if first else state[1 - old], observed, bits, block[rows]
    )


def last_kernel(lower, first, last, old, at, size, observed, bits, block, state, pixels_in, *refs):
    del pixels_in
    if last:
        state_out, pixels_out, frames_out, held, sem, sem2 = refs
    else:
        state_out, pixels_out, held, sem = refs
    held[...], done = tile(
        lower, first, state[old], None if first else state[1 - old], observed, bits, block[...]
    )
    copy = pltpu.make_async_copy(held, pixels_out.at[at : at + size], sem)
    copy.start()
    state_out[1 - old] = done
    if last:
        copy2 = pltpu.make_async_copy(state_out.at[1 - old], frames_out, sem2)
        copy2.start()
        copy2.wait()
    copy.wait()


def struct(shape, dtype):
    return jax.ShapeDtypeStruct(shape, dtype)


def body(observed, mask_bits, frame_factors, pixel_factors):
    width, rank = pixel_factors.shape
    visits = observed.shape[1] // width
    size = width // CHUNKS
    chunk_shape = struct((size, rank), jnp.bfloat16)
    state_shape = struct((2,) + frame_factors.shape, jnp.float32)
    observed_shape = struct(observed.shape, observed.dtype)
    dma = pltpu.SemaphoreType.DMA

    def call(kernel, **kw):
        return pl.pallas_call(
            kernel, compiler_params=params(), cost_estimate=cost(observed, size, rank), **kw
        )

    def first_kernel(*refs):
        load_kernel(width, size, *refs)

    observed_v, bits, block, state, new = call(
        first_kernel,
        out_shape=(
            observed_shape,
            struct(mask_bits.shape, mask_bits.dtype),
            struct(pixel_factors.shape, pixel_factors.dtype),
            state_shape,
            chunk_shape,
        ),
        in_specs=[HBM] * 4,
        out_specs=(VMEM,) * 5,
        scratch_shapes=[dma((4,))],
    )(observed, mask_bits, frame_factors, pixel_factors)
    coming = [shifted(new, "blk")]

    def second_kernel(*refs):
        rest_kernel(width, 1, size, *refs)

    new, state, observed_v = call(
        second_kernel,
        out_shape=(chunk_shape, state_shape, observed_shape),
        in_specs=[HBM] + [VMEM] * 4,
        out_specs=(VMEM,) * 3,
        scratch_shapes=[dma],
        input_output_aliases={3: 1, 4: 2},
    )(observed, bits, block, state, observed_v)
    coming.append(shifted(new, "blk"))

    def step(visit, chunk, block, state, rows):
        def kernel(*refs):
            step_kernel(visit * width + chunk * size, chunk == 0, visit % 2, rows, *refs)

        return call(
            kernel,
            out_shape=(chunk_shape, state_shape),
            in_specs=[VMEM] * 4,
            out_specs=(VMEM,) * 2,
            input_output_aliases={3: 1},
        )(observed_v, bits, block, state)

    for c in range(2, CHUNKS):
        new, state = step(0, c, block, state, slice(c * size, (c + 1) * size))
        coming.append(shifted(new, "blk"))

    for visit in range(1, visits - 1):
        axis = "blk" if visit < visits - 2 else "wide"
        sent = []
        for c in range(CHUNKS):
            new, state = step(visit, c, coming[c], state, slice(None))
            sent.append(shifted(new, axis))
        coming = sent

    visit = visits - 1
    pixels_out = None
    for c in range(CHUNKS):
        last = c == CHUNKS - 1

        def kernel(*refs, c=c, last=last):
            if c == 0:
                refs = refs[:4] + (None,) + refs[4:]
            last_kernel(visit * width + c * size, c == 0, last, visit % 2, c * size, size, *refs)

        out_shape = [state_shape, struct(pixel_factors.shape, pixel_factors.dtype)]
        out_specs = [VMEM, HBM]
        scratch = [pltpu.VMEM((size, rank), jnp.bfloat16), dma]
        if last:
            out_shape.append(struct(frame_factors.shape, jnp.float32))
            out_specs.append(HBM)
            scratch.append(dma)
        args = [observed_v, bits, coming[c], state]
        specs = [VMEM] * 4
        aliases = {3: 0}
        if c:
            args.append(pixels_out)
            specs.append(HBM)
            aliases[4] = 1
        outs = call(
            kernel,
            out_shape=tuple(out_shape),
            in_specs=specs,
            out_specs=tuple(out_specs),
            scratch_shapes=scratch,
            input_output_aliases=aliases,
        )(*args)
        state, pixels_out = outs[:2]
    return outs[2], pixels_out


def solution(mesh):
    spec = P(("blk", "wide"), None)
    return jax.shard_map(
        body, mesh=mesh, in_specs=(spec,) * 4, out_specs=(spec, spec), check_vma=False
    )
```

time: 58.4 us -> 43.2 us (0.74)
  waiting for transfers between devices: 30.5 us -> 7.27 us
  Pallas kernels: 0 us -> 14.3 us
  matrix products: 8.04 us -> 0 us
  starting transfers between devices: 10.6 us -> 15.7 us
  other arithmetic: 3.32 us -> 0 us
    ppermute x7 -> x16, waiting for transfers between devices: 30.5 us -> 7.27 us  [shifted(): lax.ppermute(value, axis, [(s, (s + 1) % count) for s in range(count)])]
    pallas_call x0 -> x20, Pallas kernels: none -> 14.3 us  [the longest x14 8.06 us: step(): call(kernel, out_shape=(chunk_shape, state_shape), in_specs=[VMEM] * 4, o...]
    dot_general x18 -> x0, matrix products: 8.04 us -> none  [the longest x8 3.33 us: pixel_update(): lax.dot_general(scaled[:, first_row:end_row], frames_low, (((0,), (0,)),...]
    ppermute x7 -> x16, starting transfers between devices: 10.6 us -> 15.7 us  [shifted(): lax.ppermute(value, axis, [(s, (s + 1) % count) for s in range(count)])]
    convert_element_type x1 -> x0, other arithmetic: 3.32 us -> none  [body(): visible_all = unpack_mask(mask_bits).astype(jnp.bfloat16)]
    shift_right_arithmetic x3 -> x0, local copies, waits for them, and re-layouts: 1.44 us -> none  [unpack_mask(): jnp.right_shift(packed[..., None, :], shifts[:, None])]
    unnamed x10 -> x8, local copies, waits for them, and re-layouts: 3.45 us -> 4.81 us
  transfers between devices with their start and end apart: 7 -> 16, of which waited for: 5 -> 9; matrix products, arithmetic and copies ran while one was open for 4% -> 0% of each run, Pallas kernels for 0% -> 28%
where the time goes in v1:
time: 43.2 us; the launch traced here: 42.9 us
  starting transfers between devices  15.7 us (36%)
  Pallas kernels  14.3 us (33%)
  waiting for transfers between devices  7.27 us (17%)
  local copies, waits for them, and re-layouts  4.81 us (11%)
  between operations  0.8 us (2%)
    ppermute x16, starting transfers between devices, shifted(): lax.ppermute(value, axis, [(s, (s + 1) % count) for s in range(count)])  15.7 us
    pallas_call x14, Pallas kernels, step(): call(kernel, out_shape=(chunk_shape, state_shape), in_specs=[VMEM] * 4, o...  8.06 us
    ppermute x16, waiting for transfers between devices, shifted(): lax.ppermute(value, axis, [(s, (s + 1) % count) for s in range(count)])  7.27 us
    unnamed x8, local copies, waits for them, and re-layouts  4.81 us
    pallas_call x4, Pallas kernels, body(): call(kernel, out_shape=tuple(out_shape), in_specs=specs, out_specs=tuple(...  4.7 us
    pallas_call x1, Pallas kernels, body(): call(first_kernel, out_shape=(observed_shape, struct(mask_bits.shape, mas...  0.88 us
  transfers between devices with their start and end apart: 16, of which 9 were waited for; matrix products, arithmetic and copies ran while one was open for 0% of the time, Pallas kernels for 28%

profile of v1, /device:TPU:0, one launch (start us, length us, event | category | flops | bytes accessed | tf_op | source)
XLA Modules:
  0.0 42.9 jit_solution(4111856091456859556)
XLA Ops:
  0.6 1.7 %copy-done = bf16[256,5120]{1,0:T(8,128)(2,1)S(1)} copy-done((bf16[256,5120]{1,0:T(8,128)(2,1)S(1)}, bf16[256,5120]{1,0:T(8,128)(2,1)}, u32[]{:S(2)}) %copy-start) | copy-done | bytes 2621464
  2.4 1.1 %copy-done.1 = s32[256,640]{1,0:T(8,128)S(1)} copy-done((s32[256,640]{1,0:T(8,128)S(1)}, s32[256,640]{1,0:T(8,128)}, u32[]{:S(2)}) %copy-start.1) | copy-done | bytes 655384
  3.5 1.0 %copy-done.2 = bf16[1024,256]{1,0:T(8,128)(2,1)S(1)} copy-done((bf16[1024,256]{1,0:T(8,128)(2,1)S(1)}, bf16[1024,256]{1,0:T(8,128)(2,1)}, u32[]{:S(2)}) %copy-start.2) | copy-done | bytes 524312
  4.5 0.9 %copy-done.3 = f32[256,256]{1,0:T(8,128)S(1)} copy-done((f32[256,256]{1,0:T(8,128)S(1)}, f32[256,256]{1,0:T(8,128)}, u32[]{:S(2)}) %copy-start.3) | copy-done | bytes 262168
  5.5 0.9 %shard_map.59 = (bf16[256,5120]{1,0:T(8,128)(2,1)S(1)}, s32[256,640]{1,0:T(8,128)S(1)}, bf16[1024,256]{1,0:T(8,128)(2,1)S(1)}, f32[2,256,256]{2,1,0:T(8,128)S(1)}, bf16[256,256]{1,0:T(8,128)(2,1)S(1)}) custom-call(bf16[256,5120]{1,0:T(8,128)(2,1)S(1)} %copy-done, s32[256,640]{1,0:T(8,128)S(1)} %copy-done.1, f32[256,256]{1,0:T(8,128)S(1)} %copy-done.3, ...), custom_call_target="tpu_custom_call" | custom-call | tf_op jit(solution)/shard_map/pallas_call | solution.py:134
  6.8 0.7 %shard_map.60 = (bf16[256,256]{1,0:T(8,128)(2,1)S(1)}, f32[2,256,256]{2,1,0:T(8,128)S(1)}, bf16[256,5120]{1,0:T(8,128)(2,1)S(1)}) custom-call(bf16[256,5120]{1,0:T(8,128)(2,1)S(1)} %copy-done, s32[256,640]{1,0:T(8,128)S(1)} %get-tuple-element.46.refs_1_, ...), custom_call_target="tpu_custom_call", output_to_operand_aliasing={{1}: (3, {}), {2}: (4, {})} | custom-call | tf_op jit(solution)/shard_map/pallas_call | solution.py:152
  7.6 2.7 %collective-permute-start.2 = (bf16[256,256]{1,0:T(8,128)(2,1)S(1)}, bf16[256,256]{1,0:T(8,128)(2,1)S(1)}, u32[]{:S(2)}, u32[]{:S(2)}) collective-permute-start(bf16[256,256]{1,0:T(8,128)(2,1)S(1)} %get-tuple-element.55), channel_id=1, source_target_pairs={{0,8},{8,16},{16,24},{24,0},{1,9},{9,17},{17,25},{25,1},{2,10},{10... | collective-permute-start | bytes 393224 | tf_op jit(solution)/shard_map/ppermute | solution.py:20
  10.2 0.6 %shard_map.61 = (bf16[256,256]{1,0:T(8,128)(2,1)S(1)}, f32[2,256,256]{2,1,0:T(8,128)S(1)}) custom-call(bf16[256,5120]{1,0:T(8,128)(2,1)S(1)} %get-tuple-element.50.refs_0_, s32[256,640]{1,0:T(8,128)S(1)} %get-tuple-element.46.refs_1_, bf16[1024,256]{1,0:T(8,128)(2,1)S(1)} %get-tuple-element.47.refs_2_, ...), custom_call_target="tpu_custom_call", output_to_operand_aliasing={{1}: (3, {})} | custom-call | tf_op jit(solution)/shard_map/pallas_call | solution.py:166
  11.5 0.7 %shard_map.63 = (bf16[256,256]{1,0:T(8,128)(2,1)S(1)}, f32[2,256,256]{2,1,0:T(8,128)S(1)}) custom-call(bf16[256,5120]{1,0:T(8,128)(2,1)S(1)} %get-tuple-element.50.refs_0_, s32[256,640]{1,0:T(8,128)S(1)} %get-tuple-element.46.refs_1_, bf16[256,256]{1,0:T(8,128)(2,1)S(1)} %collective-permute-done.3.refs_2_, ...), custom_call_target="tpu_custom_call", output_to_operand_aliasing={{1}: (3, {})} | custom-call | tf_op jit(solution)/shard_map/pallas_call | solution.py:166
  12.2 0.6 %collective-permute-done.2.refs_2_ = bf16[256,256]{1,0:T(8,128)(2,1)S(1)} collective-permute-done((bf16[256,256]{1,0:T(8,128)(2,1)S(1)}, bf16[256,256]{1,0:T(8,128)(2,1)S(1)}, u32[]{:S(2)}, u32[]{:S(2)}) %collective-permute-start.2) | collective-permute-done | bytes 131104 | tf_op jit(solution)/shard_map/ppermute | solution.py:20
  13.4 1.8 %collective-permute-start.6 = (bf16[256,256]{1,0:T(8,128)(2,1)S(1)}, bf16[256,256]{1,0:T(8,128)(2,1)S(1)}, u32[]{:S(2)}, u32[]{:S(2)}) collective-permute-start(bf16[256,256]{1,0:T(8,128)(2,1)S(1)} %get-tuple-element.63), channel_id=1, source_target_pairs={{0,8},{8,16},{16,24},{24,0},{1,9},{9,17},{17,25},{25,1},{2,10},{10... | collective-permute-start | bytes 393224 | tf_op jit(solution)/shard_map/ppermute | solution.py:20
  15.8 0.7 %collective-permute-start.5 = (bf16[256,256]{1,0:T(8,128)(2,1)S(1)}, bf16[256,256]{1,0:T(8,128)(2,1)S(1)}, u32[]{:S(2)}, u32[]{:S(2)}) collective-permute-start(bf16[256,256]{1,0:T(8,128)(2,1)S(1)} %get-tuple-element.62), channel_id=1, source_target_pairs={{0,8},{8,16},{16,24},{24,0},{1,9},{9,17},{17,25},{25,1},{2,10},{10... | collective-permute-start | bytes 393224 | tf_op jit(solution)/shard_map/ppermute | solution.py:20
  17.2 0.7 %collective-permute-start.4 = (bf16[256,256]{1,0:T(8,128)(2,1)S(1)}, bf16[256,256]{1,0:T(8,128)(2,1)S(1)}, u32[]{:S(2)}, u32[]{:S(2)}) collective-permute-start(bf16[256,256]{1,0:T(8,128)(2,1)S(1)} %get-tuple-element.61), channel_id=1, source_target_pairs={{0,8},{8,16},{16,24},{24,0},{1,9},{9,17},{17,25},{25,1},{2,10},{10... | collective-permute-start | bytes 393224 | tf_op jit(solution)/shard_map/ppermute | solution.py:20
  18.0 0.7 %shard_map.67 = (bf16[256,256]{1,0:T(8,128)(2,1)S(1)}, f32[2,256,256]{2,1,0:T(8,128)S(1)}) custom-call(bf16[256,5120]{1,0:T(8,128)(2,1)S(1)} %get-tuple-element.50.refs_0_, s32[256,640]{1,0:T(8,128)S(1)} %get-tuple-element.46.refs_1_, bf16[256,256]{1,0:T(8,128)(2,1)S(1)} %collective-permute-done.7.refs_2_, ...), custom_call_target="tpu_custom_call", output_to_operand_aliasing={{1}: (3, {})} | custom-call | tf_op jit(solution)/shard_map/pallas_call | solution.py:166
  18.7 0.7 %collective-permute-start.11 = (bf16[256,256]{1,0:T(8,128)(2,1)S(1)}, bf16[256,256]{1,0:T(8,128)(2,1)S(1)}, u32[]{:S(2)}, u32[]{:S(2)}) collective-permute-start(bf16[256,256]{1,0:T(8,128)(2,1)S(1)} %get-tuple-element.72), channel_id=1, source_target_pairs={{0,8},{8,16},{16,24},{24,0},{1,9},{9,17},{17,25},{25,1},{2,10},{10... | collective-permute-start | bytes 393224 | tf_op jit(solution)/shard_map/ppermute | solution.py:20
  20.0 0.8 %collective-permute-start.10 = (bf16[256,256]{1,0:T(8,128)(2,1)S(1)}, bf16[256,256]{1,0:T(8,128)(2,1)S(1)}, u32[]{:S(2)}, u32[]{:S(2)}) collective-permute-start(bf16[256,256]{1,0:T(8,128)(2,1)S(1)} %get-tuple-element.71), channel_id=1, source_target_pairs={{0,8},{8,16},{16,24},{24,0},{1,9},{9,17},{17,25},{25,1},{2,10},{10... | collective-permute-start | bytes 393224 | tf_op jit(solution)/shard_map/ppermute | solution.py:20
  21.4 0.7 %collective-permute-start.9 = (bf16[256,256]{1,0:T(8,128)(2,1)S(1)}, bf16[256,256]{1,0:T(8,128)(2,1)S(1)}, u32[]{:S(2)}, u32[]{:S(2)}) collective-permute-start(bf16[256,256]{1,0:T(8,128)(2,1)S(1)} %get-tuple-element.70), channel_id=1, source_target_pairs={{0,8},{8,16},{16,24},{24,0},{1,9},{9,17},{17,25},{25,1},{2,10},{10... | collective-permute-start | bytes 393224 | tf_op jit(solution)/shard_map/ppermute | solution.py:20
  22.8 0.7 %collective-permute-start.8 = (bf16[256,256]{1,0:T(8,128)(2,1)S(1)}, bf16[256,256]{1,0:T(8,128)(2,1)S(1)}, u32[]{:S(2)}, u32[]{:S(2)}) collective-permute-start(bf16[256,256]{1,0:T(8,128)(2,1)S(1)} %get-tuple-element.69), channel_id=1, source_target_pairs={{0,8},{8,16},{16,24},{24,0},{1,9},{9,17},{17,25},{25,1},{2,10},{10... | collective-permute-start | bytes 393224 | tf_op jit(solution)/shard_map/ppermute | solution.py:20
  23.6 0.7 %shard_map.71 = (bf16[256,256]{1,0:T(8,128)(2,1)S(1)}, f32[2,256,256]{2,1,0:T(8,128)S(1)}) custom-call(bf16[256,5120]{1,0:T(8,128)(2,1)S(1)} %get-tuple-element.50.refs_0_, s32[256,640]{1,0:T(8,128)S(1)} %get-tuple-element.46.refs_1_, bf16[256,256]{1,0:T(8,128)(2,1)S(1)} %collective-permute-done.11.refs_2_, ...), custom_call_target="tpu_custom_call", output_to_operand_aliasing={{1}: (3, {})} | custom-call | tf_op jit(solution)/shard_map/pallas_call | solution.py:166
  24.3 1.6 %collective-permute-start.15 = (bf16[256,256]{1,0:T(8,128)(2,1)S(1)}, bf16[256,256]{1,0:T(8,128)(2,1)S(1)}, u32[]{:S(2)}, u32[]{:S(2)}) collective-permute-start(bf16[256,256]{1,0:T(8,128)(2,1)S(1)} %get-tuple-element.80), channel_id=1, source_target_pairs={{0,1},{1,2},{2,3},{3,4},{4,5},{5,6},{6,7},{7,0},{8,9},{9,10},{10,1... | collective-permute-start | bytes 393224 | tf_op jit(solution)/shard_map/ppermute | solution.py:20
  26.4 1.6 %collective-permute-start.14 = (bf16[256,256]{1,0:T(8,128)(2,1)S(1)}, bf16[256,256]{1,0:T(8,128)(2,1)S(1)}, u32[]{:S(2)}, u32[]{:S(2)}) collective-permute-start(bf16[256,256]{1,0:T(8,128)(2,1)S(1)} %get-tuple-element.79), channel_id=1, source_target_pairs={{0,1},{1,2},{2,3},{3,4},{4,5},{5,6},{6,7},{7,0},{8,9},{9,10},{10,1... | collective-permute-start | bytes 393224 | tf_op jit(solution)/shard_map/ppermute | solution.py:20
  28.6 1.6 %collective-permute-start.13 = (bf16[256,256]{1,0:T(8,128)(2,1)S(1)}, bf16[256,256]{1,0:T(8,128)(2,1)S(1)}, u32[]{:S(2)}, u32[]{:S(2)}) collective-permute-start(bf16[256,256]{1,0:T(8,128)(2,1)S(1)} %get-tuple-element.78), channel_id=1, source_target_pairs={{0,1},{1,2},{2,3},{3,4},{4,5},{5,6},{6,7},{7,0},{8,9},{9,10},{10,1... | collective-permute-start | bytes 393224 | tf_op jit(solution)/shard_map/ppermute | solution.py:20
  30.2 0.6 %shard_map.74 = (bf16[256,256]{1,0:T(8,128)(2,1)S(1)}, f32[2,256,256]{2,1,0:T(8,128)S(1)}) custom-call(bf16[256,5120]{1,0:T(8,128)(2,1)S(1)} %get-tuple-element.50.refs_0_, s32[256,640]{1,0:T(8,128)S(1)} %get-tuple-element.46.refs_1_, bf16[256,256]{1,0:T(8,128)(2,1)S(1)} %collective-permute-done.8.refs_2_, ...), custom_call_target="tpu_custom_call", output_to_operand_aliasing={{1}: (3, {})} | custom-call | tf_op jit(solution)/shard_map/pallas_call | solution.py:166
  30.7 1.6 %collective-permute-start.12 = (bf16[256,256]{1,0:T(8,128)(2,1)S(1)}, bf16[256,256]{1,0:T(8,128)(2,1)S(1)}, u32[]{:S(2)}, u32[]{:S(2)}) collective-permute-start(bf16[256,256]{1,0:T(8,128)(2,1)S(1)} %get-tuple-element.77), channel_id=1, source_target_pairs={{0,1},{1,2},{2,3},{3,4},{4,5},{5,6},{6,7},{7,0},{8,9},{9,10},{10,1... | collective-permute-start | bytes 393224 | tf_op jit(solution)/shard_map/ppermute | solution.py:20
  32.3 1.1 %collective-permute-done.15.refs_2_ = bf16[256,256]{1,0:T(8,128)(2,1)S(1)} collective-permute-done((bf16[256,256]{1,0:T(8,128)(2,1)S(1)}, bf16[256,256]{1,0:T(8,128)(2,1)S(1)}, u32[]{:S(2)}, u32[]{:S(2)}) %collective-permute-start.15) | collective-permute-done | bytes 131104 | tf_op jit(solution)/shard_map/ppermute | solution.py:20
  33.4 1.1 %shard_map.75 = (f32[2,256,256]{2,1,0:T(8,128)S(1)}, bf16[1024,256]{1,0:T(8,128)(2,1)}) custom-call(bf16[256,5120]{1,0:T(8,128)(2,1)S(1)} %get-tuple-element.50.refs_0_, s32[256,640]{1,0:T(8,128)S(1)} %get-tuple-element.46.refs_1_, bf16[256,256]{1,0:T(8,128)(2,1)S(1)} %collective-permute-done.15.refs_2_, ...), custom_call_target="tpu_custom_call", output_to_operand_aliasing={{0}: (3, {})} | custom-call | tf_op jit(solution)/shard_map/pallas_call | solution.py:210
  34.6 1.7 %collective-permute-done.14.refs_2_ = bf16[256,256]{1,0:T(8,128)(2,1)S(1)} collective-permute-done((bf16[256,256]{1,0:T(8,128)(2,1)S(1)}, bf16[256,256]{1,0:T(8,128)(2,1)S(1)}, u32[]{:S(2)}, u32[]{:S(2)}) %collective-permute-start.14) | collective-permute-done | bytes 131104 | tf_op jit(solution)/shard_map/ppermute | solution.py:20
  36.2 1.1 %shard_map.76 = (f32[2,256,256]{2,1,0:T(8,128)S(1)}, bf16[1024,256]{1,0:T(8,128)(2,1)}) custom-call(bf16[256,5120]{1,0:T(8,128)(2,1)S(1)} %get-tuple-element.50.refs_0_, s32[256,640]{1,0:T(8,128)S(1)} %get-tuple-element.46.refs_1_, bf16[256,256]{1,0:T(8,128)(2,1)S(1)} %collective-permute-done.14.refs_2_, ...), custom_call_target="tpu_custom_call", output_to_operand_aliasing={{0}: (3, {}), {1}: (4, {})} | custom-call | tf_op jit(solution)/shard_map/pallas_call | solution.py:210
  37.4 1.7 %collective-permute-done.13.refs_2_ = bf16[256,256]{1,0:T(8,128)(2,1)S(1)} collective-permute-done((bf16[256,256]{1,0:T(8,128)(2,1)S(1)}, bf16[256,256]{1,0:T(8,128)(2,1)S(1)}, u32[]{:S(2)}, u32[]{:S(2)}) %collective-permute-start.13) | collective-permute-done | bytes 131104 | tf_op jit(solution)/shard_map/ppermute | solution.py:20
  39.0 1.1 %shard_map.77 = (f32[2,256,256]{2,1,0:T(8,128)S(1)}, bf16[1024,256]{1,0:T(8,128)(2,1)}) custom-call(bf16[256,5120]{1,0:T(8,128)(2,1)S(1)} %get-tuple-element.50.refs_0_, s32[256,640]{1,0:T(8,128)S(1)} %get-tuple-element.46.refs_1_, bf16[256,256]{1,0:T(8,128)(2,1)S(1)} %collective-permute-done.13.refs_2_, ...), custom_call_target="tpu_custom_call", output_to_operand_aliasing={{0}: (3, {}), {1}: (4, {})} | custom-call | tf_op jit(solution)/shard_map/pallas_call | solution.py:210
  40.2 1.5 %collective-permute-done.12.refs_2_ = bf16[256,256]{1,0:T(8,128)(2,1)S(1)} collective-permute-done((bf16[256,256]{1,0:T(8,128)(2,1)S(1)}, bf16[256,256]{1,0:T(8,128)(2,1)S(1)}, u32[]{:S(2)}, u32[]{:S(2)}) %collective-permute-start.12) | collective-permute-done | bytes 131104 | tf_op jit(solution)/shard_map/ppermute | solution.py:20
  41.7 1.3 %shard_map.78 = (f32[2,256,256]{2,1,0:T(8,128)S(1)}, bf16[1024,256]{1,0:T(8,128)(2,1)}, f32[256,256]{1,0:T(8,128)}) custom-call(bf16[256,5120]{1,0:T(8,128)(2,1)S(1)} %get-tuple-element.50.refs_0_, s32[256,640]{1,0:T(8,128)S(1)} %get-tuple-element.46.refs_1_, ...), custom_call_target="tpu_custom_call", output_to_operand_aliasing={{0}: (3, {}), {1}: (4, {})} | custom-call | tf_op jit(solution)/shard_map/pallas_call | solution.py:210
  (28 shorter events, 6.4 us)
Async XLA Ops:
  0.6 1.7 %copy-start = (bf16[256,5120]{1,0:T(8,128)(2,1)S(1)}, bf16[256,5120]{1,0:T(8,128)(2,1)}, u32[]{:S(2)}) copy-start(bf16[256,5120]{1,0:T(8,128)(2,1)} %refs_0_.3) | copy-start | bytes 7864324
  2.4 1.1 %copy-start.1 = (s32[256,640]{1,0:T(8,128)S(1)}, s32[256,640]{1,0:T(8,128)}, u32[]{:S(2)}) copy-start(s32[256,640]{1,0:T(8,128)} %refs_1_.1) | copy-start | bytes 1966084
  3.5 1.0 %copy-start.2 = (bf16[1024,256]{1,0:T(8,128)(2,1)S(1)}, bf16[1024,256]{1,0:T(8,128)(2,1)}, u32[]{:S(2)}) copy-start(bf16[1024,256]{1,0:T(8,128)(2,1)} %refs_3_.1) | copy-start | bytes 1572868
  4.5 0.9 %copy-start.3 = (f32[256,256]{1,0:T(8,128)S(1)}, f32[256,256]{1,0:T(8,128)}, u32[]{:S(2)}) copy-start(f32[256,256]{1,0:T(8,128)} %refs_2_.1) | copy-start | bytes 786436
  6.3 5.1 %collective-permute-start.3 = (bf16[256,256]{1,0:T(8,128)(2,1)S(1)}, bf16[256,256]{1,0:T(8,128)(2,1)S(1)}, u32[]{:S(2)}, u32[]{:S(2)}) collective-permute-start(bf16[256,256]{1,0:T(8,128)(2,1)S(1)} %get-tuple-element.56), channel_id=1, source_target_pairs={{0,8},{8,16},{16,24},{24,0},{1,9},{9,17},{17,25},{25,1},{2,10},{10... | collective-permute-start | bytes 393224 | tf_op jit(solution)/shard_map/ppermute | solution.py:20
  7.6 5.3 %collective-permute-start.2 = (bf16[256,256]{1,0:T(8,128)(2,1)S(1)}, bf16[256,256]{1,0:T(8,128)(2,1)S(1)}, u32[]{:S(2)}, u32[]{:S(2)}) collective-permute-start(bf16[256,256]{1,0:T(8,128)(2,1)S(1)} %get-tuple-element.55), channel_id=1, source_target_pairs={{0,8},{8,16},{16,24},{24,0},{1,9},{9,17},{17,25},{25,1},{2,10},{10... | collective-permute-start | bytes 393224 | tf_op jit(solution)/shard_map/ppermute | solution.py:20
  10.8 4.4 %collective-permute-start.1 = (bf16[256,256]{1,0:T(8,128)(2,1)S(1)}, bf16[256,256]{1,0:T(8,128)(2,1)S(1)}, u32[]{:S(2)}, u32[]{:S(2)}) collective-permute-start(bf16[256,256]{1,0:T(8,128)(2,1)S(1)} %get-tuple-element.54), channel_id=1, source_target_pairs={{0,8},{8,16},{16,24},{24,0},{1,9},{9,17},{17,25},{25,1},{2,10},{10... | collective-permute-start | bytes 393224 | tf_op jit(solution)/shard_map/ppermute | solution.py:20
  11.4 5.2 %collective-permute-start = (bf16[256,256]{1,0:T(8,128)(2,1)S(1)}, bf16[256,256]{1,0:T(8,128)(2,1)S(1)}, u32[]{:S(2)}, u32[]{:S(2)}) collective-permute-start(bf16[256,256]{1,0:T(8,128)(2,1)S(1)} %get-tuple-element.53), channel_id=1, source_target_pairs={{0,8},{8,16},{16,24},{24,0},{1,9},{9,17},{17,25},{25,1},{2,10},{10... | collective-permute-start | bytes 393224 | tf_op jit(solution)/shard_map/ppermute | solution.py:20
  12.1 5.9 %collective-permute-start.7 = (bf16[256,256]{1,0:T(8,128)(2,1)S(1)}, bf16[256,256]{1,0:T(8,128)(2,1)S(1)}, u32[]{:S(2)}, u32[]{:S(2)}) collective-permute-start(bf16[256,256]{1,0:T(8,128)(2,1)S(1)} %get-tuple-element.64), channel_id=1, source_target_pairs={{0,8},{8,16},{16,24},{24,0},{1,9},{9,17},{17,25},{25,1},{2,10},{10... | collective-permute-start | bytes 393224 | tf_op jit(solution)/shard_map/ppermute | solution.py:20
  13.4 6.0 %collective-permute-start.6 = (bf16[256,256]{1,0:T(8,128)(2,1)S(1)}, bf16[256,256]{1,0:T(8,128)(2,1)S(1)}, u32[]{:S(2)}, u32[]{:S(2)}) collective-permute-start(bf16[256,256]{1,0:T(8,128)(2,1)S(1)} %get-tuple-element.63), channel_id=1, source_target_pairs={{0,8},{8,16},{16,24},{24,0},{1,9},{9,17},{17,25},{25,1},{2,10},{10... | collective-permute-start | bytes 393224 | tf_op jit(solution)/shard_map/ppermute | solution.py:20
  15.8 5.1 %collective-permute-start.5 = (bf16[256,256]{1,0:T(8,128)(2,1)S(1)}, bf16[256,256]{1,0:T(8,128)(2,1)S(1)}, u32[]{:S(2)}, u32[]{:S(2)}) collective-permute-start(bf16[256,256]{1,0:T(8,128)(2,1)S(1)} %get-tuple-element.62), channel_id=1, source_target_pairs={{0,8},{8,16},{16,24},{24,0},{1,9},{9,17},{17,25},{25,1},{2,10},{10... | collective-permute-start | bytes 393224 | tf_op jit(solution)/shard_map/ppermute | solution.py:20
  17.2 5.1 %collective-permute-start.4 = (bf16[256,256]{1,0:T(8,128)(2,1)S(1)}, bf16[256,256]{1,0:T(8,128)(2,1)S(1)}, u32[]{:S(2)}, u32[]{:S(2)}) collective-permute-start(bf16[256,256]{1,0:T(8,128)(2,1)S(1)} %get-tuple-element.61), channel_id=1, source_target_pairs={{0,8},{8,16},{16,24},{24,0},{1,9},{9,17},{17,25},{25,1},{2,10},{10... | collective-permute-start | bytes 393224 | tf_op jit(solution)/shard_map/ppermute | solution.py:20
  18.7 4.9 %collective-permute-start.11 = (bf16[256,256]{1,0:T(8,128)(2,1)S(1)}, bf16[256,256]{1,0:T(8,128)(2,1)S(1)}, u32[]{:S(2)}, u32[]{:S(2)}) collective-permute-start(bf16[256,256]{1,0:T(8,128)(2,1)S(1)} %get-tuple-element.72), channel_id=1, source_target_pairs={{0,8},{8,16},{16,24},{24,0},{1,9},{9,17},{17,25},{25,1},{2,10},{10... | collective-permute-start | bytes 393224 | tf_op jit(solution)/shard_map/ppermute | solution.py:20
  20.0 5.9 %collective-permute-start.10 = (bf16[256,256]{1,0:T(8,128)(2,1)S(1)}, bf16[256,256]{1,0:T(8,128)(2,1)S(1)}, u32[]{:S(2)}, u32[]{:S(2)}) collective-permute-start(bf16[256,256]{1,0:T(8,128)(2,1)S(1)} %get-tuple-element.71), channel_id=1, source_target_pairs={{0,8},{8,16},{16,24},{24,0},{1,9},{9,17},{17,25},{25,1},{2,10},{10... | collective-permute-start | bytes 393224 | tf_op jit(solution)/shard_map/ppermute | solution.py:20
  21.4 6.6 %collective-permute-start.9 = (bf16[256,256]{1,0:T(8,128)(2,1)S(1)}, bf16[256,256]{1,0:T(8,128)(2,1)S(1)}, u32[]{:S(2)}, u32[]{:S(2)}) collective-permute-start(bf16[256,256]{1,0:T(8,128)(2,1)S(1)} %get-tuple-element.70), channel_id=1, source_target_pairs={{0,8},{8,16},{16,24},{24,0},{1,9},{9,17},{17,25},{25,1},{2,10},{10... | collective-permute-start | bytes 393224 | tf_op jit(solution)/shard_map/ppermute | solution.py:20
  22.8 7.4 %collective-permute-start.8 = (bf16[256,256]{1,0:T(8,128)(2,1)S(1)}, bf16[256,256]{1,0:T(8,128)(2,1)S(1)}, u32[]{:S(2)}, u32[]{:S(2)}) collective-permute-start(bf16[256,256]{1,0:T(8,128)(2,1)S(1)} %get-tuple-element.69), channel_id=1, source_target_pairs={{0,8},{8,16},{16,24},{24,0},{1,9},{9,17},{17,25},{25,1},{2,10},{10... | collective-permute-start | bytes 393224 | tf_op jit(solution)/shard_map/ppermute | solution.py:20
  24.3 9.1 %collective-permute-start.15 = (bf16[256,256]{1,0:T(8,128)(2,1)S(1)}, bf16[256,256]{1,0:T(8,128)(2,1)S(1)}, u32[]{:S(2)}, u32[]{:S(2)}) collective-permute-start(bf16[256,256]{1,0:T(8,128)(2,1)S(1)} %get-tuple-element.80), channel_id=1, source_target_pairs={{0,1},{1,2},{2,3},{3,4},{4,5},{5,6},{6,7},{7,0},{8,9},{9,10},{10,1... | collective-permute-start | bytes 393224 | tf_op jit(solution)/shard_map/ppermute | solution.py:20
  26.4 9.8 %collective-permute-start.14 = (bf16[256,256]{1,0:T(8,128)(2,1)S(1)}, bf16[256,256]{1,0:T(8,128)(2,1)S(1)}, u32[]{:S(2)}, u32[]{:S(2)}) collective-permute-start(bf16[256,256]{1,0:T(8,128)(2,1)S(1)} %get-tuple-element.79), channel_id=1, source_target_pairs={{0,1},{1,2},{2,3},{3,4},{4,5},{5,6},{6,7},{7,0},{8,9},{9,10},{10,1... | collective-permute-start | bytes 393224 | tf_op jit(solution)/shard_map/ppermute | solution.py:20
  28.6 10.5 %collective-permute-start.13 = (bf16[256,256]{1,0:T(8,128)(2,1)S(1)}, bf16[256,256]{1,0:T(8,128)(2,1)S(1)}, u32[]{:S(2)}, u32[]{:S(2)}) collective-permute-start(bf16[256,256]{1,0:T(8,128)(2,1)S(1)} %get-tuple-element.78), channel_id=1, source_target_pairs={{0,1},{1,2},{2,3},{3,4},{4,5},{5,6},{6,7},{7,0},{8,9},{9,10},{10,1... | collective-permute-start | bytes 393224 | tf_op jit(solution)/shard_map/ppermute | solution.py:20
  30.7 10.9 %collective-permute-start.12 = (bf16[256,256]{1,0:T(8,128)(2,1)S(1)}, bf16[256,256]{1,0:T(8,128)(2,1)S(1)}, u32[]{:S(2)}, u32[]{:S(2)}) collective-permute-start(bf16[256,256]{1,0:T(8,128)(2,1)S(1)} %get-tuple-element.77), channel_id=1, source_target_pairs={{0,1},{1,2},{2,3},{3,4},{4,5},{5,6},{6,7},{7,0},{8,9},{9,10},{10,1... | collective-permute-start | bytes 393224 | tf_op jit(solution)/shard_map/ppermute | solution.py:20

commit v2 on v0

v2 whole, which is shorter than its diff:
```python
import jax
import jax.numpy as jnp
from jax import lax
from jax.experimental import pallas as pl
from jax.experimental.pallas import tpu as pltpu
from jax.sharding import PartitionSpec as P

VISITS = 5
CHUNKS = 2
PIECES = 2

step_frames = 0.01
step_pixels = 0.02
decay_weight = 0.1

VMEM = pl.BlockSpec(memory_space=pltpu.VMEM)
HBM = pl.BlockSpec(memory_space=pltpu.HBM)
DMA = pltpu.SemaphoreType.DMA


def over_chip(value):
    count = lax.axis_size("blk")
    return lax.ppermute(value, "blk", [(s, s + 1 - 2 * (s % 2)) for s in range(count)])


def to_next_pair(value):
    count = lax.axis_size("blk")
    return lax.ppermute(value, "blk", [(s, (s + 2) % count) for s in range(count)])


def to_next_wide(value):
    count = lax.axis_size("wide")
    return lax.ppermute(value, "wide", [(s, (s + 1) % count) for s in range(count)])


def my_core():
    return lax.axis_index("blk") % 2


def flags(bits, lower, count):
    words = bits.shape[1]
    pieces = []
    at = lower
    while at < lower + count:
        flag, word = divmod(at, words)
        size = min(words - word, lower + count - at)
        pieces.append(lax.shift_right_logical(bits[:, word : word + size], flag) & 1)
        at += size
    whole = pieces[0] if len(pieces) == 1 else jnp.concatenate(pieces, axis=1)
    return whole.astype(jnp.float32).astype(jnp.bfloat16)


def tile(frames, block, wanted, visible):
    frames_low = frames.astype(jnp.bfloat16)
    predicted = lax.dot_general(
        frames_low, block, (((1,), (1,)), ((), ())), preferred_element_type=jnp.float32
    )
    errors = wanted.astype(jnp.float32) - predicted
    scaled = jnp.clip(errors, -1.0, 1.0).astype(jnp.bfloat16) * visible
    grad_pixels = lax.dot_general(
        scaled, frames_low, (((0,), (0,)), ((), ())), preferred_element_type=jnp.float32
    )
    current = block.astype(jnp.float32)
    new = (current + step_pixels * (grad_pixels - decay_weight * current)).astype(jnp.bfloat16)
    return new, jnp.dot(scaled, block, preferred_element_type=jnp.float32)


def moved(frames, grad):
    return frames + step_frames * (grad - decay_weight * frames)


def struct(shape, dtype):
    return jax.ShapeDtypeStruct(shape, dtype)


def call(kernel, args, specs, outs, out_specs, scratch=(), aliases=None):
    return pl.pallas_call(
        kernel,
        out_shape=tuple(outs),
        in_specs=list(specs),
        out_specs=tuple(out_specs),
        scratch_shapes=list(scratch),
        input_output_aliases=aliases or {},
        compiler_params=pltpu.CompilerParams(vmem_limit_bytes=24 * 1024 * 1024),
        cost_estimate=pl.CostEstimate(flops=0, bytes_accessed=0, transcendentals=0),
    )(*args)


def body(observed, mask_bits, frame_factors, pixel_factors):
    width, rank = pixel_factors.shape
    rows = frame_factors.shape[0]
    half = width // 2
    size = half // CHUNKS
    later = VISITS - 1
    low = jnp.bfloat16
    chunk_t = struct((size, rank), low)
    frames_t = struct((rows, rank), jnp.float32)
    both_t = struct((2, rows, rank), jnp.float32)
    observed, mask_bits, frame_factors, pixel_factors = (
        pltpu.with_memory_space_constraint(a, pltpu.HBM)
        for a in (observed, mask_bits, frame_factors, pixel_factors)
    )

    def own_tile(give, c, observed0, bits, pixels, frames, visible):
        for core in range(2):
            mine = 1 - core if give else core

            @pl.when(my_core() == core)
            def _(lower=mine * half + c * size):
                visible[...] = flags(bits, lower, size)

        mine = 1 - my_core() if give else my_core()
        at = pl.multiple_of(mine * half + c * size, size)
        return tile(frames, pixels[pl.ds(at, size), :], observed0[:, pl.ds(at, size)], visible[...])

    def load_kernel(observed, mask_bits, frames, pixels, observed0, bits, pixels_v, state, new, visible, sems):
        copies = [
            pltpu.make_async_copy(frames, state.at[0], sems.at[0]),
            pltpu.make_async_copy(pixels, pixels_v, sems.at[1]),
            pltpu.make_async_copy(mask_bits, bits, sems.at[2]),
            pltpu.make_async_copy(observed.at[:, :width], observed0, sems.at[3]),
        ]
        for copy in copies:
            copy.start()
        for copy in copies:
            copy.wait()
        new[...], grad = own_tile(True, 0, observed0, bits, pixels_v, state[0], visible)
        state[1] = moved(state[0], grad)

    observed0, bits, pixels_v, state, new = call(
        load_kernel,
        (observed, mask_bits, frame_factors, pixel_factors),
        [HBM] * 4,
        (
            struct((rows, width), low),
            struct(mask_bits.shape, mask_bits.dtype),
            struct(pixel_factors.shape, low),
            both_t,
            chunk_t,
        ),
        [VMEM] * 5,
        scratch=[pltpu.VMEM((rows, size), low), DMA((4,))],
    )

    def own_step(give, c, state, last=False):
        def kernel(observed0, bits, pixels, state, new, state_out, *rest):
            frames = state[0]
            new[...], grad = own_tile(give, c, observed0, bits, pixels, frames, rest[-1])
            done = state[1] + step_frames * grad
            state_out[0] = frames
            state_out[1] = done
            if last:
                rest[0][...] = done

        outs = [chunk_t, both_t] + ([frames_t] if last else [])
        return call(
            kernel,
            (observed0, bits, pixels_v, state),
            [VMEM] * 4,
            outs,
            [VMEM] * len(outs),
            scratch=[pltpu.VMEM((rows, size), low)],
            aliases={3: 1},
        )

    def route(got, kept):
        def kernel(got, kept, out):
            out[...] = jnp.where(my_core() == 0, got[...], kept[...])

        return call(kernel, (got, kept), [VMEM] * 2, [chunk_t], [VMEM])[0]

    got, kept, first_sent = [], [], []
    for c in range(CHUNKS):
        if c:
            new, state = own_step(True, c, state)
        got.append(over_chip(new))
        last = c == CHUNKS - 1
        outs = own_step(False, c, state, last)
        kept.append(outs[0])
        state = outs[1]
        routed = route(got[c], kept[c])
        first_sent.append(to_next_pair(routed))
    own = outs[2]
    other = over_chip(own)

    def share_kernel(observed, bits, after, observed_own, visible_own, share1, share, sems):
        del after
        core_here = my_core()
        copies = []
        for v in range(later):
            for n, (mine, target) in enumerate(
                (
                    (core_here, observed_own.at[:, v * half : (v + 1) * half]),
                    (1 - core_here, share1.at[:rows] if v == 0 else share.at[v - 1, :rows]),
                )
            ):
                at = pl.multiple_of((v + 1) * width + mine * half, half)
                copies.append(
                    pltpu.make_async_copy(observed.at[:, pl.ds(at, half)], target, sems.at[v, n])
                )
        for copy in copies:
            copy.start()
        for core in range(2):

            @pl.when(my_core() == core)
            def _(core=core):
                for v in range(later):
                    at = (v + 1) * width
                    visible_own[:, v * half : (v + 1) * half] = flags(bits, at + core * half, half)
                    theirs = flags(bits, at + (1 - core) * half, half)
                    if v == 0:
                        share1[rows:] = theirs
                    else:
                        share[v - 1, rows:] = theirs

        for copy in copies:
            copy.wait()

    own_t = struct((rows, later * half), low)
    observed_own, visible_own, share1, share = call(
        share_kernel,
        (observed, bits, routed),
        [HBM, VMEM, VMEM],
        (own_t, own_t, struct((2 * rows, half), low), struct((later - 1, 2 * rows, half), low)),
        [VMEM] * 4,
        scratch=[DMA((later, 2))],
    )
    share1 = over_chip(share1)
    share = over_chip(share)

    def operand(idx, v, c, observed_own, visible_own, share1, share):
        at = (v - 1) * half + c * size
        cols = slice(c * size, (c + 1) * size)
        theirs = share1 if v == 1 else share.at[v - 2]
        here = my_core() == idx
        wanted = jnp.where(here, observed_own[:, at : at + size], theirs[:rows, cols])
        visible = jnp.where(here, visible_own[:, at : at + size], theirs[rows:, cols])
        return wanted, visible

    def stage(c, even, odd, block, state, part, sums, update=(), extra=None):
        visited = [(idx, v) for idx, v in ((0, even), (1, odd)) if v is not None]
        last = c == CHUNKS - 1
        n_sums = len(sums)
        piece = len(visited) * rows // PIECES

        def kernel(observed_own, visible_own, share1, share, block, state, part, *refs):
            got = refs[:n_sums]
            outs = refs[n_sums:]
            new, state_out, part_out = outs[:3]
            frames = [state[0], state[1]]
            grads = [part[0], part[1]]
            if got:
                total = jnp.concatenate([g[...] for g in got], axis=0).astype(jnp.float32)
                for n, idx in enumerate(update):
                    frames[idx] = moved(frames[idx], grads[idx] + total[n * rows : (n + 1) * rows])
            held = block[...]
            for idx, v in visited:
                held, grad = tile(
                    frames[idx], held, *operand(idx, v, c, observed_own, visible_own, share1, share)
                )
                grads[idx] = grad if c == 0 else grads[idx] + grad
            new[...] = held
            for idx in range(2):
                state_out[idx] = frames[idx]
                part_out[idx] = grads[idx]
            if last:
                sent = jnp.concatenate([grads[idx].astype(low) for idx, _ in visited], axis=0)
                for n in range(PIECES):
                    outs[3 + n][...] = sent[n * piece : (n + 1) * piece]

        outs = [chunk_t, both_t, both_t]
        if last:
            outs += [struct((piece, rank), low)] * PIECES
        return call(
            kernel,
            (observed_own, visible_own, share1, share, block, state, part, *sums),
            [VMEM] * (7 + n_sums),
            outs,
            [VMEM] * len(outs),
            aliases={5: 1, 6: 2},
        )

    def pair_kernel(c, observed_own, visible_own, share1, share, got, kept, own, other, part, new, state, part_out, *sent):
        first = my_core() == 0
        frames = jnp.where(first, other[...], own[...])
        if c == 0:
            state[0] = jnp.where(first, own[...], other[...])
            state[1] = frames
        block = jnp.where(first, kept[...], got[...])
        new[...], grad = tile(frames, block, *operand(1, 1, c, observed_own, visible_own, share1, share))
        if c:
            grad = grad + part[1]
        part_out[1] = grad
        if sent:
            sent[0][...] = grad.astype(low)

    second_sent, sums = [], []
    part = None
    for c in range(CHUNKS):
        last = c == CHUNKS - 1

        def kernel(*refs, c=c):
            refs = list(refs)
            if c == 0:
                refs.insert(8, None)
            else:
                refs.insert(10, None)
            pair_kernel(c, *refs)

        args = [observed_own, visible_own, share1, share, got[c], kept[c], own, other]
        outs = [chunk_t, both_t, both_t]
        if c:
            args.append(part)
            outs = [chunk_t, both_t]
        if last:
            outs.append(struct((rows, rank), low))
        outs = call(kernel, args, [VMEM] * len(args), outs, [VMEM] * len(outs))
        second_sent.append(to_next_pair(outs[0]))
        if c == 0:
            state, part = outs[1:3]
        else:
            part = outs[1]
        if last:
            sums = [over_chip(outs[-1])]

    def stages(even, odd, blocks, state, part, sums, update, send):
        sent = []
        for c in range(CHUNKS):
            outs = stage(c, even, odd, blocks[c], state, part, sums if c == 0 else (), update)
            sent.append(send(outs[0]))
            state, part = outs[1:3]
        return sent, state, part, [over_chip(s) for s in outs[3:]]

    third_sent, state, part, sums = stages(1, 2, first_sent, state, part, sums, (1,), to_next_pair)
    odd_sent, state, part, sums = stages(2, 3, second_sent, state, part, sums, (0, 1), to_next_wide)
    even_sent, state, part, sums = stages(3, None, third_sent, state, part, sums, (0, 1), to_next_wide)

    odd_done = []
    for c in range(CHUNKS):
        outs = stage(c, None, 4, odd_sent[c], state, part, ())
        odd_done.append(outs[0])
        state, part = outs[1:3]

    mine, theirs = [], []
    for c in range(CHUNKS):
        last = c == CHUNKS - 1
        n_sums = len(sums) if c == 0 else 0

        def kernel(observed_own, visible_own, share1, share, block, state, part, done, *refs, c=c, last=last):
            got, outs = refs[:n_sums], refs[n_sums:]
            frames, grad = state[0], part[0]
            if got:
                total = jnp.concatenate([g[...] for g in got], axis=0).astype(jnp.float32)
                frames = moved(frames, grad + total)
            new, step = tile(
                frames, block[...], *operand(0, 4, c, observed_own, visible_own, share1, share)
            )
            grad = step if c == 0 else grad + step
            first = my_core() == 0
            outs[0][...] = jnp.where(first, new, done[...])
            outs[1][...] = jnp.where(first, done[...], new)
            outs[2][0] = frames
            outs[2][1] = state[1]
            outs[3][0] = grad
            outs[3][1] = part[1]
            if last:
                outs[4][...] = jnp.where(first, part[1], grad).astype(low)

        outs = [chunk_t, chunk_t, both_t, both_t]
        if last:
            outs.append(struct((rows, rank), low))
        args = [observed_own, visible_own, share1, share, even_sent[c], state, part, odd_done[c]]
        args += sums if c == 0 else []
        outs = call(kernel, args, [VMEM] * len(args), outs, [VMEM] * len(outs), aliases={5: 2, 6: 3})
        mine.append(outs[0])
        theirs.append(over_chip(outs[1]))
        state, part = outs[2:4]
    total = over_chip(outs[4])

    def write_kernel(*refs):
        mine, theirs = refs[:CHUNKS], refs[CHUNKS : 2 * CHUNKS]
        state, part, total, frames_out, pixels_out, frames, sems = refs[2 * CHUNKS :]
        core = my_core()
        copies = []
        for c in range(CHUNKS):
            for n, (source, at) in enumerate(((mine[c], core), (theirs[c], 1 - core))):
                to = pl.multiple_of(at * half + c * size, size)
                copies.append(
                    pltpu.make_async_copy(source, pixels_out.at[pl.ds(to, size)], sems.at[c, n])
                )
        for copy in copies:
            copy.start()
        first = core == 0
        frames[...] = moved(
            jnp.where(first, state[0], state[1]),
            jnp.where(first, part[0], part[1]) + total[...].astype(jnp.float32),
        )
        copy = pltpu.make_async_copy(frames, frames_out, sems.at[CHUNKS, 0])
        copy.start()
        for one in copies:
            one.wait()
        copy.wait()

    return call(
        write_kernel,
        (*mine, *theirs, state, part, total),
        [VMEM] * (2 * CHUNKS + 3),
        (frames_t, struct(pixel_factors.shape, low)),
        [HBM] * 2,
        scratch=[pltpu.VMEM((rows, rank), jnp.float32), DMA((CHUNKS + 1, 2))],
    )


def solution(mesh):
    spec = P(("blk", "wide"), None)
    return jax.shard_map(
        body, mesh=mesh, in_specs=(spec,) * 4, out_specs=(spec, spec), check_vma=False
    )
```

time: 58.4 us -> 53.3 us (0.913)
  Pallas kernels: 0 us -> 16.2 us
  waiting for transfers between devices: 30.5 us -> 17.9 us
  matrix products: 8.04 us -> 0 us
  starting transfers between devices: 10.6 us -> 18.1 us
  local copies, waits for them, and re-layouts: 4.94 us -> 0 us
  other arithmetic: 3.32 us -> 0 us
    pallas_call x0 -> x20, Pallas kernels: none -> 16.2 us  [call(): pl.pallas_call(kernel, out_shape=tuple(outs), in_specs=list(specs), out_s...]
    ppermute x7 -> x25, waiting for transfers between devices: 30.5 us -> 17.9 us  [the longest x6 6.51 us: to_next_pair(): lax.ppermute(value, 'blk', [(s, (s + 2) % count) for s in range(count)])]
    dot_general x18 -> x0, matrix products: 8.04 us -> none  [the longest x8 3.33 us: pixel_update(): lax.dot_general(scaled[:, first_row:end_row], frames_low, (((0,), (0,)),...]
    ppermute x7 -> x25, starting transfers between devices: 10.6 us -> 18.1 us  [the longest x6 8.6 us: to_next_pair(): lax.ppermute(value, 'blk', [(s, (s + 2) % count) for s in range(count)])]
    unnamed x10 -> x0, local copies, waits for them, and re-layouts: 3.45 us -> none
    convert_element_type x1 -> x0, other arithmetic: 3.32 us -> none  [body(): visible_all = unpack_mask(mask_bits).astype(jnp.bfloat16)]
    shift_right_arithmetic x3 -> x0, local copies, waits for them, and re-layouts: 1.44 us -> none  [unpack_mask(): jnp.right_shift(packed[..., None, :], shifts[:, None])]
  transfers between devices with their start and end apart: 7 -> 25, of which waited for: 5 -> 11; matrix products, arithmetic and copies ran while one was open for 4% -> 0% of each run, Pallas kernels for 0% -> 19%
where the time goes in v2:
time: 53.3 us; the launch traced here: 53.1 us
  starting transfers between devices  18.1 us (34%)
  waiting for transfers between devices  17.9 us (34%)
  Pallas kernels  16.2 us (30%)
  between operations  0.81 us (2%)
    pallas_call x20, Pallas kernels, call(): pl.pallas_call(kernel, out_shape=tuple(outs), in_specs=list(specs), out_s...  16.2 us
    ppermute x6, starting transfers between devices, to_next_pair(): lax.ppermute(value, 'blk', [(s, (s + 2) % count) for s in range(count)])  8.6 us
    ppermute x6, waiting for transfers between devices, to_next_pair(): lax.ppermute(value, 'blk', [(s, (s + 2) % count) for s in range(count)])  6.51 us
    ppermute x4, waiting for transfers between devices, to_next_wide(): lax.ppermute(value, 'wide', [(s, (s + 1) % count) for s in range(count)])  6.31 us
    ppermute x4, starting transfers between devices, to_next_wide(): lax.ppermute(value, 'wide', [(s, (s + 1) % count) for s in range(count)])  6.09 us
    ppermute x15, waiting for transfers between devices, over_chip(): lax.ppermute(value, 'blk', [(s, s + 1 - 2 * (s % 2)) for s in range(count)])  5.11 us
    ppermute x15, starting transfers between devices, over_chip(): lax.ppermute(value, 'blk', [(s, s + 1 - 2 * (s % 2)) for s in range(count)])  3.44 us
  transfers between devices with their start and end apart: 25, of which 11 were waited for; matrix products, arithmetic and copies ran while one was open for 0% of the time, Pallas kernels for 19%

profile of v2, /device:TPU:0, one launch (start us, length us, event | category | flops | bytes accessed | tf_op | source)
XLA Modules:
  0.0 53.1 jit_solution(4307320491315016893)
XLA Ops:
  0.6 2.1 %shard_map.59 = (bf16[256,1024]{1,0:T(8,128)(2,1)S(1)}, s32[256,640]{1,0:T(8,128)S(1)}, bf16[1024,256]{1,0:T(8,128)(2,1)S(1)}, f32[2,256,256]{2,1,0:T(8,128)S(1)}, bf16[256,256]{1,0:T(8,128)(2,1)S(1)}) custom-call(bf16[256,5120]{1,0:T(8,128)(2,1)} %observed.3, s32[256,640]{1,0:T(8,128)} %mask_bits.1, f32[256,256]{1,0:T(8,128)} %frames.1, ...), custom_call_target="tpu_custom_call" | custom-call | tf_op jit(solution)/shard_map/pallas_call | solution.py:77
  2.7 0.6 %shard_map.60 = (bf16[256,256]{1,0:T(8,128)(2,1)S(1)}, f32[2,256,256]{2,1,0:T(8,128)S(1)}) custom-call(bf16[256,1024]{1,0:T(8,128)(2,1)S(1)} %get-tuple-element.63.observed0, s32[256,640]{1,0:T(8,128)S(1)} %get-tuple-element.62.bits, bf16[1024,256]{1,0:T(8,128)(2,1)S(1)} %get-tuple-element.64.pixels, ...), custom_call_target="tpu_custom_call", output_to_operand_aliasing={{1}: (3, {})} | custom-call | tf_op jit(solution)/shard_map/pallas_call | solution.py:77
  3.4 0.6 %shard_map.61 = (bf16[256,256]{1,0:T(8,128)(2,1)S(1)}, f32[2,256,256]{2,1,0:T(8,128)S(1)}) custom-call(bf16[256,1024]{1,0:T(8,128)(2,1)S(1)} %get-tuple-element.63.observed0, s32[256,640]{1,0:T(8,128)S(1)} %get-tuple-element.62.bits, bf16[1024,256]{1,0:T(8,128)(2,1)S(1)} %get-tuple-element.64.pixels, ...), custom_call_target="tpu_custom_call", output_to_operand_aliasing={{1}: (3, {})} | custom-call | tf_op jit(solution)/shard_map/pallas_call | solution.py:77
  4.5 0.6 %shard_map.62 = (bf16[256,256]{1,0:T(8,128)(2,1)S(1)}, f32[2,256,256]{2,1,0:T(8,128)S(1)}, f32[256,256]{1,0:T(8,128)S(1)}) custom-call(bf16[256,1024]{1,0:T(8,128)(2,1)S(1)} %get-tuple-element.63.observed0, s32[256,640]{1,0:T(8,128)S(1)} %get-tuple-element.62.bits, bf16[1024,256]{1,0:T(8,128)(2,1)S(1)} %get-tuple-element.64.pixels, ...), custom_call_target="tpu_custom_call", output_to_operand_aliasing={{1}: (3, {})} | custom-call | tf_op jit(solution)/shard_map/pallas_call | solution.py:77
  5.5 1.6 %shard_map.64 = (bf16[256,2048]{1,0:T(8,128)(2,1)S(1)}, bf16[256,2048]{1,0:T(8,128)(2,1)S(1)}, bf16[512,512]{1,0:T(8,128)(2,1)S(1)}, bf16[3,512,512]{2,1,0:T(8,128)(2,1)S(1)}) custom-call(bf16[256,5120]{1,0:T(8,128)(2,1)} %observed.3, s32[256,640]{1,0:T(8,128)S(1)} %get-tuple-element.62.bits, bf16[256,256]{1,0:T(8,128)(2,1)S(1)} %shard_map.63.after), custom_call_target="tpu_custom_call" | custom-call | tf_op jit(solution)/shard_map/pallas_call | solution.py:77
  8.2 3.7 %collective-permute-done.3.got.refs_4_ = bf16[256,256]{1,0:T(8,128)(2,1)S(1)} collective-permute-done((bf16[256,256]{1,0:T(8,128)(2,1)S(1)}, bf16[256,256]{1,0:T(8,128)(2,1)S(1)}, u32[]{:S(2)}, u32[]{:S(2)}) %collective-permute-start.3) | collective-permute-done | bytes 131104 | tf_op jit(solution)/shard_map/ppermute | solution.py:23
  11.9 2.9 %collective-permute-start.4 = (bf16[256,256]{1,0:T(8,128)(2,1)S(1)}, bf16[256,256]{1,0:T(8,128)(2,1)S(1)}, u32[]{:S(2)}, u32[]{:S(2)}) collective-permute-start(bf16[256,256]{1,0:T(8,128)(2,1)S(1)} %shard_map.65), channel_id=1, source_target_pairs={{0,16},{8,24},{16,0},{24,8},{1,17},{9,25},{17,1},{25,9},{2,18},{10... | collective-permute-start | bytes 393224 | tf_op jit(solution)/shard_map/ppermute | solution.py:28
  16.3 1.9 %collective-permute-start.9 = (bf16[256,256]{1,0:T(8,128)(2,1)S(1)}, bf16[256,256]{1,0:T(8,128)(2,1)S(1)}, u32[]{:S(2)}, u32[]{:S(2)}) collective-permute-start(bf16[256,256]{1,0:T(8,128)(2,1)S(1)} %get-tuple-element.83), channel_id=1, source_target_pairs={{0,16},{8,24},{16,0},{24,8},{1,17},{9,25},{17,1},{25,9},{2,18},{10... | collective-permute-start | bytes 393224 | tf_op jit(solution)/shard_map/ppermute | solution.py:28
  18.7 1.0 %shard_map.68 = (bf16[256,256]{1,0:T(8,128)(2,1)S(1)}, f32[2,256,256]{2,1,0:T(8,128)S(1)}, f32[2,256,256]{2,1,0:T(8,128)S(1)}) custom-call(bf16[256,2048]{1,0:T(8,128)(2,1)S(1)} %get-tuple-element.70.refs_0_.observed_own, bf16[256,2048]{1,0:T(8,128)(2,1)S(1)} %get-tuple-element.71.refs_1_.visible_own, ...), custom_call_target="tpu_custom_call", output_to_operand_aliasing={{1}: (5, {}), {2}: (6, {})} | custom-call | tf_op jit(solution)/shard_map/pallas_call | solution.py:77
  19.7 2.7 %collective-permute-done.10.block = bf16[256,256]{1,0:T(8,128)(2,1)S(1)} collective-permute-done((bf16[256,256]{1,0:T(8,128)(2,1)S(1)}, bf16[256,256]{1,0:T(8,128)(2,1)S(1)}, u32[]{:S(2)}, u32[]{:S(2)}) %collective-permute-start.10) | collective-permute-done | bytes 131104 | tf_op jit(solution)/shard_map/ppermute | solution.py:28
  22.5 1.0 %shard_map.69 = (bf16[256,256]{1,0:T(8,128)(2,1)S(1)}, f32[2,256,256]{2,1,0:T(8,128)S(1)}, f32[2,256,256]{2,1,0:T(8,128)S(1)}, bf16[256,256]{1,0:T(8,128)(2,1)S(1)}, bf16[256,256]{1,0:T(8,128)(2,1)S(1)}) custom-call(bf16[256,2048]{1,0:T(8,128)(2,1)S(1)} %get-tuple-element.70.refs_0_.observed_own, ...), custom_call_target="tpu_custom_call", output_to_operand_aliasing={{1}: (5, {}), {2}: (6, {})} | custom-call | tf_op jit(solution)/shard_map/pallas_call | solution.py:77
  24.0 1.6 %collective-permute-start.8 = (bf16[256,256]{1,0:T(8,128)(2,1)S(1)}, bf16[256,256]{1,0:T(8,128)(2,1)S(1)}, u32[]{:S(2)}, u32[]{:S(2)}) collective-permute-start(bf16[256,256]{1,0:T(8,128)(2,1)S(1)} %get-tuple-element.82), channel_id=1, source_target_pairs={{0,16},{8,24},{16,0},{24,8},{1,17},{9,25},{17,1},{25,9},{2,18},{10... | collective-permute-start | bytes 393224 | tf_op jit(solution)/shard_map/ppermute | solution.py:28
  26.0 1.1 %shard_map.70 = (bf16[256,256]{1,0:T(8,128)(2,1)S(1)}, f32[2,256,256]{2,1,0:T(8,128)S(1)}, f32[2,256,256]{2,1,0:T(8,128)S(1)}) custom-call(bf16[256,2048]{1,0:T(8,128)(2,1)S(1)} %get-tuple-element.70.refs_0_.observed_own, bf16[256,2048]{1,0:T(8,128)(2,1)S(1)} %get-tuple-element.71.refs_1_.visible_own, ...), custom_call_target="tpu_custom_call", output_to_operand_aliasing={{1}: (5, {}), {2}: (6, {})} | custom-call | tf_op jit(solution)/shard_map/pallas_call | solution.py:77
  27.1 3.2 %collective-permute-done.8.block = bf16[256,256]{1,0:T(8,128)(2,1)S(1)} collective-permute-done((bf16[256,256]{1,0:T(8,128)(2,1)S(1)}, bf16[256,256]{1,0:T(8,128)(2,1)S(1)}, u32[]{:S(2)}, u32[]{:S(2)}) %collective-permute-start.8) | collective-permute-done | bytes 131104 | tf_op jit(solution)/shard_map/ppermute | solution.py:28
  30.4 1.0 %shard_map.71 = (bf16[256,256]{1,0:T(8,128)(2,1)S(1)}, f32[2,256,256]{2,1,0:T(8,128)S(1)}, f32[2,256,256]{2,1,0:T(8,128)S(1)}, bf16[256,256]{1,0:T(8,128)(2,1)S(1)}, bf16[256,256]{1,0:T(8,128)(2,1)S(1)}) custom-call(bf16[256,2048]{1,0:T(8,128)(2,1)S(1)} %get-tuple-element.70.refs_0_.observed_own, ...), custom_call_target="tpu_custom_call", output_to_operand_aliasing={{1}: (5, {}), {2}: (6, {})} | custom-call | tf_op jit(solution)/shard_map/pallas_call | solution.py:77
  31.9 1.6 %collective-permute-start.18 = (bf16[256,256]{1,0:T(8,128)(2,1)S(1)}, bf16[256,256]{1,0:T(8,128)(2,1)S(1)}, u32[]{:S(2)}, u32[]{:S(2)}) collective-permute-start(bf16[256,256]{1,0:T(8,128)(2,1)S(1)} %get-tuple-element.99), channel_id=1, source_target_pairs={{0,16},{8,24},{16,0},{24,8},{1,17},{9,25},{17,1},{25,9},{2,18},{10... | collective-permute-start | bytes 393224 | tf_op jit(solution)/shard_map/ppermute | solution.py:28
  33.5 1.4 %collective-permute-start.17 = (bf16[256,256]{1,0:T(8,128)(2,1)S(1)}, bf16[256,256]{1,0:T(8,128)(2,1)S(1)}, u32[]{:S(2)}, u32[]{:S(2)}) collective-permute-start(bf16[256,256]{1,0:T(8,128)(2,1)S(1)} %get-tuple-element.98), channel_id=1, source_target_pairs={{0,1},{1,2},{2,3},{3,4},{4,5},{5,6},{6,7},{7,0},{8,9},{9,10},{10,1... | collective-permute-start | bytes 393224 | tf_op jit(solution)/shard_map/ppermute | solution.py:33
  34.9 1.5 %collective-permute-start.16 = (bf16[256,256]{1,0:T(8,128)(2,1)S(1)}, bf16[256,256]{1,0:T(8,128)(2,1)S(1)}, u32[]{:S(2)}, u32[]{:S(2)}) collective-permute-start(bf16[256,256]{1,0:T(8,128)(2,1)S(1)} %get-tuple-element.97), channel_id=1, source_target_pairs={{0,1},{1,2},{2,3},{3,4},{4,5},{5,6},{6,7},{7,0},{8,9},{9,10},{10,1... | collective-permute-start | bytes 393224 | tf_op jit(solution)/shard_map/ppermute | solution.py:33
  36.4 0.7 %shard_map.72 = (bf16[256,256]{1,0:T(8,128)(2,1)S(1)}, f32[2,256,256]{2,1,0:T(8,128)S(1)}, f32[2,256,256]{2,1,0:T(8,128)S(1)}) custom-call(bf16[256,2048]{1,0:T(8,128)(2,1)S(1)} %get-tuple-element.70.refs_0_.observed_own, bf16[256,2048]{1,0:T(8,128)(2,1)S(1)} %get-tuple-element.71.refs_1_.visible_own, ...), custom_call_target="tpu_custom_call", output_to_operand_aliasing={{1}: (5, {}), {2}: (6, {})} | custom-call | tf_op jit(solution)/shard_map/pallas_call | solution.py:77
  37.1 1.6 %collective-permute-start.15 = (bf16[256,256]{1,0:T(8,128)(2,1)S(1)}, bf16[256,256]{1,0:T(8,128)(2,1)S(1)}, u32[]{:S(2)}, u32[]{:S(2)}) collective-permute-start(bf16[256,256]{1,0:T(8,128)(2,1)S(1)} %get-tuple-element.96), channel_id=1, source_target_pairs={{0,1},{1,2},{2,3},{3,4},{4,5},{5,6},{6,7},{7,0},{8,9},{9,10},{10,1... | collective-permute-start | bytes 393224 | tf_op jit(solution)/shard_map/ppermute | solution.py:33
  38.7 0.6 %shard_map.73 = (bf16[256,256]{1,0:T(8,128)(2,1)S(1)}, f32[2,256,256]{2,1,0:T(8,128)S(1)}, f32[2,256,256]{2,1,0:T(8,128)S(1)}, bf16[128,256]{1,0:T(8,128)(2,1)S(1)}, bf16[128,256]{1,0:T(8,128)(2,1)S(1)}) custom-call(bf16[256,2048]{1,0:T(8,128)(2,1)S(1)} %get-tuple-element.70.refs_0_.observed_own, ...), custom_call_target="tpu_custom_call", output_to_operand_aliasing={{1}: (5, {}), {2}: (6, {})} | custom-call | tf_op jit(solution)/shard_map/pallas_call | solution.py:77
  39.3 1.6 %collective-permute-start.21 = (bf16[256,256]{1,0:T(8,128)(2,1)S(1)}, bf16[256,256]{1,0:T(8,128)(2,1)S(1)}, u32[]{:S(2)}, u32[]{:S(2)}) collective-permute-start(bf16[256,256]{1,0:T(8,128)(2,1)S(1)} %get-tuple-element.112), channel_id=1, source_target_pairs={{0,1},{1,2},{2,3},{3,4},{4,5},{5,6},{6,7},{7,0},{8,9},{9,10},{10,1... | collective-permute-start | bytes 393224 | tf_op jit(solution)/shard_map/ppermute | solution.py:33
  40.9 1.7 %collective-permute-done.17.block = bf16[256,256]{1,0:T(8,128)(2,1)S(1)} collective-permute-done((bf16[256,256]{1,0:T(8,128)(2,1)S(1)}, bf16[256,256]{1,0:T(8,128)(2,1)S(1)}, u32[]{:S(2)}, u32[]{:S(2)}) %collective-permute-start.17) | collective-permute-done | bytes 131104 | tf_op jit(solution)/shard_map/ppermute | solution.py:33
  42.6 0.6 %shard_map.74 = (bf16[256,256]{1,0:T(8,128)(2,1)S(1)}, f32[2,256,256]{2,1,0:T(8,128)S(1)}, f32[2,256,256]{2,1,0:T(8,128)S(1)}) custom-call(bf16[256,2048]{1,0:T(8,128)(2,1)S(1)} %get-tuple-element.70.refs_0_.observed_own, bf16[256,2048]{1,0:T(8,128)(2,1)S(1)} %get-tuple-element.71.refs_1_.visible_own, ...), custom_call_target="tpu_custom_call", output_to_operand_aliasing={{1}: (5, {}), {2}: (6, {})} | custom-call | tf_op jit(solution)/shard_map/pallas_call | solution.py:77
  43.2 2.2 %collective-permute-done.16.block = bf16[256,256]{1,0:T(8,128)(2,1)S(1)} collective-permute-done((bf16[256,256]{1,0:T(8,128)(2,1)S(1)}, bf16[256,256]{1,0:T(8,128)(2,1)S(1)}, u32[]{:S(2)}, u32[]{:S(2)}) %collective-permute-start.16) | collective-permute-done | bytes 131104 | tf_op jit(solution)/shard_map/ppermute | solution.py:33
  45.4 1.3 %shard_map.75 = (bf16[256,256]{1,0:T(8,128)(2,1)S(1)}, f32[2,256,256]{2,1,0:T(8,128)S(1)}, f32[2,256,256]{2,1,0:T(8,128)S(1)}, bf16[128,256]{1,0:T(8,128)(2,1)}, bf16[128,256]{1,0:T(8,128)(2,1)}) custom-call(bf16[256,2048]{1,0:T(8,128)(2,1)S(1)} %get-tuple-element.70.refs_0_.observed_own, ...), custom_call_target="tpu_custom_call", output_to_operand_aliasing={{1}: (5, {}), {2}: (6, {})} | custom-call | tf_op jit(solution)/shard_map/pallas_call | solution.py:77
  46.6 1.5 %collective-permute-done.15.block = bf16[256,256]{1,0:T(8,128)(2,1)S(1)} collective-permute-done((bf16[256,256]{1,0:T(8,128)(2,1)S(1)}, bf16[256,256]{1,0:T(8,128)(2,1)S(1)}, u32[]{:S(2)}, u32[]{:S(2)}) %collective-permute-start.15) | collective-permute-done | bytes 131104 | tf_op jit(solution)/shard_map/ppermute | solution.py:33
  48.2 0.7 %shard_map.76 = (bf16[256,256]{1,0:T(8,128)(2,1)S(1)}, bf16[256,256]{1,0:T(8,128)(2,1)S(1)}, f32[2,256,256]{2,1,0:T(8,128)S(1)}, f32[2,256,256]{2,1,0:T(8,128)S(1)}) custom-call(bf16[256,2048]{1,0:T(8,128)(2,1)S(1)} %get-tuple-element.70.refs_0_.observed_own, ...), custom_call_target="tpu_custom_call", output_to_operand_aliasing={{2}: (5, {}), {3}: (6, {})} | custom-call | tf_op jit(solution)/shard_map/pallas_call | solution.py:77
  48.9 0.9 %collective-permute-done.21.block = bf16[256,256]{1,0:T(8,128)(2,1)S(1)} collective-permute-done((bf16[256,256]{1,0:T(8,128)(2,1)S(1)}, bf16[256,256]{1,0:T(8,128)(2,1)S(1)}, u32[]{:S(2)}, u32[]{:S(2)}) %collective-permute-start.21) | collective-permute-done | bytes 131104 | tf_op jit(solution)/shard_map/ppermute | solution.py:33
  49.8 0.7 %shard_map.77 = (bf16[256,256]{1,0:T(8,128)(2,1)S(1)}, bf16[256,256]{1,0:T(8,128)(2,1)S(1)}, f32[2,256,256]{2,1,0:T(8,128)S(1)}, f32[2,256,256]{2,1,0:T(8,128)S(1)}, bf16[256,256]{1,0:T(8,128)(2,1)S(1)}) custom-call(bf16[256,2048]{1,0:T(8,128)(2,1)S(1)} %get-tuple-element.70.refs_0_.observed_own, ...), custom_call_target="tpu_custom_call", output_to_operand_aliasing={{2}: (5, {}), {3}: (6, {})} | custom-call | tf_op jit(solution)/shard_map/pallas_call | solution.py:77
  51.1 0.8 %collective-permute-done.23.refs_3_ = bf16[256,256]{1,0:T(8,128)(2,1)S(1)} collective-permute-done((bf16[256,256]{1,0:T(8,128)(2,1)S(1)}, bf16[256,256]{1,0:T(8,128)(2,1)S(1)}, u32[]{:S(2)}, u32[]{:S(2)}) %collective-permute-start.23) | collective-permute-done | bytes 131104 | tf_op jit(solution)/shard_map/ppermute | solution.py:23
  52.1 0.9 %shard_map.78 = (f32[256,256]{1,0:T(8,128)}, bf16[1024,256]{1,0:T(8,128)(2,1)}) custom-call(bf16[256,256]{1,0:T(8,128)(2,1)S(1)} %get-tuple-element.111.refs_0_, bf16[256,256]{1,0:T(8,128)(2,1)S(1)} %get-tuple-element.116.refs_1_, bf16[256,256]{1,0:T(8,128)(2,1)S(1)} %collective-permute-done.22.refs_2_, ...), custom_call_target="tpu_custom_call" | custom-call | tf_op jit(solution)/shard_map/pallas_call | solution.py:77
  (38 shorter events, 6.4 us)
Async XLA Ops:
  4.0 1.5 %collective-permute-start = (bf16[256,256]{1,0:T(8,128)(2,1)S(1)}, bf16[256,256]{1,0:T(8,128)(2,1)S(1)}, u32[]{:S(2)}, u32[]{:S(2)}) collective-permute-start(bf16[256,256]{1,0:T(8,128)(2,1)S(1)} %get-tuple-element.67), channel_id=1, source_target_pairs={{0,8},{8,0},{16,24},{24,16},{1,9},{9,1},{17,25},{25,17},{2,10},{10... | collective-permute-start | bytes 393224 | tf_op jit(solution)/shard_map/ppermute | solution.py:23
  7.1 7.7 %collective-permute-start.2 = (bf16[3,512,512]{2,1,0:T(8,128)(2,1)S(1)}, bf16[3,512,512]{2,1,0:T(8,128)(2,1)S(1)}, u32[]{:S(2)}, u32[]{:S(2)}) collective-permute-start(bf16[3,512,512]{2,1,0:T(8,128)(2,1)S(1)} %get-tuple-element.73), channel_id=1, source_target_pairs={{0,8},{8,0},{16,24},{24,16},{1,9},{9,1},{17,25},{25,17},{2,10},{10... | collective-permute-start | bytes 4718600 | tf_op jit(solution)/shard_map/ppermute | solution.py:23
  7.6 7.3 %collective-permute-start.1 = (bf16[512,512]{1,0:T(8,128)(2,1)S(1)}, bf16[512,512]{1,0:T(8,128)(2,1)S(1)}, u32[]{:S(2)}, u32[]{:S(2)}) collective-permute-start(bf16[512,512]{1,0:T(8,128)(2,1)S(1)} %get-tuple-element.72), channel_id=1, source_target_pairs={{0,8},{8,0},{16,24},{24,16},{1,9},{9,1},{17,25},{25,17},{2,10},{10... | collective-permute-start | bytes 1572872 | tf_op jit(solution)/shard_map/ppermute | solution.py:23
  7.7 7.2 %collective-permute-start.5 = (f32[256,256]{1,0:T(8,128)S(1)}, f32[256,256]{1,0:T(8,128)S(1)}, u32[]{:S(2)}, u32[]{:S(2)}) collective-permute-start(f32[256,256]{1,0:T(8,128)S(1)} %get-tuple-element.76.refs_6_), channel_id=1, source_target_pairs={{0,8},{8,0},{16,24},{24,16},{1,9},{9,1},{17,25},{25,17},{2,10},{10... | collective-permute-start | bytes 786440 | tf_op jit(solution)/shard_map/ppermute | solution.py:23
  8.1 3.8 %collective-permute-start.3 = (bf16[256,256]{1,0:T(8,128)(2,1)S(1)}, bf16[256,256]{1,0:T(8,128)(2,1)S(1)}, u32[]{:S(2)}, u32[]{:S(2)}) collective-permute-start(bf16[256,256]{1,0:T(8,128)(2,1)S(1)} %get-tuple-element.74), channel_id=1, source_target_pairs={{0,8},{8,0},{16,24},{24,16},{1,9},{9,1},{17,25},{25,17},{2,10},{10... | collective-permute-start | bytes 393224 | tf_op jit(solution)/shard_map/ppermute | solution.py:23
  11.9 6.8 %collective-permute-start.4 = (bf16[256,256]{1,0:T(8,128)(2,1)S(1)}, bf16[256,256]{1,0:T(8,128)(2,1)S(1)}, u32[]{:S(2)}, u32[]{:S(2)}) collective-permute-start(bf16[256,256]{1,0:T(8,128)(2,1)S(1)} %shard_map.65), channel_id=1, source_target_pairs={{0,16},{8,24},{16,0},{24,8},{1,17},{9,25},{17,1},{25,9},{2,18},{10... | collective-permute-start | bytes 393224 | tf_op jit(solution)/shard_map/ppermute | solution.py:28
  16.0 2.7 %collective-permute-start.6 = (bf16[256,256]{1,0:T(8,128)(2,1)S(1)}, bf16[256,256]{1,0:T(8,128)(2,1)S(1)}, u32[]{:S(2)}, u32[]{:S(2)}) collective-permute-start(bf16[256,256]{1,0:T(8,128)(2,1)S(1)} %get-tuple-element.80), channel_id=1, source_target_pairs={{0,8},{8,0},{16,24},{24,16},{1,9},{9,1},{17,25},{25,17},{2,10},{10... | collective-permute-start | bytes 393224 | tf_op jit(solution)/shard_map/ppermute | solution.py:23
  16.1 6.4 %collective-permute-start.10 = (bf16[256,256]{1,0:T(8,128)(2,1)S(1)}, bf16[256,256]{1,0:T(8,128)(2,1)S(1)}, u32[]{:S(2)}, u32[]{:S(2)}) collective-permute-start(bf16[256,256]{1,0:T(8,128)(2,1)S(1)} %shard_map.63.after), channel_id=1, source_target_pairs={{0,16},{8,24},{16,0},{24,8},{1,17},{9,25},{17,1},{25,9},{2,18},{10... | collective-permute-start | bytes 393224 | tf_op jit(solution)/shard_map/ppermute | solution.py:28
  16.3 9.8 %collective-permute-start.9 = (bf16[256,256]{1,0:T(8,128)(2,1)S(1)}, bf16[256,256]{1,0:T(8,128)(2,1)S(1)}, u32[]{:S(2)}, u32[]{:S(2)}) collective-permute-start(bf16[256,256]{1,0:T(8,128)(2,1)S(1)} %get-tuple-element.83), channel_id=1, source_target_pairs={{0,16},{8,24},{16,0},{24,8},{1,17},{9,25},{17,1},{25,9},{2,18},{10... | collective-permute-start | bytes 393224 | tf_op jit(solution)/shard_map/ppermute | solution.py:28
  23.4 2.6 %collective-permute-start.11 = (bf16[256,256]{1,0:T(8,128)(2,1)S(1)}, bf16[256,256]{1,0:T(8,128)(2,1)S(1)}, u32[]{:S(2)}, u32[]{:S(2)}) collective-permute-start(bf16[256,256]{1,0:T(8,128)(2,1)S(1)} %get-tuple-element.88), channel_id=1, source_target_pairs={{0,8},{8,0},{16,24},{24,16},{1,9},{9,1},{17,25},{25,17},{2,10},{10... | collective-permute-start | bytes 393224 | tf_op jit(solution)/shard_map/ppermute | solution.py:23
  23.5 2.5 %collective-permute-start.12 = (bf16[256,256]{1,0:T(8,128)(2,1)S(1)}, bf16[256,256]{1,0:T(8,128)(2,1)S(1)}, u32[]{:S(2)}, u32[]{:S(2)}) collective-permute-start(bf16[256,256]{1,0:T(8,128)(2,1)S(1)} %get-tuple-element.89), channel_id=1, source_target_pairs={{0,8},{8,0},{16,24},{24,16},{1,9},{9,1},{17,25},{25,17},{2,10},{10... | collective-permute-start | bytes 393224 | tf_op jit(solution)/shard_map/ppermute | solution.py:23
  24.0 6.4 %collective-permute-start.8 = (bf16[256,256]{1,0:T(8,128)(2,1)S(1)}, bf16[256,256]{1,0:T(8,128)(2,1)S(1)}, u32[]{:S(2)}, u32[]{:S(2)}) collective-permute-start(bf16[256,256]{1,0:T(8,128)(2,1)S(1)} %get-tuple-element.82), channel_id=1, source_target_pairs={{0,16},{8,24},{16,0},{24,8},{1,17},{9,25},{17,1},{25,9},{2,18},{10... | collective-permute-start | bytes 393224 | tf_op jit(solution)/shard_map/ppermute | solution.py:28
  25.6 9.3 %collective-permute-start.7 = (bf16[256,256]{1,0:T(8,128)(2,1)S(1)}, bf16[256,256]{1,0:T(8,128)(2,1)S(1)}, u32[]{:S(2)}, u32[]{:S(2)}) collective-permute-start(bf16[256,256]{1,0:T(8,128)(2,1)S(1)} %get-tuple-element.81), channel_id=1, source_target_pairs={{0,16},{8,24},{16,0},{24,8},{1,17},{9,25},{17,1},{25,9},{2,18},{10... | collective-permute-start | bytes 393224 | tf_op jit(solution)/shard_map/ppermute | solution.py:28
  31.3 5.1 %collective-permute-start.13 = (bf16[256,256]{1,0:T(8,128)(2,1)S(1)}, bf16[256,256]{1,0:T(8,128)(2,1)S(1)}, u32[]{:S(2)}, u32[]{:S(2)}) collective-permute-start(bf16[256,256]{1,0:T(8,128)(2,1)S(1)} %get-tuple-element.94), channel_id=1, source_target_pairs={{0,8},{8,0},{16,24},{24,16},{1,9},{9,1},{17,25},{25,17},{2,10},{10... | collective-permute-start | bytes 393224 | tf_op jit(solution)/shard_map/ppermute | solution.py:23
  31.4 5.0 %collective-permute-start.14 = (bf16[256,256]{1,0:T(8,128)(2,1)S(1)}, bf16[256,256]{1,0:T(8,128)(2,1)S(1)}, u32[]{:S(2)}, u32[]{:S(2)}) collective-permute-start(bf16[256,256]{1,0:T(8,128)(2,1)S(1)} %get-tuple-element.95), channel_id=1, source_target_pairs={{0,8},{8,0},{16,24},{24,16},{1,9},{9,1},{17,25},{25,17},{2,10},{10... | collective-permute-start | bytes 393224 | tf_op jit(solution)/shard_map/ppermute | solution.py:23
  31.9 6.8 %collective-permute-start.18 = (bf16[256,256]{1,0:T(8,128)(2,1)S(1)}, bf16[256,256]{1,0:T(8,128)(2,1)S(1)}, u32[]{:S(2)}, u32[]{:S(2)}) collective-permute-start(bf16[256,256]{1,0:T(8,128)(2,1)S(1)} %get-tuple-element.99), channel_id=1, source_target_pairs={{0,16},{8,24},{16,0},{24,8},{1,17},{9,25},{17,1},{25,9},{2,18},{10... | collective-permute-start | bytes 393224 | tf_op jit(solution)/shard_map/ppermute | solution.py:28
  33.5 9.1 %collective-permute-start.17 = (bf16[256,256]{1,0:T(8,128)(2,1)S(1)}, bf16[256,256]{1,0:T(8,128)(2,1)S(1)}, u32[]{:S(2)}, u32[]{:S(2)}) collective-permute-start(bf16[256,256]{1,0:T(8,128)(2,1)S(1)} %get-tuple-element.98), channel_id=1, source_target_pairs={{0,1},{1,2},{2,3},{3,4},{4,5},{5,6},{6,7},{7,0},{8,9},{9,10},{10,1... | collective-permute-start | bytes 393224 | tf_op jit(solution)/shard_map/ppermute | solution.py:33
  34.9 10.5 %collective-permute-start.16 = (bf16[256,256]{1,0:T(8,128)(2,1)S(1)}, bf16[256,256]{1,0:T(8,128)(2,1)S(1)}, u32[]{:S(2)}, u32[]{:S(2)}) collective-permute-start(bf16[256,256]{1,0:T(8,128)(2,1)S(1)} %get-tuple-element.97), channel_id=1, source_target_pairs={{0,1},{1,2},{2,3},{3,4},{4,5},{5,6},{6,7},{7,0},{8,9},{9,10},{10,1... | collective-permute-start | bytes 393224 | tf_op jit(solution)/shard_map/ppermute | solution.py:33
  37.1 11.1 %collective-permute-start.15 = (bf16[256,256]{1,0:T(8,128)(2,1)S(1)}, bf16[256,256]{1,0:T(8,128)(2,1)S(1)}, u32[]{:S(2)}, u32[]{:S(2)}) collective-permute-start(bf16[256,256]{1,0:T(8,128)(2,1)S(1)} %get-tuple-element.96), channel_id=1, source_target_pairs={{0,1},{1,2},{2,3},{3,4},{4,5},{5,6},{6,7},{7,0},{8,9},{9,10},{10,1... | collective-permute-start | bytes 393224 | tf_op jit(solution)/shard_map/ppermute | solution.py:33
  39.3 10.5 %collective-permute-start.21 = (bf16[256,256]{1,0:T(8,128)(2,1)S(1)}, bf16[256,256]{1,0:T(8,128)(2,1)S(1)}, u32[]{:S(2)}, u32[]{:S(2)}) collective-permute-start(bf16[256,256]{1,0:T(8,128)(2,1)S(1)} %get-tuple-element.112), channel_id=1, source_target_pairs={{0,1},{1,2},{2,3},{3,4},{4,5},{5,6},{6,7},{7,0},{8,9},{9,10},{10,1... | collective-permute-start | bytes 393224 | tf_op jit(solution)/shard_map/ppermute | solution.py:33
  40.9 5.7 %collective-permute-start.19 = (bf16[128,256]{1,0:T(8,128)(2,1)S(1)}, bf16[128,256]{1,0:T(8,128)(2,1)S(1)}, u32[]{:S(2)}, u32[]{:S(2)}) collective-permute-start(bf16[128,256]{1,0:T(8,128)(2,1)S(1)} %get-tuple-element.109), channel_id=1, source_target_pairs={{0,8},{8,0},{16,24},{24,16},{1,9},{9,1},{17,25},{25,17},{2,10},{10... | collective-permute-start | bytes 196616 | tf_op jit(solution)/shard_map/ppermute | solution.py:23
  42.5 4.1 %collective-permute-start.20 = (bf16[128,256]{1,0:T(8,128)(2,1)S(1)}, bf16[128,256]{1,0:T(8,128)(2,1)S(1)}, u32[]{:S(2)}, u32[]{:S(2)}) collective-permute-start(bf16[128,256]{1,0:T(8,128)(2,1)S(1)} %get-tuple-element.110), channel_id=1, source_target_pairs={{0,8},{8,0},{16,24},{24,16},{1,9},{9,1},{17,25},{25,17},{2,10},{10... | collective-permute-start | bytes 196616 | tf_op jit(solution)/shard_map/ppermute | solution.py:23
  48.8 2.3 %collective-permute-start.22 = (bf16[256,256]{1,0:T(8,128)(2,1)S(1)}, bf16[256,256]{1,0:T(8,128)(2,1)S(1)}, u32[]{:S(2)}, u32[]{:S(2)}) collective-permute-start(bf16[256,256]{1,0:T(8,128)(2,1)S(1)} %get-tuple-element.117), channel_id=1, source_target_pairs={{0,8},{8,0},{16,24},{24,16},{1,9},{9,1},{17,25},{25,17},{2,10},{10... | collective-permute-start | bytes 393224 | tf_op jit(solution)/shard_map/ppermute | solution.py:23
  50.5 1.4 %collective-permute-start.23 = (bf16[256,256]{1,0:T(8,128)(2,1)S(1)}, bf16[256,256]{1,0:T(8,128)(2,1)S(1)}, u32[]{:S(2)}, u32[]{:S(2)}) collective-permute-start(bf16[256,256]{1,0:T(8,128)(2,1)S(1)} %get-tuple-element.118), channel_id=1, source_target_pairs={{0,8},{8,0},{16,24},{24,16},{1,9},{9,1},{17,25},{25,17},{2,10},{10... | collective-permute-start | bytes 393224 | tf_op jit(solution)/shard_map/ppermute | solution.py:23
  50.6 1.5 %collective-permute-start.24 = (bf16[256,256]{1,0:T(8,128)(2,1)S(1)}, bf16[256,256]{1,0:T(8,128)(2,1)S(1)}, u32[]{:S(2)}, u32[]{:S(2)}) collective-permute-start(bf16[256,256]{1,0:T(8,128)(2,1)S(1)} %get-tuple-element.121), channel_id=1, source_target_pairs={{0,8},{8,0},{16,24},{24,16},{1,9},{9,1},{17,25},{25,17},{2,10},{10... | collective-permute-start | bytes 393224 | tf_op jit(solution)/shard_map/ppermute | solution.py:23

commit v3 on v0

v3 whole, which is shorter than its diff:
```python
import jax
import jax.numpy as jnp
from jax import lax
from jax.experimental import pallas as pl
from jax.experimental.pallas import tpu as pltpu
from jax.sharding import PartitionSpec as P

CHUNKS = 4
LAST_FLOPS = 200_000_000

step_frames = 0.01
step_pixels = 0.02
decay_weight = 0.1

LOW = jnp.bfloat16
VMEM = pl.BlockSpec(memory_space=pltpu.VMEM)
HBM = pl.BlockSpec(memory_space=pltpu.HBM)
DMA = pltpu.SemaphoreType.DMA


def shifted(value, axis):
    count = lax.axis_size(axis)
    return lax.ppermute(value, axis, [(s, (s + 1) % count) for s in range(count)])


def struct(shape, dtype=LOW):
    return jax.ShapeDtypeStruct(shape, dtype)


def call(name, kernel, args, outs, in_specs=None, out_specs=None, scratch=(), aliases=None, flops=0):
    return pl.pallas_call(
        kernel,
        name=name,
        out_shape=tuple(outs),
        in_specs=in_specs or [VMEM] * len(args),
        out_specs=tuple(out_specs or [VMEM] * len(outs)),
        scratch_shapes=list(scratch),
        input_output_aliases=aliases or {},
        compiler_params=pltpu.CompilerParams(vmem_limit_bytes=24 * 1024 * 1024),
        cost_estimate=pl.CostEstimate(flops=flops, bytes_accessed=0, transcendentals=0),
    )(*args)


def flags(bits, lower, count):
    words = bits.shape[1]
    pieces = []
    at = lower
    while at < lower + count:
        flag, word = divmod(at, words)
        size = min(words - word, lower + count - at)
        pieces.append(lax.shift_right_logical(bits[:, word : word + size], flag) & 1)
        at += size
    return pieces[0] if len(pieces) == 1 else jnp.concatenate(pieces, axis=1)


def tile(frames, block, wanted, visible):
    frames_low = frames.astype(LOW)
    predicted = lax.dot_general(
        frames_low, block, (((1,), (1,)), ((), ())), preferred_element_type=jnp.float32
    )
    errors = wanted.astype(jnp.float32) - predicted
    clipped = jnp.clip(errors, -1.0, 1.0)
    scaled = jnp.where(visible != 0, clipped, 0.0).astype(LOW)
    grad_pixels = lax.dot_general(
        scaled, frames_low, (((0,), (0,)), ((), ())), preferred_element_type=jnp.float32
    )
    current = block.astype(jnp.float32)
    new = (current + step_pixels * (grad_pixels - decay_weight * current)).astype(LOW)
    return new, jnp.dot(scaled, block, preferred_element_type=jnp.float32)


def added(frames, done, grad):
    if done is None:
        return frames + step_frames * (grad - decay_weight * frames)
    return done + step_frames * grad


def body(observed, mask_bits, frame_factors, pixel_factors):
    width, rank = pixel_factors.shape
    rows = frame_factors.shape[0]
    visits = observed.shape[1] // width
    size = width // CHUNKS
    chunk_t = struct((size, rank))
    frames_t = struct((rows, rank), jnp.float32)
    whole = observed
    observed, mask_bits, frame_factors, pixel_factors = (
        pltpu.with_memory_space_constraint(a, pltpu.HBM)
        for a in (observed, mask_bits, frame_factors, pixel_factors)
    )

    def load_kernel(observed, mask_bits, frames_in, pixels_in, observed0, bits, pixels, frames, new, done, sems):
        first = [
            pltpu.make_async_copy(mask_bits.at[:, :size], bits.at[:, :size], sems.at[0]),
            pltpu.make_async_copy(pixels_in.at[:size], pixels.at[:size], sems.at[1]),
            pltpu.make_async_copy(observed.at[:, :size], observed0.at[:, :size], sems.at[2]),
            pltpu.make_async_copy(frames_in, frames, sems.at[3]),
        ]
        rest = [
            pltpu.make_async_copy(pixels_in.at[size:], pixels.at[size:], sems.at[4]),
            pltpu.make_async_copy(observed.at[:, size:width], observed0.at[:, size:], sems.at[5]),
            pltpu.make_async_copy(mask_bits.at[:, size:], bits.at[:, size:], sems.at[6]),
        ]
        for copy in first + rest:
            copy.start()
        for copy in first:
            copy.wait()
        new[...], grad = tile(frames[...], pixels[:size], observed0[:, :size], flags(bits, 0, size))
        done[...] = added(frames[...], None, grad)
        for copy in rest:
            copy.wait()

    observed0, bits, pixels, frames, new, done = call(
        "load",
        load_kernel,
        [observed, mask_bits, frame_factors, pixel_factors],
        [
            struct((rows, width)),
            struct(mask_bits.shape, mask_bits.dtype),
            struct((width, rank)),
            frames_t,
            chunk_t,
            frames_t,
        ],
        in_specs=[HBM] * 4,
        scratch=[DMA((7,))],
    )
    def step(visit, chunk, block, frames, done, wanted):
        at = chunk * size
        first = done is None
        whole = block.shape[0] > size
        columns = visit * width + at

        def kernel(wanted, bits, block, frames, *refs):
            block = block[at : at + size] if whole else block[...]
            new, grad = tile(
                frames[...], block, wanted[:, columns : columns + size], flags(bits, visit * width + at, size)
            )
            refs[-2][...] = new
            refs[-1][...] = added(frames[...], None if first else refs[0][...], grad)

        args = [wanted, bits, block, frames] + ([] if first else [done])
        return call(
            "step",
            kernel,
            args,
            [chunk_t, frames_t],
            aliases={} if first else {4: 1},
            flops=LAST_FLOPS if visit == visits - 1 else 0,
        )

    later, new = lax.optimization_barrier((whole, new))
    coming = [shifted(new, "blk")]
    for c in range(1, CHUNKS):
        new, done = step(0, c, pixels, frames, done, observed0)
        coming.append(shifted(new, "blk"))

    for visit in range(1, visits - 1):
        axis = "blk" if visit < visits - 2 else "wide"
        frames, done = done, None
        sent = []
        for c in range(CHUNKS):
            new, done = step(visit, c, coming[c], frames, done, later)
            sent.append(shifted(new, axis))
        coming = sent

    frames, done = done, None
    visit = visits - 1
    made = []
    for c in range(CHUNKS - 1):
        new, done = step(visit, c, coming[c], frames, done, later)
        made.append(new)

    def last_kernel(wanted, bits, block, frames, done, *refs):
        made, (frames_out, pixels_out, new, sum_v, sems) = refs[: CHUNKS - 1], refs[CHUNKS - 1 :]
        copies = [
            pltpu.make_async_copy(ref, pixels_out.at[c * size : (c + 1) * size], sems.at[c])
            for c, ref in enumerate(made)
        ]
        at = width - size
        copies.append(pltpu.make_async_copy(new, pixels_out.at[at:], sems.at[CHUNKS - 1]))
        copies.append(pltpu.make_async_copy(sum_v, frames_out, sems.at[CHUNKS]))
        for copy in copies[: CHUNKS - 1]:
            copy.start()
        columns = visit * width + at
        new[...], grad = tile(
            frames[...], block[...], wanted[:, columns : columns + size], flags(bits, visit * width + at, size)
        )
        copies[-2].start()
        sum_v[...] = added(frames[...], done[...], grad)
        copies[-1].start()
        for copy in copies:
            copy.wait()

    return call(
        "last",
        last_kernel,
        [later, bits, coming[-1], frames, done, *made],
        [frames_t, struct((width, rank))],
        out_specs=[HBM] * 2,
        scratch=[pltpu.VMEM((size, rank), LOW), pltpu.VMEM((rows, rank), jnp.float32), DMA((CHUNKS + 1,))],
        flops=LAST_FLOPS,
    )


def solution(mesh):
    spec = P(("blk", "wide"), None)
    return jax.shard_map(
        body, mesh=mesh, in_specs=(spec,) * 4, out_specs=(spec, spec), check_vma=False
    )
```

time: 58.4 us -> 39 us (0.67)
  waiting for transfers between devices: 30.5 us -> 8.54 us
  Pallas kernels: 0 us -> 12.9 us
  matrix products: 8.04 us -> 0 us
  starting transfers between devices: 10.6 us -> 16.6 us
  local copies, waits for them, and re-layouts: 4.94 us -> 0.01 us
  other arithmetic: 3.32 us -> 0 us
    ppermute x7 -> x16, waiting for transfers between devices: 30.5 us -> 8.54 us  [shifted(): lax.ppermute(value, axis, [(s, (s + 1) % count) for s in range(count)])]
    pallas_call x0 -> x20, Pallas kernels: none -> 12.9 us  [call(): pl.pallas_call(kernel, name=name, out_shape=tuple(outs), in_specs=in_spec...]
    dot_general x18 -> x0, matrix products: 8.04 us -> none  [the longest x8 3.33 us: pixel_update(): lax.dot_general(scaled[:, first_row:end_row], frames_low, (((0,), (0,)),...]
    ppermute x7 -> x16, starting transfers between devices: 10.6 us -> 16.6 us  [shifted(): lax.ppermute(value, axis, [(s, (s + 1) % count) for s in range(count)])]
    unnamed x10 -> x2, local copies, waits for them, and re-layouts: 3.45 us -> 0.01 us
    convert_element_type x1 -> x0, other arithmetic: 3.32 us -> none  [body(): visible_all = unpack_mask(mask_bits).astype(jnp.bfloat16)]
    shift_right_arithmetic x3 -> x0, local copies, waits for them, and re-layouts: 1.44 us -> none  [unpack_mask(): jnp.right_shift(packed[..., None, :], shifts[:, None])]
  transfers between devices with their start and end apart: 7 -> 16, of which waited for: 5 -> 6; matrix products, arithmetic and copies ran while one was open for 4% -> 0% of each run, Pallas kernels for 0% -> 25%
where the time goes in v3:
time: 39 us; the launch traced here: 38.9 us
  starting transfers between devices  16.6 us (43%)
  Pallas kernels  12.9 us (33%)
  waiting for transfers between devices  8.54 us (22%)
  between operations  0.81 us (2%)
    ppermute x16, starting transfers between devices, shifted(): lax.ppermute(value, axis, [(s, (s + 1) % count) for s in range(count)])  16.6 us
    pallas_call x20, Pallas kernels, call(): pl.pallas_call(kernel, name=name, out_shape=tuple(outs), in_specs=in_spec...  12.9 us
    ppermute x16, waiting for transfers between devices, shifted(): lax.ppermute(value, axis, [(s, (s + 1) % count) for s in range(count)])  8.54 us
  transfers between devices with their start and end apart: 16, of which 6 were waited for; matrix products, arithmetic and copies ran while one was open for 0% of the time, Pallas kernels for 25%

profile of v3, /device:TPU:0, one launch (start us, length us, event | category | flops | bytes accessed | tf_op | source)
XLA Modules:
  0.0 38.9 jit_solution(3239926393577992425)
XLA Ops:
  0.6 1.8 %load.1 = (bf16[256,1024]{1,0:T(8,128)(2,1)S(1)}, s32[256,640]{1,0:T(8,128)S(1)}, bf16[1024,256]{1,0:T(8,128)(2,1)S(1)}, f32[256,256]{1,0:T(8,128)S(1)}, bf16[25...) custom-call(bf16[256,5120]{1,0:T(8,128)(2,1)} %wanted.15, s32[256,640]{1,0:T(8,128)} %mask_bits.1, f32[256,256]{1,0:T(8,128)} %frames_in.1, ...), custom_call_target="tpu_custom_call" | custom-call | tf_op jit(solution)/shard_map/load/pallas_call | solution.py:31
  2.9 0.6 %step.18 = (bf16[256,256]{1,0:T(8,128)(2,1)S(1)}, f32[256,256]{1,0:T(8,128)S(1)}) custom-call(bf16[256,1024]{1,0:T(8,128)(2,1)S(1)} %get-tuple-element.49.wanted, s32[256,640]{1,0:T(8,128)S(1)} %get-tuple-element.48.bits, bf16[1024,256]{1,0:T(8,128)(2,1)S(1)} %get-tuple-element.50.block, ...), custom_call_target="tpu_custom_call", output_to_operand_aliasing={{1}: (4, {})} | custom-call | tf_op jit(solution)/shard_map/step/pallas_call | solution.py:31
  3.5 2.7 %collective-permute-start.2 = (bf16[256,256]{1,0:T(8,128)(2,1)S(1)}, bf16[256,256]{1,0:T(8,128)(2,1)S(1)}, u32[]{:S(2)}, u32[]{:S(2)}) collective-permute-start(bf16[256,256]{1,0:T(8,128)(2,1)S(1)} %get-tuple-element.58), channel_id=1, source_target_pairs={{0,8},{8,16},{16,24},{24,0},{1,9},{9,17},{17,25},{25,1},{2,10},{10... | collective-permute-start | bytes 393224 | tf_op jit(solution)/shard_map/ppermute | solution.py:23
  6.1 0.6 %step.19 = (bf16[256,256]{1,0:T(8,128)(2,1)S(1)}, f32[256,256]{1,0:T(8,128)S(1)}) custom-call(bf16[256,1024]{1,0:T(8,128)(2,1)S(1)} %get-tuple-element.49.wanted, s32[256,640]{1,0:T(8,128)S(1)} %get-tuple-element.48.bits, bf16[1024,256]{1,0:T(8,128)(2,1)S(1)} %get-tuple-element.50.block, ...), custom_call_target="tpu_custom_call", output_to_operand_aliasing={{1}: (4, {})} | custom-call | tf_op jit(solution)/shard_map/step/pallas_call | solution.py:31
  6.8 0.6 %step.20 = (bf16[256,256]{1,0:T(8,128)(2,1)S(1)}, f32[256,256]{1,0:T(8,128)S(1)}) custom-call(bf16[256,1024]{1,0:T(8,128)(2,1)S(1)} %get-tuple-element.49.wanted, s32[256,640]{1,0:T(8,128)S(1)} %get-tuple-element.48.bits, bf16[1024,256]{1,0:T(8,128)(2,1)S(1)} %get-tuple-element.50.block, ...), custom_call_target="tpu_custom_call", output_to_operand_aliasing={{1}: (4, {})} | custom-call | tf_op jit(solution)/shard_map/step/pallas_call | solution.py:31
  8.9 0.6 %step.22 = (bf16[256,256]{1,0:T(8,128)(2,1)S(1)}, f32[256,256]{1,0:T(8,128)S(1)}) custom-call(bf16[256,5120]{1,0:T(8,128)(2,1)S(1)} %copy-done, s32[256,640]{1,0:T(8,128)S(1)} %get-tuple-element.48.bits, bf16[256,256]{1,0:T(8,128)(2,1)S(1)} %collective-permute-done.2.block, ...), custom_call_target="tpu_custom_call", output_to_operand_aliasing={{1}: (4, {})} | custom-call | tf_op jit(solution)/shard_map/step/pallas_call | solution.py:31
  9.5 1.7 %collective-permute-start.6 = (bf16[256,256]{1,0:T(8,128)(2,1)S(1)}, bf16[256,256]{1,0:T(8,128)(2,1)S(1)}, u32[]{:S(2)}, u32[]{:S(2)}) collective-permute-start(bf16[256,256]{1,0:T(8,128)(2,1)S(1)} %get-tuple-element.66), channel_id=1, source_target_pairs={{0,8},{8,16},{16,24},{24,0},{1,9},{9,17},{17,25},{25,1},{2,10},{10... | collective-permute-start | bytes 393224 | tf_op jit(solution)/shard_map/ppermute | solution.py:23
  11.2 0.6 %step.23 = (bf16[256,256]{1,0:T(8,128)(2,1)S(1)}, f32[256,256]{1,0:T(8,128)S(1)}) custom-call(bf16[256,5120]{1,0:T(8,128)(2,1)S(1)} %copy-done, s32[256,640]{1,0:T(8,128)S(1)} %get-tuple-element.48.bits, bf16[256,256]{1,0:T(8,128)(2,1)S(1)} %collective-permute-done.1.block, ...), custom_call_target="tpu_custom_call", output_to_operand_aliasing={{1}: (4, {})} | custom-call | tf_op jit(solution)/shard_map/step/pallas_call | solution.py:31
  11.7 0.8 %collective-permute-start.5 = (bf16[256,256]{1,0:T(8,128)(2,1)S(1)}, bf16[256,256]{1,0:T(8,128)(2,1)S(1)}, u32[]{:S(2)}, u32[]{:S(2)}) collective-permute-start(bf16[256,256]{1,0:T(8,128)(2,1)S(1)} %get-tuple-element.65), channel_id=1, source_target_pairs={{0,8},{8,16},{16,24},{24,0},{1,9},{9,17},{17,25},{25,1},{2,10},{10... | collective-permute-start | bytes 393224 | tf_op jit(solution)/shard_map/ppermute | solution.py:23
  12.6 0.6 %step.24 = (bf16[256,256]{1,0:T(8,128)(2,1)S(1)}, f32[256,256]{1,0:T(8,128)S(1)}) custom-call(bf16[256,5120]{1,0:T(8,128)(2,1)S(1)} %copy-done, s32[256,640]{1,0:T(8,128)S(1)} %get-tuple-element.48.bits, bf16[256,256]{1,0:T(8,128)(2,1)S(1)} %collective-permute-done.block, f32[256,256]{1,0:T(8,128)S(1)} %get-tuple-element.56.frames, ...), custom_call_target="tpu_custom_call", output_to_operand_aliasing={{1}: (4, {})} | custom-call | tf_op jit(solution)/shard_map/step/pallas_call | solution.py:31
  13.1 0.8 %collective-permute-start.4 = (bf16[256,256]{1,0:T(8,128)(2,1)S(1)}, bf16[256,256]{1,0:T(8,128)(2,1)S(1)}, u32[]{:S(2)}, u32[]{:S(2)}) collective-permute-start(bf16[256,256]{1,0:T(8,128)(2,1)S(1)} %get-tuple-element.63), channel_id=1, source_target_pairs={{0,8},{8,16},{16,24},{24,0},{1,9},{9,17},{17,25},{25,1},{2,10},{10... | collective-permute-start | bytes 393224 | tf_op jit(solution)/shard_map/ppermute | solution.py:23
  14.5 0.8 %collective-permute-start.11 = (bf16[256,256]{1,0:T(8,128)(2,1)S(1)}, bf16[256,256]{1,0:T(8,128)(2,1)S(1)}, u32[]{:S(2)}, u32[]{:S(2)}) collective-permute-start(bf16[256,256]{1,0:T(8,128)(2,1)S(1)} %get-tuple-element.75), channel_id=1, source_target_pairs={{0,8},{8,16},{16,24},{24,0},{1,9},{9,17},{17,25},{25,1},{2,10},{10... | collective-permute-start | bytes 393224 | tf_op jit(solution)/shard_map/ppermute | solution.py:23
  15.4 0.6 %step.26 = (bf16[256,256]{1,0:T(8,128)(2,1)S(1)}, f32[256,256]{1,0:T(8,128)S(1)}) custom-call(bf16[256,5120]{1,0:T(8,128)(2,1)S(1)} %copy-done, s32[256,640]{1,0:T(8,128)S(1)} %get-tuple-element.48.bits, bf16[256,256]{1,0:T(8,128)(2,1)S(1)} %collective-permute-done.6.block, ...), custom_call_target="tpu_custom_call", output_to_operand_aliasing={{1}: (4, {})} | custom-call | tf_op jit(solution)/shard_map/step/pallas_call | solution.py:31
  15.9 0.8 %collective-permute-start.10 = (bf16[256,256]{1,0:T(8,128)(2,1)S(1)}, bf16[256,256]{1,0:T(8,128)(2,1)S(1)}, u32[]{:S(2)}, u32[]{:S(2)}) collective-permute-start(bf16[256,256]{1,0:T(8,128)(2,1)S(1)} %get-tuple-element.74), channel_id=1, source_target_pairs={{0,8},{8,16},{16,24},{24,0},{1,9},{9,17},{17,25},{25,1},{2,10},{10... | collective-permute-start | bytes 393224 | tf_op jit(solution)/shard_map/ppermute | solution.py:23
  16.8 0.6 %step.27 = (bf16[256,256]{1,0:T(8,128)(2,1)S(1)}, f32[256,256]{1,0:T(8,128)S(1)}) custom-call(bf16[256,5120]{1,0:T(8,128)(2,1)S(1)} %copy-done, s32[256,640]{1,0:T(8,128)S(1)} %get-tuple-element.48.bits, bf16[256,256]{1,0:T(8,128)(2,1)S(1)} %collective-permute-done.5.block, ...), custom_call_target="tpu_custom_call", output_to_operand_aliasing={{1}: (4, {})} | custom-call | tf_op jit(solution)/shard_map/step/pallas_call | solution.py:31
  17.3 0.8 %collective-permute-start.9 = (bf16[256,256]{1,0:T(8,128)(2,1)S(1)}, bf16[256,256]{1,0:T(8,128)(2,1)S(1)}, u32[]{:S(2)}, u32[]{:S(2)}) collective-permute-start(bf16[256,256]{1,0:T(8,128)(2,1)S(1)} %get-tuple-element.73), channel_id=1, source_target_pairs={{0,8},{8,16},{16,24},{24,0},{1,9},{9,17},{17,25},{25,1},{2,10},{10... | collective-permute-start | bytes 393224 | tf_op jit(solution)/shard_map/ppermute | solution.py:23
  18.2 0.6 %step.28 = (bf16[256,256]{1,0:T(8,128)(2,1)S(1)}, f32[256,256]{1,0:T(8,128)S(1)}) custom-call(bf16[256,5120]{1,0:T(8,128)(2,1)S(1)} %copy-done, s32[256,640]{1,0:T(8,128)S(1)} %get-tuple-element.48.bits, bf16[256,256]{1,0:T(8,128)(2,1)S(1)} %collective-permute-done.4.block, ...), custom_call_target="tpu_custom_call", output_to_operand_aliasing={{1}: (4, {})} | custom-call | tf_op jit(solution)/shard_map/step/pallas_call | solution.py:31
  18.7 0.8 %collective-permute-start.8 = (bf16[256,256]{1,0:T(8,128)(2,1)S(1)}, bf16[256,256]{1,0:T(8,128)(2,1)S(1)}, u32[]{:S(2)}, u32[]{:S(2)}) collective-permute-start(bf16[256,256]{1,0:T(8,128)(2,1)S(1)} %get-tuple-element.71), channel_id=1, source_target_pairs={{0,8},{8,16},{16,24},{24,0},{1,9},{9,17},{17,25},{25,1},{2,10},{10... | collective-permute-start | bytes 393224 | tf_op jit(solution)/shard_map/ppermute | solution.py:23
  20.1 1.6 %collective-permute-start.15 = (bf16[256,256]{1,0:T(8,128)(2,1)S(1)}, bf16[256,256]{1,0:T(8,128)(2,1)S(1)}, u32[]{:S(2)}, u32[]{:S(2)}) collective-permute-start(bf16[256,256]{1,0:T(8,128)(2,1)S(1)} %get-tuple-element.83), channel_id=1, source_target_pairs={{0,1},{1,2},{2,3},{3,4},{4,5},{5,6},{6,7},{7,0},{8,9},{9,10},{10,1... | collective-permute-start | bytes 393224 | tf_op jit(solution)/shard_map/ppermute | solution.py:23
  21.7 0.6 %step.30 = (bf16[256,256]{1,0:T(8,128)(2,1)S(1)}, f32[256,256]{1,0:T(8,128)S(1)}) custom-call(bf16[256,5120]{1,0:T(8,128)(2,1)S(1)} %copy-done, s32[256,640]{1,0:T(8,128)S(1)} %get-tuple-element.48.bits, bf16[256,256]{1,0:T(8,128)(2,1)S(1)} %collective-permute-done.10.block, ...), custom_call_target="tpu_custom_call", output_to_operand_aliasing={{1}: (4, {})} | custom-call | tf_op jit(solution)/shard_map/step/pallas_call | solution.py:31
  22.3 1.6 %collective-permute-start.14 = (bf16[256,256]{1,0:T(8,128)(2,1)S(1)}, bf16[256,256]{1,0:T(8,128)(2,1)S(1)}, u32[]{:S(2)}, u32[]{:S(2)}) collective-permute-start(bf16[256,256]{1,0:T(8,128)(2,1)S(1)} %get-tuple-element.82), channel_id=1, source_target_pairs={{0,1},{1,2},{2,3},{3,4},{4,5},{5,6},{6,7},{7,0},{8,9},{9,10},{10,1... | collective-permute-start | bytes 393224 | tf_op jit(solution)/shard_map/ppermute | solution.py:23
  23.8 0.6 %step.31 = (bf16[256,256]{1,0:T(8,128)(2,1)S(1)}, f32[256,256]{1,0:T(8,128)S(1)}) custom-call(bf16[256,5120]{1,0:T(8,128)(2,1)S(1)} %copy-done, s32[256,640]{1,0:T(8,128)S(1)} %get-tuple-element.48.bits, bf16[256,256]{1,0:T(8,128)(2,1)S(1)} %collective-permute-done.9.block, ...), custom_call_target="tpu_custom_call", output_to_operand_aliasing={{1}: (4, {})} | custom-call | tf_op jit(solution)/shard_map/step/pallas_call | solution.py:31
  24.4 1.6 %collective-permute-start.13 = (bf16[256,256]{1,0:T(8,128)(2,1)S(1)}, bf16[256,256]{1,0:T(8,128)(2,1)S(1)}, u32[]{:S(2)}, u32[]{:S(2)}) collective-permute-start(bf16[256,256]{1,0:T(8,128)(2,1)S(1)} %get-tuple-element.81), channel_id=1, source_target_pairs={{0,1},{1,2},{2,3},{3,4},{4,5},{5,6},{6,7},{7,0},{8,9},{9,10},{10,1... | collective-permute-start | bytes 393224 | tf_op jit(solution)/shard_map/ppermute | solution.py:23
  26.0 0.6 %step.32 = (bf16[256,256]{1,0:T(8,128)(2,1)S(1)}, f32[256,256]{1,0:T(8,128)S(1)}) custom-call(bf16[256,5120]{1,0:T(8,128)(2,1)S(1)} %copy-done, s32[256,640]{1,0:T(8,128)S(1)} %get-tuple-element.48.bits, bf16[256,256]{1,0:T(8,128)(2,1)S(1)} %collective-permute-done.8.block, ...), custom_call_target="tpu_custom_call", output_to_operand_aliasing={{1}: (4, {})} | custom-call | tf_op jit(solution)/shard_map/step/pallas_call | solution.py:31
  26.5 1.6 %collective-permute-start.12 = (bf16[256,256]{1,0:T(8,128)(2,1)S(1)}, bf16[256,256]{1,0:T(8,128)(2,1)S(1)}, u32[]{:S(2)}, u32[]{:S(2)}) collective-permute-start(bf16[256,256]{1,0:T(8,128)(2,1)S(1)} %get-tuple-element.79), channel_id=1, source_target_pairs={{0,1},{1,2},{2,3},{3,4},{4,5},{5,6},{6,7},{7,0},{8,9},{9,10},{10,1... | collective-permute-start | bytes 393224 | tf_op jit(solution)/shard_map/ppermute | solution.py:23
  28.1 1.1 %collective-permute-done.15.block = bf16[256,256]{1,0:T(8,128)(2,1)S(1)} collective-permute-done((bf16[256,256]{1,0:T(8,128)(2,1)S(1)}, bf16[256,256]{1,0:T(8,128)(2,1)S(1)}, u32[]{:S(2)}, u32[]{:S(2)}) %collective-permute-start.15) | collective-permute-done | bytes 131104 | tf_op jit(solution)/shard_map/ppermute | solution.py:23
  29.8 2.3 %collective-permute-done.14.block = bf16[256,256]{1,0:T(8,128)(2,1)S(1)} collective-permute-done((bf16[256,256]{1,0:T(8,128)(2,1)S(1)}, bf16[256,256]{1,0:T(8,128)(2,1)S(1)}, u32[]{:S(2)}, u32[]{:S(2)}) %collective-permute-start.14) | collective-permute-done | bytes 131104 | tf_op jit(solution)/shard_map/ppermute | solution.py:23
  32.1 0.6 %step.34 = (bf16[256,256]{1,0:T(8,128)(2,1)S(1)}, f32[256,256]{1,0:T(8,128)S(1)}) custom-call(bf16[256,5120]{1,0:T(8,128)(2,1)S(1)} %copy-done, s32[256,640]{1,0:T(8,128)S(1)} %get-tuple-element.48.bits, bf16[256,256]{1,0:T(8,128)(2,1)S(1)} %collective-permute-done.14.block, ...), custom_call_target="tpu_custom_call", output_to_operand_aliasing={{1}: (4, {})} | custom-call | flops 200000000 | tf_op jit(solution)/shard_map/step/pallas_call | solution.py:31
  32.6 2.3 %collective-permute-done.13.block = bf16[256,256]{1,0:T(8,128)(2,1)S(1)} collective-permute-done((bf16[256,256]{1,0:T(8,128)(2,1)S(1)}, bf16[256,256]{1,0:T(8,128)(2,1)S(1)}, u32[]{:S(2)}, u32[]{:S(2)}) %collective-permute-start.13) | collective-permute-done | bytes 131104 | tf_op jit(solution)/shard_map/ppermute | solution.py:23
  34.9 0.6 %step.35 = (bf16[256,256]{1,0:T(8,128)(2,1)S(1)}, f32[256,256]{1,0:T(8,128)S(1)}) custom-call(bf16[256,5120]{1,0:T(8,128)(2,1)S(1)} %copy-done, s32[256,640]{1,0:T(8,128)S(1)} %get-tuple-element.48.bits, bf16[256,256]{1,0:T(8,128)(2,1)S(1)} %collective-permute-done.13.block, ...), custom_call_target="tpu_custom_call", output_to_operand_aliasing={{1}: (4, {})} | custom-call | flops 200000000 | tf_op jit(solution)/shard_map/step/pallas_call | solution.py:31
  35.4 2.2 %collective-permute-done.12.block = bf16[256,256]{1,0:T(8,128)(2,1)S(1)} collective-permute-done((bf16[256,256]{1,0:T(8,128)(2,1)S(1)}, bf16[256,256]{1,0:T(8,128)(2,1)S(1)}, u32[]{:S(2)}, u32[]{:S(2)}) %collective-permute-start.12) | collective-permute-done | bytes 131104 | tf_op jit(solution)/shard_map/ppermute | solution.py:23
  37.6 1.3 %last.1 = (f32[256,256]{1,0:T(8,128)}, bf16[1024,256]{1,0:T(8,128)(2,1)}) custom-call(bf16[256,5120]{1,0:T(8,128)(2,1)S(1)} %copy-done, s32[256,640]{1,0:T(8,128)S(1)} %get-tuple-element.48.bits, bf16[256,256]{1,0:T(8,128)(2,1)S(1)} %collective-permute-done.12.block, f32[256,256]{1,0:T(8,128)S(1)} %get-tuple-element.80.frames, ...), custom_call_target="tpu_custom_call" | custom-call | flops 200000000 | tf_op jit(solution)/shard_map/last/pallas_call | solution.py:31
  (22 shorter events, 3.9 us)
Async XLA Ops:
  2.4 5.1 %collective-permute-start.3 = (bf16[256,256]{1,0:T(8,128)(2,1)S(1)}, bf16[256,256]{1,0:T(8,128)(2,1)S(1)}, u32[]{:S(2)}, u32[]{:S(2)}) collective-permute-start(bf16[256,256]{1,0:T(8,128)(2,1)S(1)} %get-tuple-element.59), channel_id=1, source_target_pairs={{0,8},{8,16},{16,24},{24,0},{1,9},{9,17},{17,25},{25,1},{2,10},{10... | collective-permute-start | bytes 393224 | tf_op jit(solution)/shard_map/ppermute | solution.py:23
  3.5 4.0 %copy-start = (bf16[256,5120]{1,0:T(8,128)(2,1)S(1)}, bf16[256,5120]{1,0:T(8,128)(2,1)}, u32[]{:S(2)}) copy-start(bf16[256,5120]{1,0:T(8,128)(2,1)} %wanted.15) | copy-start | bytes 7864324
  3.5 5.4 %collective-permute-start.2 = (bf16[256,256]{1,0:T(8,128)(2,1)S(1)}, bf16[256,256]{1,0:T(8,128)(2,1)S(1)}, u32[]{:S(2)}, u32[]{:S(2)}) collective-permute-start(bf16[256,256]{1,0:T(8,128)(2,1)S(1)} %get-tuple-element.58), channel_id=1, source_target_pairs={{0,8},{8,16},{16,24},{24,0},{1,9},{9,17},{17,25},{25,1},{2,10},{10... | collective-permute-start | bytes 393224 | tf_op jit(solution)/shard_map/ppermute | solution.py:23
  6.7 4.4 %collective-permute-start.1 = (bf16[256,256]{1,0:T(8,128)(2,1)S(1)}, bf16[256,256]{1,0:T(8,128)(2,1)S(1)}, u32[]{:S(2)}, u32[]{:S(2)}) collective-permute-start(bf16[256,256]{1,0:T(8,128)(2,1)S(1)} %get-tuple-element.57), channel_id=1, source_target_pairs={{0,8},{8,16},{16,24},{24,0},{1,9},{9,17},{17,25},{25,1},{2,10},{10... | collective-permute-start | bytes 393224 | tf_op jit(solution)/shard_map/ppermute | solution.py:23
  7.3 5.2 %collective-permute-start = (bf16[256,256]{1,0:T(8,128)(2,1)S(1)}, bf16[256,256]{1,0:T(8,128)(2,1)S(1)}, u32[]{:S(2)}, u32[]{:S(2)}) collective-permute-start(bf16[256,256]{1,0:T(8,128)(2,1)S(1)} %get-tuple-element.55), channel_id=1, source_target_pairs={{0,8},{8,16},{16,24},{24,0},{1,9},{9,17},{17,25},{25,1},{2,10},{10... | collective-permute-start | bytes 393224 | tf_op jit(solution)/shard_map/ppermute | solution.py:23
  8.0 5.9 %collective-permute-start.7 = (bf16[256,256]{1,0:T(8,128)(2,1)S(1)}, bf16[256,256]{1,0:T(8,128)(2,1)S(1)}, u32[]{:S(2)}, u32[]{:S(2)}) collective-permute-start(bf16[256,256]{1,0:T(8,128)(2,1)S(1)} %get-tuple-element.67), channel_id=1, source_target_pairs={{0,8},{8,16},{16,24},{24,0},{1,9},{9,17},{17,25},{25,1},{2,10},{10... | collective-permute-start | bytes 393224 | tf_op jit(solution)/shard_map/ppermute | solution.py:23
  9.5 5.9 %collective-permute-start.6 = (bf16[256,256]{1,0:T(8,128)(2,1)S(1)}, bf16[256,256]{1,0:T(8,128)(2,1)S(1)}, u32[]{:S(2)}, u32[]{:S(2)}) collective-permute-start(bf16[256,256]{1,0:T(8,128)(2,1)S(1)} %get-tuple-element.66), channel_id=1, source_target_pairs={{0,8},{8,16},{16,24},{24,0},{1,9},{9,17},{17,25},{25,1},{2,10},{10... | collective-permute-start | bytes 393224 | tf_op jit(solution)/shard_map/ppermute | solution.py:23
  11.7 5.1 %collective-permute-start.5 = (bf16[256,256]{1,0:T(8,128)(2,1)S(1)}, bf16[256,256]{1,0:T(8,128)(2,1)S(1)}, u32[]{:S(2)}, u32[]{:S(2)}) collective-permute-start(bf16[256,256]{1,0:T(8,128)(2,1)S(1)} %get-tuple-element.65), channel_id=1, source_target_pairs={{0,8},{8,16},{16,24},{24,0},{1,9},{9,17},{17,25},{25,1},{2,10},{10... | collective-permute-start | bytes 393224 | tf_op jit(solution)/shard_map/ppermute | solution.py:23
  13.1 5.1 %collective-permute-start.4 = (bf16[256,256]{1,0:T(8,128)(2,1)S(1)}, bf16[256,256]{1,0:T(8,128)(2,1)S(1)}, u32[]{:S(2)}, u32[]{:S(2)}) collective-permute-start(bf16[256,256]{1,0:T(8,128)(2,1)S(1)} %get-tuple-element.63), channel_id=1, source_target_pairs={{0,8},{8,16},{16,24},{24,0},{1,9},{9,17},{17,25},{25,1},{2,10},{10... | collective-permute-start | bytes 393224 | tf_op jit(solution)/shard_map/ppermute | solution.py:23
  14.5 5.1 %collective-permute-start.11 = (bf16[256,256]{1,0:T(8,128)(2,1)S(1)}, bf16[256,256]{1,0:T(8,128)(2,1)S(1)}, u32[]{:S(2)}, u32[]{:S(2)}) collective-permute-start(bf16[256,256]{1,0:T(8,128)(2,1)S(1)} %get-tuple-element.75), channel_id=1, source_target_pairs={{0,8},{8,16},{16,24},{24,0},{1,9},{9,17},{17,25},{25,1},{2,10},{10... | collective-permute-start | bytes 393224 | tf_op jit(solution)/shard_map/ppermute | solution.py:23
  15.9 5.8 %collective-permute-start.10 = (bf16[256,256]{1,0:T(8,128)(2,1)S(1)}, bf16[256,256]{1,0:T(8,128)(2,1)S(1)}, u32[]{:S(2)}, u32[]{:S(2)}) collective-permute-start(bf16[256,256]{1,0:T(8,128)(2,1)S(1)} %get-tuple-element.74), channel_id=1, source_target_pairs={{0,8},{8,16},{16,24},{24,0},{1,9},{9,17},{17,25},{25,1},{2,10},{10... | collective-permute-start | bytes 393224 | tf_op jit(solution)/shard_map/ppermute | solution.py:23
  17.3 6.5 %collective-permute-start.9 = (bf16[256,256]{1,0:T(8,128)(2,1)S(1)}, bf16[256,256]{1,0:T(8,128)(2,1)S(1)}, u32[]{:S(2)}, u32[]{:S(2)}) collective-permute-start(bf16[256,256]{1,0:T(8,128)(2,1)S(1)} %get-tuple-element.73), channel_id=1, source_target_pairs={{0,8},{8,16},{16,24},{24,0},{1,9},{9,17},{17,25},{25,1},{2,10},{10... | collective-permute-start | bytes 393224 | tf_op jit(solution)/shard_map/ppermute | solution.py:23
  18.7 7.2 %collective-permute-start.8 = (bf16[256,256]{1,0:T(8,128)(2,1)S(1)}, bf16[256,256]{1,0:T(8,128)(2,1)S(1)}, u32[]{:S(2)}, u32[]{:S(2)}) collective-permute-start(bf16[256,256]{1,0:T(8,128)(2,1)S(1)} %get-tuple-element.71), channel_id=1, source_target_pairs={{0,8},{8,16},{16,24},{24,0},{1,9},{9,17},{17,25},{25,1},{2,10},{10... | collective-permute-start | bytes 393224 | tf_op jit(solution)/shard_map/ppermute | solution.py:23
  20.1 9.1 %collective-permute-start.15 = (bf16[256,256]{1,0:T(8,128)(2,1)S(1)}, bf16[256,256]{1,0:T(8,128)(2,1)S(1)}, u32[]{:S(2)}, u32[]{:S(2)}) collective-permute-start(bf16[256,256]{1,0:T(8,128)(2,1)S(1)} %get-tuple-element.83), channel_id=1, source_target_pairs={{0,1},{1,2},{2,3},{3,4},{4,5},{5,6},{6,7},{7,0},{8,9},{9,10},{10,1... | collective-permute-start | bytes 393224 | tf_op jit(solution)/shard_map/ppermute | solution.py:23
  22.3 9.8 %collective-permute-start.14 = (bf16[256,256]{1,0:T(8,128)(2,1)S(1)}, bf16[256,256]{1,0:T(8,128)(2,1)S(1)}, u32[]{:S(2)}, u32[]{:S(2)}) collective-permute-start(bf16[256,256]{1,0:T(8,128)(2,1)S(1)} %get-tuple-element.82), channel_id=1, source_target_pairs={{0,1},{1,2},{2,3},{3,4},{4,5},{5,6},{6,7},{7,0},{8,9},{9,10},{10,1... | collective-permute-start | bytes 393224 | tf_op jit(solution)/shard_map/ppermute | solution.py:23
  24.4 10.5 %collective-permute-start.13 = (bf16[256,256]{1,0:T(8,128)(2,1)S(1)}, bf16[256,256]{1,0:T(8,128)(2,1)S(1)}, u32[]{:S(2)}, u32[]{:S(2)}) collective-permute-start(bf16[256,256]{1,0:T(8,128)(2,1)S(1)} %get-tuple-element.81), channel_id=1, source_target_pairs={{0,1},{1,2},{2,3},{3,4},{4,5},{5,6},{6,7},{7,0},{8,9},{9,10},{10,1... | collective-permute-start | bytes 393224 | tf_op jit(solution)/shard_map/ppermute | solution.py:23
  26.5 11.1 %collective-permute-start.12 = (bf16[256,256]{1,0:T(8,128)(2,1)S(1)}, bf16[256,256]{1,0:T(8,128)(2,1)S(1)}, u32[]{:S(2)}, u32[]{:S(2)}) collective-permute-start(bf16[256,256]{1,0:T(8,128)(2,1)S(1)} %get-tuple-element.79), channel_id=1, source_target_pairs={{0,1},{1,2},{2,3},{3,4},{4,5},{5,6},{6,7},{7,0},{8,9},{9,10},{10,1... | collective-permute-start | bytes 393224 | tf_op jit(solution)/shard_map/ppermute | solution.py:23

commit v4 on v3

--- a/solution.py
+++ b/solution.py
@@ -21,6 +21,15 @@
 def shifted(value, axis):
     count = lax.axis_size(axis)
     return lax.ppermute(value, axis, [(s, (s + 1) % count) for s in range(count)])
+
+
+def swapped(value):
+    count = lax.axis_size("blk")
+    return lax.ppermute(value, "blk", [(s, s + 1 - 2 * (s % 2)) for s in range(count)])
+
+
+def is_odd():
+    return lax.axis_index("blk") % 2 == 1
 
 
 def struct(shape, dtype=LOW):
@@ -82,75 +91,122 @@
     size = width // CHUNKS
     chunk_t = struct((size, rank))
     frames_t = struct((rows, rank), jnp.float32)
-    whole = observed
-    observed, mask_bits, frame_factors, pixel_factors = (
-        pltpu.with_memory_space_constraint(a, pltpu.HBM)
-        for a in (observed, mask_bits, frame_factors, pixel_factors)
-    )
-
-    def load_kernel(observed, mask_bits, frames_in, pixels_in, observed0, bits, pixels, frames, new, done, sems):
-        first = [
-            pltpu.make_async_copy(mask_bits.at[:, :size], bits.at[:, :size], sems.at[0]),
-            pltpu.make_async_copy(pixels_in.at[:size], pixels.at[:size], sems.at[1]),
-            pltpu.make_async_copy(observed.at[:, :size], observed0.at[:, :size], sems.at[2]),
-            pltpu.make_async_copy(frames_in, frames, sems.at[3]),
-        ]
-        rest = [
-            pltpu.make_async_copy(pixels_in.at[size:], pixels.at[size:], sems.at[4]),
-            pltpu.make_async_copy(observed.at[:, size:width], observed0.at[:, size:], sems.at[5]),
-            pltpu.make_async_copy(mask_bits.at[:, size:], bits.at[:, size:], sems.at[6]),
-        ]
-        for copy in first + rest:
-            copy.start()
-        for copy in first:
-            copy.wait()
-        new[...], grad = tile(frames[...], pixels[:size], observed0[:, :size], flags(bits, 0, size))
-        done[...] = added(frames[...], None, grad)
-        for copy in rest:
-            copy.wait()
-
-    observed0, bits, pixels, frames, new, done = call(
+    early = 2 * size
+    early_words = min(early, mask_bits.shape[1])
+
+    def load_kernel(observed, mask_bits, frames_in, pixels_in, new, done, wanted, bits, frames, pixels, sems):
+        @pl.when(is_odd())
+        def _():
+            copies = [
+                pltpu.make_async_copy(mask_bits.at[:, :early_words], bits, sems.at[0]),
+                pltpu.make_async_copy(pixels_in.at[:early], pixels, sems.at[1]),
+                pltpu.make_async_copy(observed.at[:, :early], wanted, sems.at[2]),
+                pltpu.make_async_copy(frames_in, frames, sems.at[3]),
+            ]
+            for copy in copies:
+                copy.start()
+            for copy in copies:
+                copy.wait()
+            new[...], grad = tile(frames[...], pixels[...], wanted[...], flags(bits, 0, early))
+            done[...] = added(frames[...], None, grad)
+
+    new, done = call(
         "load",
         load_kernel,
-        [observed, mask_bits, frame_factors, pixel_factors],
         [
-            struct((rows, width)),
-            struct(mask_bits.shape, mask_bits.dtype),
-            struct((width, rank)),
-            frames_t,
-            chunk_t,
-            frames_t,
+            pltpu.with_memory_space_constraint(a, pltpu.HBM)
+            for a in (observed, mask_bits, frame_factors, pixel_factors)
         ],
+        [struct((early, rank)), frames_t],
         in_specs=[HBM] * 4,
-        scratch=[DMA((7,))],
-    )
+        scratch=[
+            pltpu.VMEM((rows, early), LOW),
+            pltpu.VMEM((rows, early_words), mask_bits.dtype),
+            pltpu.VMEM((rows, rank), jnp.float32),
+            pltpu.VMEM((early, rank), LOW),
+            DMA((4,)),
+        ],
+    )
+    later, new = lax.optimization_barrier((observed, new))
+    arrived = shifted(new, "blk")
+    observed0, bits, pixels, frames = observed[:, :width], mask_bits, pixel_factors, frame_factors
+
+    def third_kernel(observed0, bits, pixels, frames, done, new, done_out):
+        new[...], grad = tile(
+            frames[...],
+            pixels[early : early + size],
+            observed0[:, early : early + size],
+            flags(bits, early, size),
+        )
+        start = added(frames[...], None, jnp.zeros_like(grad))
+        done_out[...] = jnp.where(is_odd(), done[...], start) + step_frames * grad
+
+    new, done = call(
+        "third",
+        third_kernel,
+        [observed0, bits, pixels, frames, done],
+        [chunk_t, frames_t],
+        aliases={4: 1},
+    )
+    third = shifted(new, "blk")
+
+    def even_kernel(observed0, bits, pixels, frames, done, new0, new1, done_out):
+        @pl.when(is_odd())
+        def _():
+            done_out[...] = done[...]
+
+        @pl.when(jnp.logical_not(is_odd()))
+        def _():
+            made, grad = tile(
+                frames[...], pixels[:early], observed0[:, :early], flags(bits, 0, early)
+            )
+            new0[...] = made[:size]
+            new1[...] = made[size:]
+            done_out[...] = done[...] + step_frames * grad
+
+    new0, new1, done = call(
+        "even",
+        even_kernel,
+        [observed0, bits, pixels, frames, done],
+        [chunk_t, chunk_t, frames_t],
+        aliases={4: 2},
+    )
+    coming = [(arrived, swapped(new0), 0), (arrived, swapped(new1), size), third]
+
     def step(visit, chunk, block, frames, done, wanted):
         at = chunk * size
         first = done is None
-        whole = block.shape[0] > size
+        whole = visit == 0
         columns = visit * width + at
 
-        def kernel(wanted, bits, block, frames, *refs):
-            block = block[at : at + size] if whole else block[...]
+        split = isinstance(block, tuple)
+
+        def kernel(wanted, bits, frames, *refs):
+            if split:
+                start = block[2]
+                held = jnp.where(is_odd(), refs[1][...], refs[0][start : start + size])
+                refs = refs[2:]
+            else:
+                held = refs[0][at : at + size] if whole else refs[0][...]
+                refs = refs[1:]
             new, grad = tile(
-                frames[...], block, wanted[:, columns : columns + size], flags(bits, visit * width + at, size)
+                frames[...], held, wanted[:, columns : columns + size], flags(bits, visit * width + at, size)
             )
             refs[-2][...] = new
             refs[-1][...] = added(frames[...], None if first else refs[0][...], grad)
 
-        args = [wanted, bits, block, frames] + ([] if first else [done])
+        blocks = list(block[:2]) if split else [block]
+        args = [wanted, bits, frames, *blocks] + ([] if first else [done])
         return call(
             "step",
             kernel,
             args,
             [chunk_t, frames_t],
-            aliases={} if first else {4: 1},
+            aliases={} if first else {len(args) - 1: 1},
             flops=LAST_FLOPS if visit == visits - 1 else 0,
         )
 
-    later, new = lax.optimization_barrier((whole, new))
-    coming = [shifted(new, "blk")]
-    for c in range(1, CHUNKS):
+    for c in range(3, CHUNKS):
         new, done = step(0, c, pixels, frames, done, observed0)
         coming.append(shifted(new, "blk"))
 

time: 39 us -> 38.4 us (0.985)
  waiting for transfers between devices: 8.54 us -> 11.9 us
  starting transfers between devices: 16.6 us -> 14.1 us
  Pallas kernels: 12.9 us -> 11.4 us
    ppermute x16 -> x15, waiting for transfers between devices: 8.54 us -> 11.9 us  [shifted(): lax.ppermute(value, axis, [(s, (s + 1) % count) for s in range(count)])]
    ppermute x16 -> x15, starting transfers between devices: 16.6 us -> 13.5 us  [shifted(): lax.ppermute(value, axis, [(s, (s + 1) % count) for s in range(count)])]
    pallas_call x20, Pallas kernels: 12.9 us -> 11.4 us  [call(): pl.pallas_call(kernel, name=name, out_shape=tuple(outs), in_specs=in_spec...]
    ppermute x0 -> x2, starting transfers between devices: none -> 0.58 us  [swapped(): lax.ppermute(value, 'blk', [(s, s + 1 - 2 * (s % 2)) for s in range(count)])]
  transfers between devices with their start and end apart: 16 -> 17, of which waited for: 6 -> 11; matrix products, arithmetic and copies ran while one was open for 0% -> 0% of each run, Pallas kernels for 25% -> 26%
where the time goes in v4:
time: 38.4 us; the launch traced here: 38.3 us
  starting transfers between devices  14.1 us (37%)
  waiting for transfers between devices  11.9 us (31%)
  Pallas kernels  11.4 us (30%)
  between operations  0.9 us (2%)
    ppermute x15, starting transfers between devices, shifted(): lax.ppermute(value, axis, [(s, (s + 1) % count) for s in range(count)])  13.5 us
    ppermute x15, waiting for transfers between devices, shifted(): lax.ppermute(value, axis, [(s, (s + 1) % count) for s in range(count)])  11.9 us
    pallas_call x20, Pallas kernels, call(): pl.pallas_call(kernel, name=name, out_shape=tuple(outs), in_specs=in_spec...  11.4 us
  transfers between devices with their start and end apart: 17, of which 11 were waited for; matrix products, arithmetic and copies ran while one was open for 0% of the time, Pallas kernels for 26%

profile of v4, /device:TPU:0, one launch (start us, length us, event | category | flops | bytes accessed | tf_op | source)
XLA Modules:
  0.0 38.3 jit_solution(5242234509487165253)
XLA Ops:
  0.7 2.5 %collective-permute-start.2 = (bf16[512,256]{1,0:T(8,128)(2,1)S(1)}, bf16[512,256]{1,0:T(8,128)(2,1)S(1)}, u32[]{:S(2)}, u32[]{:S(2)}) collective-permute-start(bf16[512,256]{1,0:T(8,128)(2,1)S(1)} %get-tuple-element.51), channel_id=1, source_target_pairs={{0,8},{8,16},{16,24},{24,0},{1,9},{9,17},{17,25},{25,1},{2,10},{10... | collective-permute-start | bytes 786440 | tf_op jit(solution)/shard_map/ppermute | solution.py:23
  3.3 0.6 %third.1 = (bf16[256,256]{1,0:T(8,128)(2,1)S(1)}, f32[256,256]{1,0:T(8,128)S(1)}) custom-call(bf16[256,1024]{1,0:T(8,128)(2,1)S(1)} %slice.3.observed0.wanted, s32[256,640]{1,0:T(8,128)S(1)} %copy-done.1, bf16[1024,256]{1,0:T(8,128)(2,1)S(1)} %copy-done.2, f32[256,256]{1,0:T(8,128)S(1)} %copy-done.3, ...), custom_call_target="tpu_custom_call", output_to_operand_aliasing={{1}: (4, {})} | custom-call | tf_op jit(solution)/shard_map/third/pallas_call | solution.py:40
  3.9 0.6 %even.1 = (bf16[256,256]{1,0:T(8,128)(2,1)S(1)}, bf16[256,256]{1,0:T(8,128)(2,1)S(1)}, f32[256,256]{1,0:T(8,128)S(1)}) custom-call(bf16[256,1024]{1,0:T(8,128)(2,1)S(1)} %slice.3.observed0.wanted, s32[256,640]{1,0:T(8,128)S(1)} %copy-done.1, bf16[1024,256]{1,0:T(8,128)(2,1)S(1)} %copy-done.2, ...), custom_call_target="tpu_custom_call", output_to_operand_aliasing={{2}: (4, {})} | custom-call | tf_op jit(solution)/shard_map/even/pallas_call | solution.py:40
  5.2 0.5 %step.16 = (bf16[256,256]{1,0:T(8,128)(2,1)S(1)}, f32[256,256]{1,0:T(8,128)S(1)}) custom-call(bf16[256,1024]{1,0:T(8,128)(2,1)S(1)} %slice.3.observed0.wanted, s32[256,640]{1,0:T(8,128)S(1)} %copy-done.1, f32[256,256]{1,0:T(8,128)S(1)} %copy-done.3, bf16[1024,256]{1,0:T(8,128)(2,1)S(1)} %copy-done.2, ...), custom_call_target="tpu_custom_call", output_to_operand_aliasing={{1}: (4, {})} | custom-call | tf_op jit(solution)/shard_map/step/pallas_call | solution.py:40
  5.7 2.5 %collective-permute-start = (bf16[256,256]{1,0:T(8,128)(2,1)S(1)}, bf16[256,256]{1,0:T(8,128)(2,1)S(1)}, u32[]{:S(2)}, u32[]{:S(2)}) collective-permute-start(bf16[256,256]{1,0:T(8,128)(2,1)S(1)} %get-tuple-element.49), channel_id=1, source_target_pairs={{0,8},{8,16},{16,24},{24,0},{1,9},{9,17},{17,25},{25,1},{2,10},{10... | collective-permute-start | bytes 393224 | tf_op jit(solution)/shard_map/ppermute | solution.py:23
  8.2 1.0 %collective-permute-done.2.refs_0_ = bf16[512,256]{1,0:T(8,128)(2,1)S(1)} collective-permute-done((bf16[512,256]{1,0:T(8,128)(2,1)S(1)}, bf16[512,256]{1,0:T(8,128)(2,1)S(1)}, u32[]{:S(2)}, u32[]{:S(2)}) %collective-permute-start.2) | collective-permute-done | bytes 262176 | tf_op jit(solution)/shard_map/ppermute | solution.py:23
  9.2 0.6 %step.17 = (bf16[256,256]{1,0:T(8,128)(2,1)S(1)}, f32[256,256]{1,0:T(8,128)S(1)}) custom-call(bf16[256,5120]{1,0:T(8,128)(2,1)S(1)} %copy-done, s32[256,640]{1,0:T(8,128)S(1)} %copy-done.1, f32[256,256]{1,0:T(8,128)S(1)} %get-tuple-element.48.frames, bf16[512,256]{1,0:T(8,128)(2,1)S(1)} %collective-permute-done.2.refs_0_, ...), custom_call_target="tpu_custom_call" | custom-call | tf_op jit(solution)/shard_map/step/pallas_call | solution.py:40
  9.8 0.6 %step.18 = (bf16[256,256]{1,0:T(8,128)(2,1)S(1)}, f32[256,256]{1,0:T(8,128)S(1)}) custom-call(bf16[256,5120]{1,0:T(8,128)(2,1)S(1)} %copy-done, s32[256,640]{1,0:T(8,128)S(1)} %copy-done.1, f32[256,256]{1,0:T(8,128)S(1)} %get-tuple-element.48.frames, bf16[512,256]{1,0:T(8,128)(2,1)S(1)} %collective-permute-done.2.refs_0_, ...), custom_call_target="tpu_custom_call", output_to_operand_aliasing={{1}: (5, {})} | custom-call | tf_op jit(solution)/shard_map/step/pallas_call | solution.py:40
  10.9 0.6 %step.19 = (bf16[256,256]{1,0:T(8,128)(2,1)S(1)}, f32[256,256]{1,0:T(8,128)S(1)}) custom-call(bf16[256,5120]{1,0:T(8,128)(2,1)S(1)} %copy-done, s32[256,640]{1,0:T(8,128)S(1)} %copy-done.1, f32[256,256]{1,0:T(8,128)S(1)} %get-tuple-element.48.frames, bf16[256,256]{1,0:T(8,128)(2,1)S(1)} %collective-permute-done.1.refs_0_, ...), custom_call_target="tpu_custom_call", output_to_operand_aliasing={{1}: (4, {})} | custom-call | tf_op jit(solution)/shard_map/step/pallas_call | solution.py:40
  12.0 0.6 %step.20 = (bf16[256,256]{1,0:T(8,128)(2,1)S(1)}, f32[256,256]{1,0:T(8,128)S(1)}) custom-call(bf16[256,5120]{1,0:T(8,128)(2,1)S(1)} %copy-done, s32[256,640]{1,0:T(8,128)S(1)} %copy-done.1, f32[256,256]{1,0:T(8,128)S(1)} %get-tuple-element.48.frames, bf16[256,256]{1,0:T(8,128)(2,1)S(1)} %collective-permute-done.refs_0_, ...), custom_call_target="tpu_custom_call", output_to_operand_aliasing={{1}: (4, {})} | custom-call | tf_op jit(solution)/shard_map/step/pallas_call | solution.py:40
  12.6 1.4 %collective-permute-start.5 = (bf16[256,256]{1,0:T(8,128)(2,1)S(1)}, bf16[256,256]{1,0:T(8,128)(2,1)S(1)}, u32[]{:S(2)}, u32[]{:S(2)}) collective-permute-start(bf16[256,256]{1,0:T(8,128)(2,1)S(1)} %get-tuple-element.58), channel_id=1, source_target_pairs={{0,8},{8,16},{16,24},{24,0},{1,9},{9,17},{17,25},{25,1},{2,10},{10... | collective-permute-start | bytes 393224 | tf_op jit(solution)/shard_map/ppermute | solution.py:23
  14.8 0.8 %collective-permute-done.7.refs_0_ = bf16[256,256]{1,0:T(8,128)(2,1)S(1)} collective-permute-done((bf16[256,256]{1,0:T(8,128)(2,1)S(1)}, bf16[256,256]{1,0:T(8,128)(2,1)S(1)}, u32[]{:S(2)}, u32[]{:S(2)}) %collective-permute-start.7) | collective-permute-done | bytes 131104 | tf_op jit(solution)/shard_map/ppermute | solution.py:23
  15.6 0.6 %step.22 = (bf16[256,256]{1,0:T(8,128)(2,1)S(1)}, f32[256,256]{1,0:T(8,128)S(1)}) custom-call(bf16[256,5120]{1,0:T(8,128)(2,1)S(1)} %copy-done, s32[256,640]{1,0:T(8,128)S(1)} %copy-done.1, f32[256,256]{1,0:T(8,128)S(1)} %get-tuple-element.57.frames, bf16[256,256]{1,0:T(8,128)(2,1)S(1)} %collective-permute-done.7.refs_0_, ...), custom_call_target="tpu_custom_call", output_to_operand_aliasing={{1}: (4, {})} | custom-call | tf_op jit(solution)/shard_map/step/pallas_call | solution.py:40
  16.2 0.8 %collective-permute-done.6.refs_0_ = bf16[256,256]{1,0:T(8,128)(2,1)S(1)} collective-permute-done((bf16[256,256]{1,0:T(8,128)(2,1)S(1)}, bf16[256,256]{1,0:T(8,128)(2,1)S(1)}, u32[]{:S(2)}, u32[]{:S(2)}) %collective-permute-start.6) | collective-permute-done | bytes 131104 | tf_op jit(solution)/shard_map/ppermute | solution.py:23
  17.0 0.6 %step.23 = (bf16[256,256]{1,0:T(8,128)(2,1)S(1)}, f32[256,256]{1,0:T(8,128)S(1)}) custom-call(bf16[256,5120]{1,0:T(8,128)(2,1)S(1)} %copy-done, s32[256,640]{1,0:T(8,128)S(1)} %copy-done.1, f32[256,256]{1,0:T(8,128)S(1)} %get-tuple-element.57.frames, bf16[256,256]{1,0:T(8,128)(2,1)S(1)} %collective-permute-done.6.refs_0_, ...), custom_call_target="tpu_custom_call", output_to_operand_aliasing={{1}: (4, {})} | custom-call | tf_op jit(solution)/shard_map/step/pallas_call | solution.py:40
  17.6 0.8 %collective-permute-done.5.refs_0_ = bf16[256,256]{1,0:T(8,128)(2,1)S(1)} collective-permute-done((bf16[256,256]{1,0:T(8,128)(2,1)S(1)}, bf16[256,256]{1,0:T(8,128)(2,1)S(1)}, u32[]{:S(2)}, u32[]{:S(2)}) %collective-permute-start.5) | collective-permute-done | bytes 131104 | tf_op jit(solution)/shard_map/ppermute | solution.py:23
  18.4 0.6 %step.24 = (bf16[256,256]{1,0:T(8,128)(2,1)S(1)}, f32[256,256]{1,0:T(8,128)S(1)}) custom-call(bf16[256,5120]{1,0:T(8,128)(2,1)S(1)} %copy-done, s32[256,640]{1,0:T(8,128)S(1)} %copy-done.1, f32[256,256]{1,0:T(8,128)S(1)} %get-tuple-element.57.frames, bf16[256,256]{1,0:T(8,128)(2,1)S(1)} %collective-permute-done.5.refs_0_, ...), custom_call_target="tpu_custom_call", output_to_operand_aliasing={{1}: (4, {})} | custom-call | tf_op jit(solution)/shard_map/step/pallas_call | solution.py:40
  19.1 0.8 %collective-permute-done.12.refs_0_ = bf16[256,256]{1,0:T(8,128)(2,1)S(1)} collective-permute-done((bf16[256,256]{1,0:T(8,128)(2,1)S(1)}, bf16[256,256]{1,0:T(8,128)(2,1)S(1)}, u32[]{:S(2)}, u32[]{:S(2)}) %collective-permute-start.12) | collective-permute-done | bytes 131104 | tf_op jit(solution)/shard_map/ppermute | solution.py:23
  20.4 1.6 %collective-permute-start.16 = (bf16[256,256]{1,0:T(8,128)(2,1)S(1)}, bf16[256,256]{1,0:T(8,128)(2,1)S(1)}, u32[]{:S(2)}, u32[]{:S(2)}) collective-permute-start(bf16[256,256]{1,0:T(8,128)(2,1)S(1)} %get-tuple-element.77), channel_id=1, source_target_pairs={{0,1},{1,2},{2,3},{3,4},{4,5},{5,6},{6,7},{7,0},{8,9},{9,10},{10,1... | collective-permute-start | bytes 393224 | tf_op jit(solution)/shard_map/ppermute | solution.py:23
  22.0 0.6 %step.26 = (bf16[256,256]{1,0:T(8,128)(2,1)S(1)}, f32[256,256]{1,0:T(8,128)S(1)}) custom-call(bf16[256,5120]{1,0:T(8,128)(2,1)S(1)} %copy-done, s32[256,640]{1,0:T(8,128)S(1)} %copy-done.1, f32[256,256]{1,0:T(8,128)S(1)} %get-tuple-element.65.frames, bf16[256,256]{1,0:T(8,128)(2,1)S(1)} %collective-permute-done.11.refs_0_, ...), custom_call_target="tpu_custom_call", output_to_operand_aliasing={{1}: (4, {})} | custom-call | tf_op jit(solution)/shard_map/step/pallas_call | solution.py:40
  22.5 1.6 %collective-permute-start.15 = (bf16[256,256]{1,0:T(8,128)(2,1)S(1)}, bf16[256,256]{1,0:T(8,128)(2,1)S(1)}, u32[]{:S(2)}, u32[]{:S(2)}) collective-permute-start(bf16[256,256]{1,0:T(8,128)(2,1)S(1)} %get-tuple-element.76), channel_id=1, source_target_pairs={{0,1},{1,2},{2,3},{3,4},{4,5},{5,6},{6,7},{7,0},{8,9},{9,10},{10,1... | collective-permute-start | bytes 393224 | tf_op jit(solution)/shard_map/ppermute | solution.py:23
  24.1 0.6 %step.27 = (bf16[256,256]{1,0:T(8,128)(2,1)S(1)}, f32[256,256]{1,0:T(8,128)S(1)}) custom-call(bf16[256,5120]{1,0:T(8,128)(2,1)S(1)} %copy-done, s32[256,640]{1,0:T(8,128)S(1)} %copy-done.1, f32[256,256]{1,0:T(8,128)S(1)} %get-tuple-element.65.frames, bf16[256,256]{1,0:T(8,128)(2,1)S(1)} %collective-permute-done.10.refs_0_, ...), custom_call_target="tpu_custom_call", output_to_operand_aliasing={{1}: (4, {})} | custom-call | tf_op jit(solution)/shard_map/step/pallas_call | solution.py:40
  24.7 1.6 %collective-permute-start.14 = (bf16[256,256]{1,0:T(8,128)(2,1)S(1)}, bf16[256,256]{1,0:T(8,128)(2,1)S(1)}, u32[]{:S(2)}, u32[]{:S(2)}) collective-permute-start(bf16[256,256]{1,0:T(8,128)(2,1)S(1)} %get-tuple-element.75), channel_id=1, source_target_pairs={{0,1},{1,2},{2,3},{3,4},{4,5},{5,6},{6,7},{7,0},{8,9},{9,10},{10,1... | collective-permute-start | bytes 393224 | tf_op jit(solution)/shard_map/ppermute | solution.py:23
  26.2 0.6 %step.28 = (bf16[256,256]{1,0:T(8,128)(2,1)S(1)}, f32[256,256]{1,0:T(8,128)S(1)}) custom-call(bf16[256,5120]{1,0:T(8,128)(2,1)S(1)} %copy-done, s32[256,640]{1,0:T(8,128)S(1)} %copy-done.1, f32[256,256]{1,0:T(8,128)S(1)} %get-tuple-element.65.frames, bf16[256,256]{1,0:T(8,128)(2,1)S(1)} %collective-permute-done.9.refs_0_, ...), custom_call_target="tpu_custom_call", output_to_operand_aliasing={{1}: (4, {})} | custom-call | tf_op jit(solution)/shard_map/step/pallas_call | solution.py:40
  26.8 1.6 %collective-permute-start.13 = (bf16[256,256]{1,0:T(8,128)(2,1)S(1)}, bf16[256,256]{1,0:T(8,128)(2,1)S(1)}, u32[]{:S(2)}, u32[]{:S(2)}) collective-permute-start(bf16[256,256]{1,0:T(8,128)(2,1)S(1)} %get-tuple-element.73), channel_id=1, source_target_pairs={{0,1},{1,2},{2,3},{3,4},{4,5},{5,6},{6,7},{7,0},{8,9},{9,10},{10,1... | collective-permute-start | bytes 393224 | tf_op jit(solution)/shard_map/ppermute | solution.py:23
  28.4 1.1 %collective-permute-done.16.refs_0_ = bf16[256,256]{1,0:T(8,128)(2,1)S(1)} collective-permute-done((bf16[256,256]{1,0:T(8,128)(2,1)S(1)}, bf16[256,256]{1,0:T(8,128)(2,1)S(1)}, u32[]{:S(2)}, u32[]{:S(2)}) %collective-permute-start.16) | collective-permute-done | bytes 131104 | tf_op jit(solution)/shard_map/ppermute | solution.py:23
  30.0 2.3 %collective-permute-done.15.refs_0_ = bf16[256,256]{1,0:T(8,128)(2,1)S(1)} collective-permute-done((bf16[256,256]{1,0:T(8,128)(2,1)S(1)}, bf16[256,256]{1,0:T(8,128)(2,1)S(1)}, u32[]{:S(2)}, u32[]{:S(2)}) %collective-permute-start.15) | collective-permute-done | bytes 131104 | tf_op jit(solution)/shard_map/ppermute | solution.py:23
  32.3 0.6 %step.30 = (bf16[256,256]{1,0:T(8,128)(2,1)S(1)}, f32[256,256]{1,0:T(8,128)S(1)}) custom-call(bf16[256,5120]{1,0:T(8,128)(2,1)S(1)} %copy-done, s32[256,640]{1,0:T(8,128)S(1)} %copy-done.1, f32[256,256]{1,0:T(8,128)S(1)} %get-tuple-element.74.frames, bf16[256,256]{1,0:T(8,128)(2,1)S(1)} %collective-permute-done.15.refs_0_, ...), custom_call_target="tpu_custom_call", output_to_operand_aliasing={{1}: (4, {})} | custom-call | flops 200000000 | tf_op jit(solution)/shard_map/step/pallas_call | solution.py:40
  32.9 2.3 %collective-permute-done.14.refs_0_ = bf16[256,256]{1,0:T(8,128)(2,1)S(1)} collective-permute-done((bf16[256,256]{1,0:T(8,128)(2,1)S(1)}, bf16[256,256]{1,0:T(8,128)(2,1)S(1)}, u32[]{:S(2)}, u32[]{:S(2)}) %collective-permute-start.14) | collective-permute-done | bytes 131104 | tf_op jit(solution)/shard_map/ppermute | solution.py:23
  35.1 0.6 %step.31 = (bf16[256,256]{1,0:T(8,128)(2,1)S(1)}, f32[256,256]{1,0:T(8,128)S(1)}) custom-call(bf16[256,5120]{1,0:T(8,128)(2,1)S(1)} %copy-done, s32[256,640]{1,0:T(8,128)S(1)} %copy-done.1, f32[256,256]{1,0:T(8,128)S(1)} %get-tuple-element.74.frames, bf16[256,256]{1,0:T(8,128)(2,1)S(1)} %collective-permute-done.14.refs_0_, ...), custom_call_target="tpu_custom_call", output_to_operand_aliasing={{1}: (4, {})} | custom-call | flops 200000000 | tf_op jit(solution)/shard_map/step/pallas_call | solution.py:40
  35.7 1.3 %collective-permute-done.13.block = bf16[256,256]{1,0:T(8,128)(2,1)S(1)} collective-permute-done((bf16[256,256]{1,0:T(8,128)(2,1)S(1)}, bf16[256,256]{1,0:T(8,128)(2,1)S(1)}, u32[]{:S(2)}, u32[]{:S(2)}) %collective-permute-start.13) | collective-permute-done | bytes 131104 | tf_op jit(solution)/shard_map/ppermute | solution.py:23
  37.0 1.3 %last.1 = (f32[256,256]{1,0:T(8,128)}, bf16[1024,256]{1,0:T(8,128)(2,1)}) custom-call(bf16[256,5120]{1,0:T(8,128)(2,1)S(1)} %copy-done, s32[256,640]{1,0:T(8,128)S(1)} %copy-done.1, bf16[256,256]{1,0:T(8,128)(2,1)S(1)} %collective-permute-done.13.block, f32[256,256]{1,0:T(8,128)S(1)} %get-tuple-element.74.frames, f32[256,256]{1,0:T(8,128)S(1)} %get-tuple-element.80.done, ...), custom_call_target="tpu_custom_call" | custom-call | flops 200000000 | tf_op jit(solution)/shard_map/last/pallas_call | solution.py:40
  (31 shorter events, 4.0 us)
Async XLA Ops:
  0.6 2.6 %copy-start.1 = (s32[256,640]{1,0:T(8,128)S(1)}, s32[256,640]{1,0:T(8,128)}, u32[]{:S(2)}) copy-start(s32[256,640]{1,0:T(8,128)} %bits.37) | copy-start | bytes 1966084
  0.6 2.6 %copy-start.2 = (bf16[1024,256]{1,0:T(8,128)(2,1)S(1)}, bf16[1024,256]{1,0:T(8,128)(2,1)}, u32[]{:S(2)}) copy-start(bf16[1024,256]{1,0:T(8,128)(2,1)} %refs_0_.1) | copy-start | bytes 1572868
  0.7 2.6 %copy-start.3 = (f32[256,256]{1,0:T(8,128)S(1)}, f32[256,256]{1,0:T(8,128)}, u32[]{:S(2)}) copy-start(f32[256,256]{1,0:T(8,128)} %frames.5) | copy-start | bytes 786436
  0.7 2.6 %copy-start = (bf16[256,5120]{1,0:T(8,128)(2,1)S(1)}, bf16[256,5120]{1,0:T(8,128)(2,1)}, u32[]{:S(2)}) copy-start(bf16[256,5120]{1,0:T(8,128)(2,1)} %wanted.15) | copy-start | bytes 7864324
  0.7 8.5 %collective-permute-start.2 = (bf16[512,256]{1,0:T(8,128)(2,1)S(1)}, bf16[512,256]{1,0:T(8,128)(2,1)S(1)}, u32[]{:S(2)}, u32[]{:S(2)}) collective-permute-start(bf16[512,256]{1,0:T(8,128)(2,1)S(1)} %get-tuple-element.51), channel_id=1, source_target_pairs={{0,8},{8,16},{16,24},{24,0},{1,9},{9,17},{17,25},{25,1},{2,10},{10... | collective-permute-start | bytes 786440 | tf_op jit(solution)/shard_map/ppermute | solution.py:23
  4.5 3.7 %collective-permute-start.4 = (bf16[256,256]{1,0:T(8,128)(2,1)S(1)}, bf16[256,256]{1,0:T(8,128)(2,1)S(1)}, u32[]{:S(2)}, u32[]{:S(2)}) collective-permute-start(bf16[256,256]{1,0:T(8,128)(2,1)S(1)} %get-tuple-element.53), channel_id=1, source_target_pairs={{0,8},{8,0},{16,24},{24,16},{1,9},{9,1},{17,25},{25,17},{2,10},{10... | collective-permute-start | bytes 393224 | tf_op jit(solution)/shard_map/ppermute | solution.py:28
  4.6 5.2 %collective-permute-start.3 = (bf16[256,256]{1,0:T(8,128)(2,1)S(1)}, bf16[256,256]{1,0:T(8,128)(2,1)S(1)}, u32[]{:S(2)}, u32[]{:S(2)}) collective-permute-start(bf16[256,256]{1,0:T(8,128)(2,1)S(1)} %get-tuple-element.52), channel_id=1, source_target_pairs={{0,8},{8,0},{16,24},{24,16},{1,9},{9,1},{17,25},{25,17},{2,10},{10... | collective-permute-start | bytes 393224 | tf_op jit(solution)/shard_map/ppermute | solution.py:28
  5.1 5.8 %collective-permute-start.1 = (bf16[256,256]{1,0:T(8,128)(2,1)S(1)}, bf16[256,256]{1,0:T(8,128)(2,1)S(1)}, u32[]{:S(2)}, u32[]{:S(2)}) collective-permute-start(bf16[256,256]{1,0:T(8,128)(2,1)S(1)} %get-tuple-element.50), channel_id=1, source_target_pairs={{0,8},{8,16},{16,24},{24,0},{1,9},{9,17},{17,25},{25,1},{2,10},{10... | collective-permute-start | bytes 393224 | tf_op jit(solution)/shard_map/ppermute | solution.py:23
  5.7 6.3 %collective-permute-start = (bf16[256,256]{1,0:T(8,128)(2,1)S(1)}, bf16[256,256]{1,0:T(8,128)(2,1)S(1)}, u32[]{:S(2)}, u32[]{:S(2)}) collective-permute-start(bf16[256,256]{1,0:T(8,128)(2,1)S(1)} %get-tuple-element.49), channel_id=1, source_target_pairs={{0,8},{8,16},{16,24},{24,0},{1,9},{9,17},{17,25},{25,1},{2,10},{10... | collective-permute-start | bytes 393224 | tf_op jit(solution)/shard_map/ppermute | solution.py:23
  9.8 4.4 %collective-permute-start.8 = (bf16[256,256]{1,0:T(8,128)(2,1)S(1)}, bf16[256,256]{1,0:T(8,128)(2,1)S(1)}, u32[]{:S(2)}, u32[]{:S(2)}) collective-permute-start(bf16[256,256]{1,0:T(8,128)(2,1)S(1)} %get-tuple-element.61), channel_id=1, source_target_pairs={{0,8},{8,16},{16,24},{24,0},{1,9},{9,17},{17,25},{25,1},{2,10},{10... | collective-permute-start | bytes 393224 | tf_op jit(solution)/shard_map/ppermute | solution.py:23
  10.4 5.2 %collective-permute-start.7 = (bf16[256,256]{1,0:T(8,128)(2,1)S(1)}, bf16[256,256]{1,0:T(8,128)(2,1)S(1)}, u32[]{:S(2)}, u32[]{:S(2)}) collective-permute-start(bf16[256,256]{1,0:T(8,128)(2,1)S(1)} %get-tuple-element.60), channel_id=1, source_target_pairs={{0,8},{8,16},{16,24},{24,0},{1,9},{9,17},{17,25},{25,1},{2,10},{10... | collective-permute-start | bytes 393224 | tf_op jit(solution)/shard_map/ppermute | solution.py:23
  11.4 5.6 %collective-permute-start.6 = (bf16[256,256]{1,0:T(8,128)(2,1)S(1)}, bf16[256,256]{1,0:T(8,128)(2,1)S(1)}, u32[]{:S(2)}, u32[]{:S(2)}) collective-permute-start(bf16[256,256]{1,0:T(8,128)(2,1)S(1)} %get-tuple-element.59), channel_id=1, source_target_pairs={{0,8},{8,16},{16,24},{24,0},{1,9},{9,17},{17,25},{25,1},{2,10},{10... | collective-permute-start | bytes 393224 | tf_op jit(solution)/shard_map/ppermute | solution.py:23
  12.6 5.9 %collective-permute-start.5 = (bf16[256,256]{1,0:T(8,128)(2,1)S(1)}, bf16[256,256]{1,0:T(8,128)(2,1)S(1)}, u32[]{:S(2)}, u32[]{:S(2)}) collective-permute-start(bf16[256,256]{1,0:T(8,128)(2,1)S(1)} %get-tuple-element.58), channel_id=1, source_target_pairs={{0,8},{8,16},{16,24},{24,0},{1,9},{9,17},{17,25},{25,1},{2,10},{10... | collective-permute-start | bytes 393224 | tf_op jit(solution)/shard_map/ppermute | solution.py:23
  14.8 5.1 %collective-permute-start.12 = (bf16[256,256]{1,0:T(8,128)(2,1)S(1)}, bf16[256,256]{1,0:T(8,128)(2,1)S(1)}, u32[]{:S(2)}, u32[]{:S(2)}) collective-permute-start(bf16[256,256]{1,0:T(8,128)(2,1)S(1)} %get-tuple-element.69), channel_id=1, source_target_pairs={{0,8},{8,16},{16,24},{24,0},{1,9},{9,17},{17,25},{25,1},{2,10},{10... | collective-permute-start | bytes 393224 | tf_op jit(solution)/shard_map/ppermute | solution.py:23
  16.2 5.8 %collective-permute-start.11 = (bf16[256,256]{1,0:T(8,128)(2,1)S(1)}, bf16[256,256]{1,0:T(8,128)(2,1)S(1)}, u32[]{:S(2)}, u32[]{:S(2)}) collective-permute-start(bf16[256,256]{1,0:T(8,128)(2,1)S(1)} %get-tuple-element.68), channel_id=1, source_target_pairs={{0,8},{8,16},{16,24},{24,0},{1,9},{9,17},{17,25},{25,1},{2,10},{10... | collective-permute-start | bytes 393224 | tf_op jit(solution)/shard_map/ppermute | solution.py:23
  17.6 6.5 %collective-permute-start.10 = (bf16[256,256]{1,0:T(8,128)(2,1)S(1)}, bf16[256,256]{1,0:T(8,128)(2,1)S(1)}, u32[]{:S(2)}, u32[]{:S(2)}) collective-permute-start(bf16[256,256]{1,0:T(8,128)(2,1)S(1)} %get-tuple-element.67), channel_id=1, source_target_pairs={{0,8},{8,16},{16,24},{24,0},{1,9},{9,17},{17,25},{25,1},{2,10},{10... | collective-permute-start | bytes 393224 | tf_op jit(solution)/shard_map/ppermute | solution.py:23
  19.0 7.2 %collective-permute-start.9 = (bf16[256,256]{1,0:T(8,128)(2,1)S(1)}, bf16[256,256]{1,0:T(8,128)(2,1)S(1)}, u32[]{:S(2)}, u32[]{:S(2)}) collective-permute-start(bf16[256,256]{1,0:T(8,128)(2,1)S(1)} %get-tuple-element.66), channel_id=1, source_target_pairs={{0,8},{8,16},{16,24},{24,0},{1,9},{9,17},{17,25},{25,1},{2,10},{10... | collective-permute-start | bytes 393224 | tf_op jit(solution)/shard_map/ppermute | solution.py:23
  20.4 9.1 %collective-permute-start.16 = (bf16[256,256]{1,0:T(8,128)(2,1)S(1)}, bf16[256,256]{1,0:T(8,128)(2,1)S(1)}, u32[]{:S(2)}, u32[]{:S(2)}) collective-permute-start(bf16[256,256]{1,0:T(8,128)(2,1)S(1)} %get-tuple-element.77), channel_id=1, source_target_pairs={{0,1},{1,2},{2,3},{3,4},{4,5},{5,6},{6,7},{7,0},{8,9},{9,10},{10,1... | collective-permute-start | bytes 393224 | tf_op jit(solution)/shard_map/ppermute | solution.py:23
  22.5 9.8 %collective-permute-start.15 = (bf16[256,256]{1,0:T(8,128)(2,1)S(1)}, bf16[256,256]{1,0:T(8,128)(2,1)S(1)}, u32[]{:S(2)}, u32[]{:S(2)}) collective-permute-start(bf16[256,256]{1,0:T(8,128)(2,1)S(1)} %get-tuple-element.76), channel_id=1, source_target_pairs={{0,1},{1,2},{2,3},{3,4},{4,5},{5,6},{6,7},{7,0},{8,9},{9,10},{10,1... | collective-permute-start | bytes 393224 | tf_op jit(solution)/shard_map/ppermute | solution.py:23
  24.7 10.5 %collective-permute-start.14 = (bf16[256,256]{1,0:T(8,128)(2,1)S(1)}, bf16[256,256]{1,0:T(8,128)(2,1)S(1)}, u32[]{:S(2)}, u32[]{:S(2)}) collective-permute-start(bf16[256,256]{1,0:T(8,128)(2,1)S(1)} %get-tuple-element.75), channel_id=1, source_target_pairs={{0,1},{1,2},{2,3},{3,4},{4,5},{5,6},{6,7},{7,0},{8,9},{9,10},{10,1... | collective-permute-start | bytes 393224 | tf_op jit(solution)/shard_map/ppermute | solution.py:23
  26.8 10.2 %collective-permute-start.13 = (bf16[256,256]{1,0:T(8,128)(2,1)S(1)}, bf16[256,256]{1,0:T(8,128)(2,1)S(1)}, u32[]{:S(2)}, u32[]{:S(2)}) collective-permute-start(bf16[256,256]{1,0:T(8,128)(2,1)S(1)} %get-tuple-element.73), channel_id=1, source_target_pairs={{0,1},{1,2},{2,3},{3,4},{4,5},{5,6},{6,7},{7,0},{8,9},{9,10},{10,1... | collective-permute-start | bytes 393224 | tf_op jit(solution)/shard_map/ppermute | solution.py:23

commit v5 on v4

--- a/solution.py
+++ b/solution.py
@@ -131,46 +131,32 @@
     arrived = shifted(new, "blk")
     observed0, bits, pixels, frames = observed[:, :width], mask_bits, pixel_factors, frame_factors
 
-    def third_kernel(observed0, bits, pixels, frames, done, new, done_out):
-        new[...], grad = tile(
-            frames[...],
-            pixels[early : early + size],
-            observed0[:, early : early + size],
-            flags(bits, early, size),
-        )
-        start = added(frames[...], None, jnp.zeros_like(grad))
-        done_out[...] = jnp.where(is_odd(), done[...], start) + step_frames * grad
-
-    new, done = call(
-        "third",
-        third_kernel,
+    def middle_kernel(observed0, bits, pixels, frames, done, new0, new1, new, done_out):
+        end = early + size
+
+        @pl.when(is_odd())
+        def _():
+            new[...], grad = tile(
+                frames[...], pixels[early:end], observed0[:, early:end], flags(bits, early, size)
+            )
+            done_out[...] = added(frames[...], done[...], grad)
+
+        @pl.when(jnp.logical_not(is_odd()))
+        def _():
+            made, grad = tile(frames[...], pixels[:end], observed0[:, :end], flags(bits, 0, end))
+            new0[...] = made[:size]
+            new1[...] = made[size:early]
+            new[...] = made[early:]
+            done_out[...] = added(frames[...], None, grad)
+
+    new0, new1, new, done = call(
+        "middle",
+        middle_kernel,
         [observed0, bits, pixels, frames, done],
-        [chunk_t, frames_t],
-        aliases={4: 1},
+        [chunk_t, chunk_t, chunk_t, frames_t],
+        aliases={4: 3},
     )
     third = shifted(new, "blk")
-
-    def even_kernel(observed0, bits, pixels, frames, done, new0, new1, done_out):
-        @pl.when(is_odd())
-        def _():
-            done_out[...] = done[...]
-
-        @pl.when(jnp.logical_not(is_odd()))
-        def _():
-            made, grad = tile(
-                frames[...], pixels[:early], observed0[:, :early], flags(bits, 0, early)
-            )
-            new0[...] = made[:size]
-            new1[...] = made[size:]
-            done_out[...] = done[...] + step_frames * grad
-
-    new0, new1, done = call(
-        "even",
-        even_kernel,
-        [observed0, bits, pixels, frames, done],
-        [chunk_t, chunk_t, frames_t],
-        aliases={4: 2},
-    )
     coming = [(arrived, swapped(new0), 0), (arrived, swapped(new1), size), third]
 
     def step(visit, chunk, block, frames, done, wanted):
@@ -210,7 +196,51 @@
         new, done = step(0, c, pixels, frames, done, observed0)
         coming.append(shifted(new, "blk"))
 
-    for visit in range(1, visits - 1):
+    def odd_kernel(wanted, bits, frames, block, new, done):
+        @pl.when(is_odd())
+        def _():
+            new[...], grad = tile(
+                frames[...], block[...], wanted[:, width : width + size], flags(bits, width, size)
+            )
+            done[...] = added(frames[...], None, grad)
+
+    def both_kernel(wanted, bits, frames, block, own, done, new0, new, done_out):
+        @pl.when(is_odd())
+        def _():
+            at = width + size
+            new[...], grad = tile(
+                frames[...], own[...], wanted[:, at : at + size], flags(bits, at, size)
+            )
+            done_out[...] = added(frames[...], done[...], grad)
+
+        @pl.when(jnp.logical_not(is_odd()))
+        def _():
+            made, grad = tile(
+                frames[...], block[...], wanted[:, width : width + early], flags(bits, width, early)
+            )
+            new0[...] = made[:size]
+            new[...] = made[size:]
+            done_out[...] = added(frames[...], None, grad)
+
+    frames = done
+    new, done = call(
+        "odd", odd_kernel, [later, bits, frames, coming[0][1]], [chunk_t, frames_t]
+    )
+    passed = shifted(new, "blk")
+    new0, new, done = call(
+        "both",
+        both_kernel,
+        [later, bits, frames, arrived, coming[1][1], done],
+        [chunk_t, chunk_t, frames_t],
+        aliases={5: 2},
+    )
+    sent = [(passed, swapped(new0), 0), shifted(new, "blk")]
+    for c in range(2, CHUNKS):
+        new, done = step(1, c, coming[c], frames, done, later)
+        sent.append(shifted(new, "blk"))
+    coming = sent
+
+    for visit in range(2, visits - 1):
         axis = "blk" if visit < visits - 2 else "wide"
         frames, done = done, None
         sent = []

time: 38.4 us -> 37.8 us (0.984)
  Pallas kernels: 11.4 us -> 10.3 us
  waiting for transfers between devices: 11.9 us -> 12.7 us
  starting transfers between devices: 14.1 us -> 13.7 us
    pallas_call x20 -> x19, Pallas kernels: 11.4 us -> 10.3 us  [call(): pl.pallas_call(kernel, name=name, out_shape=tuple(outs), in_specs=in_spec...]
    ppermute x15, waiting for transfers between devices: 11.9 us -> 12.7 us  [shifted(): lax.ppermute(value, axis, [(s, (s + 1) % count) for s in range(count)])]
    ppermute x15, starting transfers between devices: 13.5 us -> 13 us  [shifted(): lax.ppermute(value, axis, [(s, (s + 1) % count) for s in range(count)])]
  transfers between devices with their start and end apart: 17 -> 18, of which waited for: 11 -> 12; matrix products, arithmetic and copies ran while one was open for 0% -> 0% of each run, Pallas kernels for 26% -> 24%
where the time goes in v5:
time: 37.8 us; the launch traced here: 37.6 us
  starting transfers between devices  13.7 us (36%)
  waiting for transfers between devices  12.7 us (34%)
  Pallas kernels  10.3 us (27%)
  between operations  0.86 us (2%)
    ppermute x15, starting transfers between devices, shifted(): lax.ppermute(value, axis, [(s, (s + 1) % count) for s in range(count)])  13 us
    ppermute x15, waiting for transfers between devices, shifted(): lax.ppermute(value, axis, [(s, (s + 1) % count) for s in range(count)])  12.7 us
    pallas_call x19, Pallas kernels, call(): pl.pallas_call(kernel, name=name, out_shape=tuple(outs), in_specs=in_spec...  10.3 us
  transfers between devices with their start and end apart: 18, of which 12 were waited for; matrix products, arithmetic and copies ran while one was open for 0% of the time, Pallas kernels for 24%

profile of v5, /device:TPU:0, one launch (start us, length us, event | category | flops | bytes accessed | tf_op | source)
XLA Modules:
  0.0 37.6 jit_solution(16810389081972244609)
XLA Ops:
  0.7 2.5 %collective-permute-start.2 = (bf16[512,256]{1,0:T(8,128)(2,1)S(1)}, bf16[512,256]{1,0:T(8,128)(2,1)S(1)}, u32[]{:S(2)}, u32[]{:S(2)}) collective-permute-start(bf16[512,256]{1,0:T(8,128)(2,1)S(1)} %get-tuple-element.50), channel_id=1, source_target_pairs={{0,8},{8,16},{16,24},{24,0},{1,9},{9,17},{17,25},{25,1},{2,10},{10... | collective-permute-start | bytes 786440 | tf_op jit(solution)/shard_map/ppermute | solution.py:23
  3.3 0.7 %middle.1 = (bf16[256,256]{1,0:T(8,128)(2,1)S(1)}, bf16[256,256]{1,0:T(8,128)(2,1)S(1)}, bf16[256,256]{1,0:T(8,128)(2,1)S(1)}, f32[256,256]{1,0:T(8,128)S(1)}) custom-call(bf16[256,1024]{1,0:T(8,128)(2,1)S(1)} %slice.3.observed0.wanted, s32[256,640]{1,0:T(8,128)S(1)} %copy-done.1, bf16[1024,256]{1,0:T(8,128)(2,1)S(1)} %copy-done.2, ...), custom_call_target="tpu_custom_call", output_to_operand_aliasing={{3}: (4, {})} | custom-call | tf_op jit(solution)/shard_map/middle/pallas_call | solution.py:40
  5.1 0.6 %step.14 = (bf16[256,256]{1,0:T(8,128)(2,1)S(1)}, f32[256,256]{1,0:T(8,128)S(1)}) custom-call(bf16[256,1024]{1,0:T(8,128)(2,1)S(1)} %slice.3.observed0.wanted, s32[256,640]{1,0:T(8,128)S(1)} %copy-done.1, f32[256,256]{1,0:T(8,128)S(1)} %copy-done.3, bf16[1024,256]{1,0:T(8,128)(2,1)S(1)} %copy-done.2, ...), custom_call_target="tpu_custom_call", output_to_operand_aliasing={{1}: (4, {})} | custom-call | tf_op jit(solution)/shard_map/step/pallas_call | solution.py:40
  5.6 2.0 %collective-permute-start = (bf16[256,256]{1,0:T(8,128)(2,1)S(1)}, bf16[256,256]{1,0:T(8,128)(2,1)S(1)}, u32[]{:S(2)}, u32[]{:S(2)}) collective-permute-start(bf16[256,256]{1,0:T(8,128)(2,1)S(1)} %get-tuple-element.48), channel_id=1, source_target_pairs={{0,8},{8,16},{16,24},{24,0},{1,9},{9,17},{17,25},{25,1},{2,10},{10... | collective-permute-start | bytes 393224 | tf_op jit(solution)/shard_map/ppermute | solution.py:23
  7.7 0.7 %collective-permute-start.8 = (bf16[256,256]{1,0:T(8,128)(2,1)S(1)}, bf16[256,256]{1,0:T(8,128)(2,1)S(1)}, u32[]{:S(2)}, u32[]{:S(2)}) collective-permute-start(bf16[256,256]{1,0:T(8,128)(2,1)S(1)} %get-tuple-element.60), channel_id=1, source_target_pairs={{0,8},{8,16},{16,24},{24,0},{1,9},{9,17},{17,25},{25,1},{2,10},{10... | collective-permute-start | bytes 393224 | tf_op jit(solution)/shard_map/ppermute | solution.py:23
  8.4 0.8 %collective-permute-done.2.block = bf16[512,256]{1,0:T(8,128)(2,1)S(1)} collective-permute-done((bf16[512,256]{1,0:T(8,128)(2,1)S(1)}, bf16[512,256]{1,0:T(8,128)(2,1)S(1)}, u32[]{:S(2)}, u32[]{:S(2)}) %collective-permute-start.2) | collective-permute-done | bytes 262176 | tf_op jit(solution)/shard_map/ppermute | solution.py:23
  9.2 0.6 %both.1 = (bf16[256,256]{1,0:T(8,128)(2,1)S(1)}, bf16[256,256]{1,0:T(8,128)(2,1)S(1)}, f32[256,256]{1,0:T(8,128)S(1)}) custom-call(bf16[256,5120]{1,0:T(8,128)(2,1)S(1)} %copy-done, s32[256,640]{1,0:T(8,128)S(1)} %copy-done.1, f32[256,256]{1,0:T(8,128)S(1)} %get-tuple-element.47.frames, ...), custom_call_target="tpu_custom_call", output_to_operand_aliasing={{2}: (5, {})} | custom-call | tf_op jit(solution)/shard_map/both/pallas_call | solution.py:40
  10.6 0.6 %step.15 = (bf16[256,256]{1,0:T(8,128)(2,1)S(1)}, f32[256,256]{1,0:T(8,128)S(1)}) custom-call(bf16[256,5120]{1,0:T(8,128)(2,1)S(1)} %copy-done, s32[256,640]{1,0:T(8,128)S(1)} %copy-done.1, f32[256,256]{1,0:T(8,128)S(1)} %get-tuple-element.47.frames, bf16[256,256]{1,0:T(8,128)(2,1)S(1)} %collective-permute-done.1.refs_0_, ...), custom_call_target="tpu_custom_call", output_to_operand_aliasing={{1}: (4, {})} | custom-call | tf_op jit(solution)/shard_map/step/pallas_call | solution.py:40
  11.2 0.8 %collective-permute-done.refs_0_ = bf16[256,256]{1,0:T(8,128)(2,1)S(1)} collective-permute-done((bf16[256,256]{1,0:T(8,128)(2,1)S(1)}, bf16[256,256]{1,0:T(8,128)(2,1)S(1)}, u32[]{:S(2)}, u32[]{:S(2)}) %collective-permute-start) | collective-permute-done | bytes 131104 | tf_op jit(solution)/shard_map/ppermute | solution.py:23
  12.0 0.6 %step.16 = (bf16[256,256]{1,0:T(8,128)(2,1)S(1)}, f32[256,256]{1,0:T(8,128)S(1)}) custom-call(bf16[256,5120]{1,0:T(8,128)(2,1)S(1)} %copy-done, s32[256,640]{1,0:T(8,128)S(1)} %copy-done.1, f32[256,256]{1,0:T(8,128)S(1)} %get-tuple-element.47.frames, bf16[256,256]{1,0:T(8,128)(2,1)S(1)} %collective-permute-done.refs_0_, ...), custom_call_target="tpu_custom_call", output_to_operand_aliasing={{1}: (4, {})} | custom-call | tf_op jit(solution)/shard_map/step/pallas_call | solution.py:40
  12.7 0.7 %collective-permute-done.8.refs_0_ = bf16[256,256]{1,0:T(8,128)(2,1)S(1)} collective-permute-done((bf16[256,256]{1,0:T(8,128)(2,1)S(1)}, bf16[256,256]{1,0:T(8,128)(2,1)S(1)}, u32[]{:S(2)}, u32[]{:S(2)}) %collective-permute-start.8) | collective-permute-done | bytes 131104 | tf_op jit(solution)/shard_map/ppermute | solution.py:23
  13.4 0.6 %step.17 = (bf16[256,256]{1,0:T(8,128)(2,1)S(1)}, f32[256,256]{1,0:T(8,128)S(1)}) custom-call(bf16[256,5120]{1,0:T(8,128)(2,1)S(1)} %copy-done, s32[256,640]{1,0:T(8,128)S(1)} %copy-done.1, f32[256,256]{1,0:T(8,128)S(1)} %get-tuple-element.56.frames, bf16[256,256]{1,0:T(8,128)(2,1)S(1)} %collective-permute-done.8.refs_0_, ...), custom_call_target="tpu_custom_call" | custom-call | tf_op jit(solution)/shard_map/step/pallas_call | solution.py:40
  14.1 0.7 %collective-permute-done.7.refs_0_ = bf16[256,256]{1,0:T(8,128)(2,1)S(1)} collective-permute-done((bf16[256,256]{1,0:T(8,128)(2,1)S(1)}, bf16[256,256]{1,0:T(8,128)(2,1)S(1)}, u32[]{:S(2)}, u32[]{:S(2)}) %collective-permute-start.7) | collective-permute-done | bytes 131104 | tf_op jit(solution)/shard_map/ppermute | solution.py:23
  14.8 0.6 %step.18 = (bf16[256,256]{1,0:T(8,128)(2,1)S(1)}, f32[256,256]{1,0:T(8,128)S(1)}) custom-call(bf16[256,5120]{1,0:T(8,128)(2,1)S(1)} %copy-done, s32[256,640]{1,0:T(8,128)S(1)} %copy-done.1, f32[256,256]{1,0:T(8,128)S(1)} %get-tuple-element.56.frames, bf16[256,256]{1,0:T(8,128)(2,1)S(1)} %collective-permute-done.7.refs_0_, ...), custom_call_target="tpu_custom_call", output_to_operand_aliasing={{1}: (4, {})} | custom-call | tf_op jit(solution)/shard_map/step/pallas_call | solution.py:40
  15.5 0.7 %collective-permute-done.6.refs_0_ = bf16[256,256]{1,0:T(8,128)(2,1)S(1)} collective-permute-done((bf16[256,256]{1,0:T(8,128)(2,1)S(1)}, bf16[256,256]{1,0:T(8,128)(2,1)S(1)}, u32[]{:S(2)}, u32[]{:S(2)}) %collective-permute-start.6) | collective-permute-done | bytes 131104 | tf_op jit(solution)/shard_map/ppermute | solution.py:23
  16.2 0.6 %step.19 = (bf16[256,256]{1,0:T(8,128)(2,1)S(1)}, f32[256,256]{1,0:T(8,128)S(1)}) custom-call(bf16[256,5120]{1,0:T(8,128)(2,1)S(1)} %copy-done, s32[256,640]{1,0:T(8,128)S(1)} %copy-done.1, f32[256,256]{1,0:T(8,128)S(1)} %get-tuple-element.56.frames, bf16[256,256]{1,0:T(8,128)(2,1)S(1)} %collective-permute-done.6.refs_0_, ...), custom_call_target="tpu_custom_call", output_to_operand_aliasing={{1}: (4, {})} | custom-call | tf_op jit(solution)/shard_map/step/pallas_call | solution.py:40
  16.9 0.7 %collective-permute-done.5.refs_0_ = bf16[256,256]{1,0:T(8,128)(2,1)S(1)} collective-permute-done((bf16[256,256]{1,0:T(8,128)(2,1)S(1)}, bf16[256,256]{1,0:T(8,128)(2,1)S(1)}, u32[]{:S(2)}, u32[]{:S(2)}) %collective-permute-start.5) | collective-permute-done | bytes 131104 | tf_op jit(solution)/shard_map/ppermute | solution.py:23
  17.6 0.6 %step.20 = (bf16[256,256]{1,0:T(8,128)(2,1)S(1)}, f32[256,256]{1,0:T(8,128)S(1)}) custom-call(bf16[256,5120]{1,0:T(8,128)(2,1)S(1)} %copy-done, s32[256,640]{1,0:T(8,128)S(1)} %copy-done.1, f32[256,256]{1,0:T(8,128)S(1)} %get-tuple-element.56.frames, bf16[256,256]{1,0:T(8,128)(2,1)S(1)} %collective-permute-done.5.refs_0_, ...), custom_call_target="tpu_custom_call", output_to_operand_aliasing={{1}: (4, {})} | custom-call | tf_op jit(solution)/shard_map/step/pallas_call | solution.py:40
  18.3 0.7 %collective-permute-done.13.refs_0_ = bf16[256,256]{1,0:T(8,128)(2,1)S(1)} collective-permute-done((bf16[256,256]{1,0:T(8,128)(2,1)S(1)}, bf16[256,256]{1,0:T(8,128)(2,1)S(1)}, u32[]{:S(2)}, u32[]{:S(2)}) %collective-permute-start.13) | collective-permute-done | bytes 131104 | tf_op jit(solution)/shard_map/ppermute | solution.py:23
  19.6 1.6 %collective-permute-start.17 = (bf16[256,256]{1,0:T(8,128)(2,1)S(1)}, bf16[256,256]{1,0:T(8,128)(2,1)S(1)}, u32[]{:S(2)}, u32[]{:S(2)}) collective-permute-start(bf16[256,256]{1,0:T(8,128)(2,1)S(1)} %get-tuple-element.77), channel_id=1, source_target_pairs={{0,1},{1,2},{2,3},{3,4},{4,5},{5,6},{6,7},{7,0},{8,9},{9,10},{10,1... | collective-permute-start | bytes 393224 | tf_op jit(solution)/shard_map/ppermute | solution.py:23
  21.2 0.6 %step.22 = (bf16[256,256]{1,0:T(8,128)(2,1)S(1)}, f32[256,256]{1,0:T(8,128)S(1)}) custom-call(bf16[256,5120]{1,0:T(8,128)(2,1)S(1)} %copy-done, s32[256,640]{1,0:T(8,128)S(1)} %copy-done.1, f32[256,256]{1,0:T(8,128)S(1)} %get-tuple-element.65.frames, bf16[256,256]{1,0:T(8,128)(2,1)S(1)} %collective-permute-done.12.refs_0_, ...), custom_call_target="tpu_custom_call", output_to_operand_aliasing={{1}: (4, {})} | custom-call | tf_op jit(solution)/shard_map/step/pallas_call | solution.py:40
  21.7 1.6 %collective-permute-start.16 = (bf16[256,256]{1,0:T(8,128)(2,1)S(1)}, bf16[256,256]{1,0:T(8,128)(2,1)S(1)}, u32[]{:S(2)}, u32[]{:S(2)}) collective-permute-start(bf16[256,256]{1,0:T(8,128)(2,1)S(1)} %get-tuple-element.76), channel_id=1, source_target_pairs={{0,1},{1,2},{2,3},{3,4},{4,5},{5,6},{6,7},{7,0},{8,9},{9,10},{10,1... | collective-permute-start | bytes 393224 | tf_op jit(solution)/shard_map/ppermute | solution.py:23
  23.3 0.6 %step.23 = (bf16[256,256]{1,0:T(8,128)(2,1)S(1)}, f32[256,256]{1,0:T(8,128)S(1)}) custom-call(bf16[256,5120]{1,0:T(8,128)(2,1)S(1)} %copy-done, s32[256,640]{1,0:T(8,128)S(1)} %copy-done.1, f32[256,256]{1,0:T(8,128)S(1)} %get-tuple-element.65.frames, bf16[256,256]{1,0:T(8,128)(2,1)S(1)} %collective-permute-done.11.refs_0_, ...), custom_call_target="tpu_custom_call", output_to_operand_aliasing={{1}: (4, {})} | custom-call | tf_op jit(solution)/shard_map/step/pallas_call | solution.py:40
  23.9 1.6 %collective-permute-start.15 = (bf16[256,256]{1,0:T(8,128)(2,1)S(1)}, bf16[256,256]{1,0:T(8,128)(2,1)S(1)}, u32[]{:S(2)}, u32[]{:S(2)}) collective-permute-start(bf16[256,256]{1,0:T(8,128)(2,1)S(1)} %get-tuple-element.75), channel_id=1, source_target_pairs={{0,1},{1,2},{2,3},{3,4},{4,5},{5,6},{6,7},{7,0},{8,9},{9,10},{10,1... | collective-permute-start | bytes 393224 | tf_op jit(solution)/shard_map/ppermute | solution.py:23
  25.4 0.6 %step.24 = (bf16[256,256]{1,0:T(8,128)(2,1)S(1)}, f32[256,256]{1,0:T(8,128)S(1)}) custom-call(bf16[256,5120]{1,0:T(8,128)(2,1)S(1)} %copy-done, s32[256,640]{1,0:T(8,128)S(1)} %copy-done.1, f32[256,256]{1,0:T(8,128)S(1)} %get-tuple-element.65.frames, bf16[256,256]{1,0:T(8,128)(2,1)S(1)} %collective-permute-done.10.refs_0_, ...), custom_call_target="tpu_custom_call", output_to_operand_aliasing={{1}: (4, {})} | custom-call | tf_op jit(solution)/shard_map/step/pallas_call | solution.py:40
  26.0 1.6 %collective-permute-start.14 = (bf16[256,256]{1,0:T(8,128)(2,1)S(1)}, bf16[256,256]{1,0:T(8,128)(2,1)S(1)}, u32[]{:S(2)}, u32[]{:S(2)}) collective-permute-start(bf16[256,256]{1,0:T(8,128)(2,1)S(1)} %get-tuple-element.73), channel_id=1, source_target_pairs={{0,1},{1,2},{2,3},{3,4},{4,5},{5,6},{6,7},{7,0},{8,9},{9,10},{10,1... | collective-permute-start | bytes 393224 | tf_op jit(solution)/shard_map/ppermute | solution.py:23
  27.6 1.1 %collective-permute-done.17.refs_0_ = bf16[256,256]{1,0:T(8,128)(2,1)S(1)} collective-permute-done((bf16[256,256]{1,0:T(8,128)(2,1)S(1)}, bf16[256,256]{1,0:T(8,128)(2,1)S(1)}, u32[]{:S(2)}, u32[]{:S(2)}) %collective-permute-start.17) | collective-permute-done | bytes 131104 | tf_op jit(solution)/shard_map/ppermute | solution.py:23
  29.2 2.3 %collective-permute-done.16.refs_0_ = bf16[256,256]{1,0:T(8,128)(2,1)S(1)} collective-permute-done((bf16[256,256]{1,0:T(8,128)(2,1)S(1)}, bf16[256,256]{1,0:T(8,128)(2,1)S(1)}, u32[]{:S(2)}, u32[]{:S(2)}) %collective-permute-start.16) | collective-permute-done | bytes 131104 | tf_op jit(solution)/shard_map/ppermute | solution.py:23
  31.5 0.6 %step.26 = (bf16[256,256]{1,0:T(8,128)(2,1)S(1)}, f32[256,256]{1,0:T(8,128)S(1)}) custom-call(bf16[256,5120]{1,0:T(8,128)(2,1)S(1)} %copy-done, s32[256,640]{1,0:T(8,128)S(1)} %copy-done.1, f32[256,256]{1,0:T(8,128)S(1)} %get-tuple-element.74.frames, bf16[256,256]{1,0:T(8,128)(2,1)S(1)} %collective-permute-done.16.refs_0_, ...), custom_call_target="tpu_custom_call", output_to_operand_aliasing={{1}: (4, {})} | custom-call | flops 200000000 | tf_op jit(solution)/shard_map/step/pallas_call | solution.py:40
  32.0 2.2 %collective-permute-done.15.refs_0_ = bf16[256,256]{1,0:T(8,128)(2,1)S(1)} collective-permute-done((bf16[256,256]{1,0:T(8,128)(2,1)S(1)}, bf16[256,256]{1,0:T(8,128)(2,1)S(1)}, u32[]{:S(2)}, u32[]{:S(2)}) %collective-permute-start.15) | collective-permute-done | bytes 131104 | tf_op jit(solution)/shard_map/ppermute | solution.py:23
  34.9 1.5 %collective-permute-done.14.block = bf16[256,256]{1,0:T(8,128)(2,1)S(1)} collective-permute-done((bf16[256,256]{1,0:T(8,128)(2,1)S(1)}, bf16[256,256]{1,0:T(8,128)(2,1)S(1)}, u32[]{:S(2)}, u32[]{:S(2)}) %collective-permute-start.14) | collective-permute-done | bytes 131104 | tf_op jit(solution)/shard_map/ppermute | solution.py:23
  36.3 1.3 %last.1 = (f32[256,256]{1,0:T(8,128)}, bf16[1024,256]{1,0:T(8,128)(2,1)}) custom-call(bf16[256,5120]{1,0:T(8,128)(2,1)S(1)} %copy-done, s32[256,640]{1,0:T(8,128)S(1)} %copy-done.1, bf16[256,256]{1,0:T(8,128)(2,1)S(1)} %collective-permute-done.14.block, f32[256,256]{1,0:T(8,128)S(1)} %get-tuple-element.74.frames, f32[256,256]{1,0:T(8,128)S(1)} %get-tuple-element.80.done, ...), custom_call_target="tpu_custom_call" | custom-call | flops 200000000 | tf_op jit(solution)/shard_map/last/pallas_call | solution.py:40
  (32 shorter events, 4.2 us)
Async XLA Ops:
  0.6 2.6 %copy-start.1 = (s32[256,640]{1,0:T(8,128)S(1)}, s32[256,640]{1,0:T(8,128)}, u32[]{:S(2)}) copy-start(s32[256,640]{1,0:T(8,128)} %bits.35) | copy-start | bytes 1966084
  0.6 2.6 %copy-start.2 = (bf16[1024,256]{1,0:T(8,128)(2,1)S(1)}, bf16[1024,256]{1,0:T(8,128)(2,1)}, u32[]{:S(2)}) copy-start(bf16[1024,256]{1,0:T(8,128)(2,1)} %refs_0_.1) | copy-start | bytes 1572868
  0.7 2.6 %copy-start.3 = (f32[256,256]{1,0:T(8,128)S(1)}, f32[256,256]{1,0:T(8,128)}, u32[]{:S(2)}) copy-start(f32[256,256]{1,0:T(8,128)} %frames.3) | copy-start | bytes 786436
  0.7 2.6 %copy-start = (bf16[256,5120]{1,0:T(8,128)(2,1)S(1)}, bf16[256,5120]{1,0:T(8,128)(2,1)}, u32[]{:S(2)}) copy-start(bf16[256,5120]{1,0:T(8,128)(2,1)} %wanted.15) | copy-start | bytes 7864324
  0.7 8.5 %collective-permute-start.2 = (bf16[512,256]{1,0:T(8,128)(2,1)S(1)}, bf16[512,256]{1,0:T(8,128)(2,1)S(1)}, u32[]{:S(2)}, u32[]{:S(2)}) collective-permute-start(bf16[512,256]{1,0:T(8,128)(2,1)S(1)} %get-tuple-element.50), channel_id=1, source_target_pairs={{0,8},{8,16},{16,24},{24,0},{1,9},{9,17},{17,25},{25,1},{2,10},{10... | collective-permute-start | bytes 786440 | tf_op jit(solution)/shard_map/ppermute | solution.py:23
  4.0 3.7 %collective-permute-start.4 = (bf16[256,256]{1,0:T(8,128)(2,1)S(1)}, bf16[256,256]{1,0:T(8,128)(2,1)S(1)}, u32[]{:S(2)}, u32[]{:S(2)}) collective-permute-start(bf16[256,256]{1,0:T(8,128)(2,1)S(1)} %get-tuple-element.52), channel_id=1, source_target_pairs={{0,8},{8,0},{16,24},{24,16},{1,9},{9,1},{17,25},{25,17},{2,10},{10... | collective-permute-start | bytes 393224 | tf_op jit(solution)/shard_map/ppermute | solution.py:28
  4.6 3.8 %collective-permute-start.3 = (bf16[256,256]{1,0:T(8,128)(2,1)S(1)}, bf16[256,256]{1,0:T(8,128)(2,1)S(1)}, u32[]{:S(2)}, u32[]{:S(2)}) collective-permute-start(bf16[256,256]{1,0:T(8,128)(2,1)S(1)} %get-tuple-element.51), channel_id=1, source_target_pairs={{0,8},{8,0},{16,24},{24,16},{1,9},{9,1},{17,25},{25,17},{2,10},{10... | collective-permute-start | bytes 393224 | tf_op jit(solution)/shard_map/ppermute | solution.py:28
  4.6 6.0 %collective-permute-start.1 = (bf16[256,256]{1,0:T(8,128)(2,1)S(1)}, bf16[256,256]{1,0:T(8,128)(2,1)S(1)}, u32[]{:S(2)}, u32[]{:S(2)}) collective-permute-start(bf16[256,256]{1,0:T(8,128)(2,1)S(1)} %get-tuple-element.49), channel_id=1, source_target_pairs={{0,8},{8,16},{16,24},{24,0},{1,9},{9,17},{17,25},{25,1},{2,10},{10... | collective-permute-start | bytes 393224 | tf_op jit(solution)/shard_map/ppermute | solution.py:23
  5.6 6.4 %collective-permute-start = (bf16[256,256]{1,0:T(8,128)(2,1)S(1)}, bf16[256,256]{1,0:T(8,128)(2,1)S(1)}, u32[]{:S(2)}, u32[]{:S(2)}) collective-permute-start(bf16[256,256]{1,0:T(8,128)(2,1)S(1)} %get-tuple-element.48), channel_id=1, source_target_pairs={{0,8},{8,16},{16,24},{24,0},{1,9},{9,17},{17,25},{25,1},{2,10},{10... | collective-permute-start | bytes 393224 | tf_op jit(solution)/shard_map/ppermute | solution.py:23
  7.7 5.7 %collective-permute-start.8 = (bf16[256,256]{1,0:T(8,128)(2,1)S(1)}, bf16[256,256]{1,0:T(8,128)(2,1)S(1)}, u32[]{:S(2)}, u32[]{:S(2)}) collective-permute-start(bf16[256,256]{1,0:T(8,128)(2,1)S(1)} %get-tuple-element.60), channel_id=1, source_target_pairs={{0,8},{8,16},{16,24},{24,0},{1,9},{9,17},{17,25},{25,1},{2,10},{10... | collective-permute-start | bytes 393224 | tf_op jit(solution)/shard_map/ppermute | solution.py:23
  9.8 3.6 %collective-permute-start.9 = (bf16[256,256]{1,0:T(8,128)(2,1)S(1)}, bf16[256,256]{1,0:T(8,128)(2,1)S(1)}, u32[]{:S(2)}, u32[]{:S(2)}) collective-permute-start(bf16[256,256]{1,0:T(8,128)(2,1)S(1)} %get-tuple-element.61), channel_id=1, source_target_pairs={{0,8},{8,0},{16,24},{24,16},{1,9},{9,1},{17,25},{25,17},{2,10},{10... | collective-permute-start | bytes 393224 | tf_op jit(solution)/shard_map/ppermute | solution.py:28
  9.9 5.0 %collective-permute-start.7 = (bf16[256,256]{1,0:T(8,128)(2,1)S(1)}, bf16[256,256]{1,0:T(8,128)(2,1)S(1)}, u32[]{:S(2)}, u32[]{:S(2)}) collective-permute-start(bf16[256,256]{1,0:T(8,128)(2,1)S(1)} %get-tuple-element.59), channel_id=1, source_target_pairs={{0,8},{8,16},{16,24},{24,0},{1,9},{9,17},{17,25},{25,1},{2,10},{10... | collective-permute-start | bytes 393224 | tf_op jit(solution)/shard_map/ppermute | solution.py:23
  11.2 5.1 %collective-permute-start.6 = (bf16[256,256]{1,0:T(8,128)(2,1)S(1)}, bf16[256,256]{1,0:T(8,128)(2,1)S(1)}, u32[]{:S(2)}, u32[]{:S(2)}) collective-permute-start(bf16[256,256]{1,0:T(8,128)(2,1)S(1)} %get-tuple-element.58), channel_id=1, source_target_pairs={{0,8},{8,16},{16,24},{24,0},{1,9},{9,17},{17,25},{25,1},{2,10},{10... | collective-permute-start | bytes 393224 | tf_op jit(solution)/shard_map/ppermute | solution.py:23
  12.6 5.1 %collective-permute-start.5 = (bf16[256,256]{1,0:T(8,128)(2,1)S(1)}, bf16[256,256]{1,0:T(8,128)(2,1)S(1)}, u32[]{:S(2)}, u32[]{:S(2)}) collective-permute-start(bf16[256,256]{1,0:T(8,128)(2,1)S(1)} %get-tuple-element.57), channel_id=1, source_target_pairs={{0,8},{8,16},{16,24},{24,0},{1,9},{9,17},{17,25},{25,1},{2,10},{10... | collective-permute-start | bytes 393224 | tf_op jit(solution)/shard_map/ppermute | solution.py:23
  14.0 5.1 %collective-permute-start.13 = (bf16[256,256]{1,0:T(8,128)(2,1)S(1)}, bf16[256,256]{1,0:T(8,128)(2,1)S(1)}, u32[]{:S(2)}, u32[]{:S(2)}) collective-permute-start(bf16[256,256]{1,0:T(8,128)(2,1)S(1)} %get-tuple-element.69), channel_id=1, source_target_pairs={{0,8},{8,16},{16,24},{24,0},{1,9},{9,17},{17,25},{25,1},{2,10},{10... | collective-permute-start | bytes 393224 | tf_op jit(solution)/shard_map/ppermute | solution.py:23
  15.4 5.8 %collective-permute-start.12 = (bf16[256,256]{1,0:T(8,128)(2,1)S(1)}, bf16[256,256]{1,0:T(8,128)(2,1)S(1)}, u32[]{:S(2)}, u32[]{:S(2)}) collective-permute-start(bf16[256,256]{1,0:T(8,128)(2,1)S(1)} %get-tuple-element.68), channel_id=1, source_target_pairs={{0,8},{8,16},{16,24},{24,0},{1,9},{9,17},{17,25},{25,1},{2,10},{10... | collective-permute-start | bytes 393224 | tf_op jit(solution)/shard_map/ppermute | solution.py:23
  16.8 6.5 %collective-permute-start.11 = (bf16[256,256]{1,0:T(8,128)(2,1)S(1)}, bf16[256,256]{1,0:T(8,128)(2,1)S(1)}, u32[]{:S(2)}, u32[]{:S(2)}) collective-permute-start(bf16[256,256]{1,0:T(8,128)(2,1)S(1)} %get-tuple-element.67), channel_id=1, source_target_pairs={{0,8},{8,16},{16,24},{24,0},{1,9},{9,17},{17,25},{25,1},{2,10},{10... | collective-permute-start | bytes 393224 | tf_op jit(solution)/shard_map/ppermute | solution.py:23
  18.2 7.2 %collective-permute-start.10 = (bf16[256,256]{1,0:T(8,128)(2,1)S(1)}, bf16[256,256]{1,0:T(8,128)(2,1)S(1)}, u32[]{:S(2)}, u32[]{:S(2)}) collective-permute-start(bf16[256,256]{1,0:T(8,128)(2,1)S(1)} %get-tuple-element.66), channel_id=1, source_target_pairs={{0,8},{8,16},{16,24},{24,0},{1,9},{9,17},{17,25},{25,1},{2,10},{10... | collective-permute-start | bytes 393224 | tf_op jit(solution)/shard_map/ppermute | solution.py:23
  19.6 9.1 %collective-permute-start.17 = (bf16[256,256]{1,0:T(8,128)(2,1)S(1)}, bf16[256,256]{1,0:T(8,128)(2,1)S(1)}, u32[]{:S(2)}, u32[]{:S(2)}) collective-permute-start(bf16[256,256]{1,0:T(8,128)(2,1)S(1)} %get-tuple-element.77), channel_id=1, source_target_pairs={{0,1},{1,2},{2,3},{3,4},{4,5},{5,6},{6,7},{7,0},{8,9},{9,10},{10,1... | collective-permute-start | bytes 393224 | tf_op jit(solution)/shard_map/ppermute | solution.py:23
  21.7 9.8 %collective-permute-start.16 = (bf16[256,256]{1,0:T(8,128)(2,1)S(1)}, bf16[256,256]{1,0:T(8,128)(2,1)S(1)}, u32[]{:S(2)}, u32[]{:S(2)}) collective-permute-start(bf16[256,256]{1,0:T(8,128)(2,1)S(1)} %get-tuple-element.76), channel_id=1, source_target_pairs={{0,1},{1,2},{2,3},{3,4},{4,5},{5,6},{6,7},{7,0},{8,9},{9,10},{10,1... | collective-permute-start | bytes 393224 | tf_op jit(solution)/shard_map/ppermute | solution.py:23
  23.9 10.4 %collective-permute-start.15 = (bf16[256,256]{1,0:T(8,128)(2,1)S(1)}, bf16[256,256]{1,0:T(8,128)(2,1)S(1)}, u32[]{:S(2)}, u32[]{:S(2)}) collective-permute-start(bf16[256,256]{1,0:T(8,128)(2,1)S(1)} %get-tuple-element.75), channel_id=1, source_target_pairs={{0,1},{1,2},{2,3},{3,4},{4,5},{5,6},{6,7},{7,0},{8,9},{9,10},{10,1... | collective-permute-start | bytes 393224 | tf_op jit(solution)/shard_map/ppermute | solution.py:23
  26.0 10.3 %collective-permute-start.14 = (bf16[256,256]{1,0:T(8,128)(2,1)S(1)}, bf16[256,256]{1,0:T(8,128)(2,1)S(1)}, u32[]{:S(2)}, u32[]{:S(2)}) collective-permute-start(bf16[256,256]{1,0:T(8,128)(2,1)S(1)} %get-tuple-element.73), channel_id=1, source_target_pairs={{0,1},{1,2},{2,3},{3,4},{4,5},{5,6},{6,7},{7,0},{8,9},{9,10},{10,1... | collective-permute-start | bytes 393224 | tf_op jit(solution)/shard_map/ppermute | solution.py:23

commit v6 on v5

--- a/solution.py
+++ b/solution.py
@@ -64,18 +64,27 @@
 
 def tile(frames, block, wanted, visible):
     frames_low = frames.astype(LOW)
+    scaled = clipped_errors(frames_low, block, wanted, visible)
+    return updated(frames_low, block, scaled), jnp.dot(
+        scaled, block, preferred_element_type=jnp.float32
+    )
+
+
+def clipped_errors(frames_low, block, wanted, visible):
     predicted = lax.dot_general(
         frames_low, block, (((1,), (1,)), ((), ())), preferred_element_type=jnp.float32
     )
     errors = wanted.astype(jnp.float32) - predicted
     clipped = jnp.clip(errors, -1.0, 1.0)
-    scaled = jnp.where(visible != 0, clipped, 0.0).astype(LOW)
+    return jnp.where(visible != 0, clipped, 0.0).astype(LOW)
+
+
+def updated(frames_low, block, scaled):
     grad_pixels = lax.dot_general(
         scaled, frames_low, (((0,), (0,)), ((), ())), preferred_element_type=jnp.float32
     )
     current = block.astype(jnp.float32)
-    new = (current + step_pixels * (grad_pixels - decay_weight * current)).astype(LOW)
-    return new, jnp.dot(scaled, block, preferred_element_type=jnp.float32)
+    return (current + step_pixels * (grad_pixels - decay_weight * current)).astype(LOW)
 
 
 def added(frames, done, grad):
@@ -94,7 +103,7 @@
     early = 2 * size
     early_words = min(early, mask_bits.shape[1])
 
-    def load_kernel(observed, mask_bits, frames_in, pixels_in, new, done, wanted, bits, frames, pixels, sems):
+    def load_kernel(observed, mask_bits, frames_in, pixels_in, new, scaled, wanted, bits, frames, pixels, sems):
         @pl.when(is_odd())
         def _():
             copies = [
@@ -107,17 +116,18 @@
                 copy.start()
             for copy in copies:
                 copy.wait()
-            new[...], grad = tile(frames[...], pixels[...], wanted[...], flags(bits, 0, early))
-            done[...] = added(frames[...], None, grad)
-
-    new, done = call(
+            frames_low = frames[...].astype(LOW)
+            scaled[...] = clipped_errors(frames_low, pixels[...], wanted[...], flags(bits, 0, early))
+            new[...] = updated(frames_low, pixels[...], scaled[...])
+
+    new, scaled = call(
         "load",
         load_kernel,
         [
             pltpu.with_memory_space_constraint(a, pltpu.HBM)
             for a in (observed, mask_bits, frame_factors, pixel_factors)
         ],
-        [struct((early, rank)), frames_t],
+        [struct((early, rank)), struct((rows, early))],
         in_specs=[HBM] * 4,
         scratch=[
             pltpu.VMEM((rows, early), LOW),
@@ -131,7 +141,7 @@
     arrived = shifted(new, "blk")
     observed0, bits, pixels, frames = observed[:, :width], mask_bits, pixel_factors, frame_factors
 
-    def middle_kernel(observed0, bits, pixels, frames, done, new0, new1, new, done_out):
+    def middle_kernel(observed0, bits, pixels, frames, scaled, new0, new1, new, done):
         end = early + size
 
         @pl.when(is_odd())
@@ -139,7 +149,8 @@
             new[...], grad = tile(
                 frames[...], pixels[early:end], observed0[:, early:end], flags(bits, early, size)
             )
-            done_out[...] = added(frames[...], done[...], grad)
+            early_grad = jnp.dot(scaled[...], pixels[:early], preferred_element_type=jnp.float32)
+            done[...] = added(frames[...], None, early_grad + grad)
 
         @pl.when(jnp.logical_not(is_odd()))
         def _():
@@ -147,14 +158,13 @@
             new0[...] = made[:size]
             new1[...] = made[size:early]
             new[...] = made[early:]
-            done_out[...] = added(frames[...], None, grad)
+            done[...] = added(frames[...], None, grad)
 
     new0, new1, new, done = call(
         "middle",
         middle_kernel,
-        [observed0, bits, pixels, frames, done],
+        [observed0, bits, pixels, frames, scaled],
         [chunk_t, chunk_t, chunk_t, frames_t],
-        aliases={4: 3},
     )
     third = shifted(new, "blk")
     coming = [(arrived, swapped(new0), 0), (arrived, swapped(new1), size), third]
@@ -222,6 +232,27 @@
             new[...] = made[size:]
             done_out[...] = added(frames[...], None, grad)
 
+    def start_step(visit, block, frames):
+        at = visit * width
+
+        def kernel(wanted, bits, frames, block, new, scaled):
+            frames_low = frames[...].astype(LOW)
+            scaled[...] = clipped_errors(
+                frames_low, block[...], wanted[:, at : at + size], flags(bits, at, size)
+            )
+            new[...] = updated(frames_low, block[...], scaled[...])
+
+        return call(
+            "start", kernel, [later, bits, frames, block], [chunk_t, struct((rows, size))]
+        )
+
+    def end_step(block, frames, scaled):
+        def kernel(block, frames, scaled, done):
+            grad = jnp.dot(scaled[...], block[...], preferred_element_type=jnp.float32)
+            done[...] = added(frames[...], None, grad)
+
+        return call("end", kernel, [block, frames, scaled], [frames_t])[0]
+
     frames = done
     new, done = call(
         "odd", odd_kernel, [later, bits, frames, coming[0][1]], [chunk_t, frames_t]
@@ -245,6 +276,11 @@
         frames, done = done, None
         sent = []
         for c in range(CHUNKS):
+            if c == 0 and visit == visits - 2:
+                new, scaled = start_step(visit, coming[c], frames)
+                sent.append(shifted(new, axis))
+                done = end_step(coming[c], frames, scaled)
+                continue
             new, done = step(visit, c, coming[c], frames, done, later)
             sent.append(shifted(new, axis))
         coming = sent
@@ -268,12 +304,18 @@
         for copy in copies[: CHUNKS - 1]:
             copy.start()
         columns = visit * width + at
-        new[...], grad = tile(
-            frames[...], block[...], wanted[:, columns : columns + size], flags(bits, visit * width + at, size)
+        frames_low = frames[...].astype(LOW)
+        scaled = clipped_errors(
+            frames_low,
+            block[...],
+            wanted[:, columns : columns + size],
+            flags(bits, visit * width + at, size),
         )
-        copies[-2].start()
+        grad = jnp.dot(scaled, block[...], preferred_element_type=jnp.float32)
         sum_v[...] = added(frames[...], done[...], grad)
         copies[-1].start()
+        new[...] = updated(frames_low, block[...], scaled)
+        copies[-2].start()
         for copy in copies:
             copy.wait()
 

time: 37.8 us -> 37.6 us (level)
  waiting for transfers between devices: 12.7 us -> 12.3 us
    pallas_call x19 -> x20, Pallas kernels: 10.3 us -> 10.3 us  [call(): pl.pallas_call(kernel, name=name, out_shape=tuple(outs), in_specs=in_spec...]
where the time goes in v6:
time: 37.6 us; the launch traced here: 37.4 us
  starting transfers between devices  13.8 us (37%)
  waiting for transfers between devices  12.3 us (33%)
  Pallas kernels  10.3 us (27%)
  between operations  0.87 us (2%)
    ppermute x15, starting transfers between devices, shifted(): lax.ppermute(value, axis, [(s, (s + 1) % count) for s in range(count)])  13.2 us
    ppermute x15, waiting for transfers between devices, shifted(): lax.ppermute(value, axis, [(s, (s + 1) % count) for s in range(count)])  12.3 us
    pallas_call x20, Pallas kernels, call(): pl.pallas_call(kernel, name=name, out_shape=tuple(outs), in_specs=in_spec...  10.3 us
  transfers between devices with their start and end apart: 18, of which 12 were waited for; matrix products, arithmetic and copies ran while one was open for 0% of the time, Pallas kernels for 24%

profile of v6, /device:TPU:0, one launch (start us, length us, event | category | flops | bytes accessed | tf_op | source)
XLA Modules:
  0.0 37.4 jit_solution(8583482175651843877)
XLA Ops:
  0.7 2.5 %collective-permute-start.2 = (bf16[512,256]{1,0:T(8,128)(2,1)S(1)}, bf16[512,256]{1,0:T(8,128)(2,1)S(1)}, u32[]{:S(2)}, u32[]{:S(2)}) collective-permute-start(bf16[512,256]{1,0:T(8,128)(2,1)S(1)} %get-tuple-element.50), channel_id=1, source_target_pairs={{0,8},{8,16},{16,24},{24,0},{1,9},{9,17},{17,25},{25,1},{2,10},{10... | collective-permute-start | bytes 786440 | tf_op jit(solution)/shard_map/ppermute | solution.py:23
  3.3 0.7 %middle.1 = (bf16[256,256]{1,0:T(8,128)(2,1)S(1)}, bf16[256,256]{1,0:T(8,128)(2,1)S(1)}, bf16[256,256]{1,0:T(8,128)(2,1)S(1)}, f32[256,256]{1,0:T(8,128)S(1)}) custom-call(bf16[256,1024]{1,0:T(8,128)(2,1)S(1)} %slice.3.observed0.wanted, s32[256,640]{1,0:T(8,128)S(1)} %copy-done.1, bf16[1024,256]{1,0:T(8,128)(2,1)S(1)} %copy-done.2, ...), custom_call_target="tpu_custom_call" | custom-call | tf_op jit(solution)/shard_map/middle/pallas_call | solution.py:40
  5.6 2.1 %collective-permute-start = (bf16[256,256]{1,0:T(8,128)(2,1)S(1)}, bf16[256,256]{1,0:T(8,128)(2,1)S(1)}, u32[]{:S(2)}, u32[]{:S(2)}) collective-permute-start(bf16[256,256]{1,0:T(8,128)(2,1)S(1)} %get-tuple-element.48), channel_id=1, source_target_pairs={{0,8},{8,16},{16,24},{24,0},{1,9},{9,17},{17,25},{25,1},{2,10},{10... | collective-permute-start | bytes 393224 | tf_op jit(solution)/shard_map/ppermute | solution.py:23
  7.7 0.7 %collective-permute-start.8 = (bf16[256,256]{1,0:T(8,128)(2,1)S(1)}, bf16[256,256]{1,0:T(8,128)(2,1)S(1)}, u32[]{:S(2)}, u32[]{:S(2)}) collective-permute-start(bf16[256,256]{1,0:T(8,128)(2,1)S(1)} %get-tuple-element.60), channel_id=1, source_target_pairs={{0,8},{8,16},{16,24},{24,0},{1,9},{9,17},{17,25},{25,1},{2,10},{10... | collective-permute-start | bytes 393224 | tf_op jit(solution)/shard_map/ppermute | solution.py:23
  8.4 0.8 %collective-permute-done.2.block = bf16[512,256]{1,0:T(8,128)(2,1)S(1)} collective-permute-done((bf16[512,256]{1,0:T(8,128)(2,1)S(1)}, bf16[512,256]{1,0:T(8,128)(2,1)S(1)}, u32[]{:S(2)}, u32[]{:S(2)}) %collective-permute-start.2) | collective-permute-done | bytes 262176 | tf_op jit(solution)/shard_map/ppermute | solution.py:23
  9.2 0.6 %both.1 = (bf16[256,256]{1,0:T(8,128)(2,1)S(1)}, bf16[256,256]{1,0:T(8,128)(2,1)S(1)}, f32[256,256]{1,0:T(8,128)S(1)}) custom-call(bf16[256,5120]{1,0:T(8,128)(2,1)S(1)} %copy-done, s32[256,640]{1,0:T(8,128)S(1)} %copy-done.1, f32[256,256]{1,0:T(8,128)S(1)} %get-tuple-element.47.frames, ...), custom_call_target="tpu_custom_call", output_to_operand_aliasing={{2}: (5, {})} | custom-call | tf_op jit(solution)/shard_map/both/pallas_call | solution.py:40
  10.6 0.6 %step.14 = (bf16[256,256]{1,0:T(8,128)(2,1)S(1)}, f32[256,256]{1,0:T(8,128)S(1)}) custom-call(bf16[256,5120]{1,0:T(8,128)(2,1)S(1)} %copy-done, s32[256,640]{1,0:T(8,128)S(1)} %copy-done.1, f32[256,256]{1,0:T(8,128)S(1)} %get-tuple-element.47.frames, bf16[256,256]{1,0:T(8,128)(2,1)S(1)} %collective-permute-done.1.refs_0_, ...), custom_call_target="tpu_custom_call", output_to_operand_aliasing={{1}: (4, {})} | custom-call | tf_op jit(solution)/shard_map/step/pallas_call | solution.py:40
  11.2 0.8 %collective-permute-done.refs_0_ = bf16[256,256]{1,0:T(8,128)(2,1)S(1)} collective-permute-done((bf16[256,256]{1,0:T(8,128)(2,1)S(1)}, bf16[256,256]{1,0:T(8,128)(2,1)S(1)}, u32[]{:S(2)}, u32[]{:S(2)}) %collective-permute-start) | collective-permute-done | bytes 131104 | tf_op jit(solution)/shard_map/ppermute | solution.py:23
  12.0 0.6 %step.15 = (bf16[256,256]{1,0:T(8,128)(2,1)S(1)}, f32[256,256]{1,0:T(8,128)S(1)}) custom-call(bf16[256,5120]{1,0:T(8,128)(2,1)S(1)} %copy-done, s32[256,640]{1,0:T(8,128)S(1)} %copy-done.1, f32[256,256]{1,0:T(8,128)S(1)} %get-tuple-element.47.frames, bf16[256,256]{1,0:T(8,128)(2,1)S(1)} %collective-permute-done.refs_0_, ...), custom_call_target="tpu_custom_call", output_to_operand_aliasing={{1}: (4, {})} | custom-call | tf_op jit(solution)/shard_map/step/pallas_call | solution.py:40
  12.7 0.7 %collective-permute-done.8.refs_0_ = bf16[256,256]{1,0:T(8,128)(2,1)S(1)} collective-permute-done((bf16[256,256]{1,0:T(8,128)(2,1)S(1)}, bf16[256,256]{1,0:T(8,128)(2,1)S(1)}, u32[]{:S(2)}, u32[]{:S(2)}) %collective-permute-start.8) | collective-permute-done | bytes 131104 | tf_op jit(solution)/shard_map/ppermute | solution.py:23
  13.4 0.6 %step.16 = (bf16[256,256]{1,0:T(8,128)(2,1)S(1)}, f32[256,256]{1,0:T(8,128)S(1)}) custom-call(bf16[256,5120]{1,0:T(8,128)(2,1)S(1)} %copy-done, s32[256,640]{1,0:T(8,128)S(1)} %copy-done.1, f32[256,256]{1,0:T(8,128)S(1)} %get-tuple-element.56.frames, bf16[256,256]{1,0:T(8,128)(2,1)S(1)} %collective-permute-done.8.refs_0_, ...), custom_call_target="tpu_custom_call" | custom-call | tf_op jit(solution)/shard_map/step/pallas_call | solution.py:40
  14.1 0.7 %collective-permute-done.7.refs_0_ = bf16[256,256]{1,0:T(8,128)(2,1)S(1)} collective-permute-done((bf16[256,256]{1,0:T(8,128)(2,1)S(1)}, bf16[256,256]{1,0:T(8,128)(2,1)S(1)}, u32[]{:S(2)}, u32[]{:S(2)}) %collective-permute-start.7) | collective-permute-done | bytes 131104 | tf_op jit(solution)/shard_map/ppermute | solution.py:23
  14.8 0.6 %step.17 = (bf16[256,256]{1,0:T(8,128)(2,1)S(1)}, f32[256,256]{1,0:T(8,128)S(1)}) custom-call(bf16[256,5120]{1,0:T(8,128)(2,1)S(1)} %copy-done, s32[256,640]{1,0:T(8,128)S(1)} %copy-done.1, f32[256,256]{1,0:T(8,128)S(1)} %get-tuple-element.56.frames, bf16[256,256]{1,0:T(8,128)(2,1)S(1)} %collective-permute-done.7.refs_0_, ...), custom_call_target="tpu_custom_call", output_to_operand_aliasing={{1}: (4, {})} | custom-call | tf_op jit(solution)/shard_map/step/pallas_call | solution.py:40
  15.5 0.7 %collective-permute-done.6.refs_0_ = bf16[256,256]{1,0:T(8,128)(2,1)S(1)} collective-permute-done((bf16[256,256]{1,0:T(8,128)(2,1)S(1)}, bf16[256,256]{1,0:T(8,128)(2,1)S(1)}, u32[]{:S(2)}, u32[]{:S(2)}) %collective-permute-start.6) | collective-permute-done | bytes 131104 | tf_op jit(solution)/shard_map/ppermute | solution.py:23
  16.2 0.6 %step.18 = (bf16[256,256]{1,0:T(8,128)(2,1)S(1)}, f32[256,256]{1,0:T(8,128)S(1)}) custom-call(bf16[256,5120]{1,0:T(8,128)(2,1)S(1)} %copy-done, s32[256,640]{1,0:T(8,128)S(1)} %copy-done.1, f32[256,256]{1,0:T(8,128)S(1)} %get-tuple-element.56.frames, bf16[256,256]{1,0:T(8,128)(2,1)S(1)} %collective-permute-done.6.refs_0_, ...), custom_call_target="tpu_custom_call", output_to_operand_aliasing={{1}: (4, {})} | custom-call | tf_op jit(solution)/shard_map/step/pallas_call | solution.py:40
  16.9 0.7 %collective-permute-done.5.refs_0_ = bf16[256,256]{1,0:T(8,128)(2,1)S(1)} collective-permute-done((bf16[256,256]{1,0:T(8,128)(2,1)S(1)}, bf16[256,256]{1,0:T(8,128)(2,1)S(1)}, u32[]{:S(2)}, u32[]{:S(2)}) %collective-permute-start.5) | collective-permute-done | bytes 131104 | tf_op jit(solution)/shard_map/ppermute | solution.py:23
  17.6 0.6 %step.19 = (bf16[256,256]{1,0:T(8,128)(2,1)S(1)}, f32[256,256]{1,0:T(8,128)S(1)}) custom-call(bf16[256,5120]{1,0:T(8,128)(2,1)S(1)} %copy-done, s32[256,640]{1,0:T(8,128)S(1)} %copy-done.1, f32[256,256]{1,0:T(8,128)S(1)} %get-tuple-element.56.frames, bf16[256,256]{1,0:T(8,128)(2,1)S(1)} %collective-permute-done.5.refs_0_, ...), custom_call_target="tpu_custom_call", output_to_operand_aliasing={{1}: (4, {})} | custom-call | tf_op jit(solution)/shard_map/step/pallas_call | solution.py:40
  18.3 0.7 %collective-permute-done.13.block = bf16[256,256]{1,0:T(8,128)(2,1)S(1)} collective-permute-done((bf16[256,256]{1,0:T(8,128)(2,1)S(1)}, bf16[256,256]{1,0:T(8,128)(2,1)S(1)}, u32[]{:S(2)}, u32[]{:S(2)}) %collective-permute-start.13) | collective-permute-done | bytes 131104 | tf_op jit(solution)/shard_map/ppermute | solution.py:23
  19.5 1.6 %collective-permute-start.17 = (bf16[256,256]{1,0:T(8,128)(2,1)S(1)}, bf16[256,256]{1,0:T(8,128)(2,1)S(1)}, u32[]{:S(2)}, u32[]{:S(2)}) collective-permute-start(bf16[256,256]{1,0:T(8,128)(2,1)S(1)} %get-tuple-element.77), channel_id=1, source_target_pairs={{0,1},{1,2},{2,3},{3,4},{4,5},{5,6},{6,7},{7,0},{8,9},{9,10},{10,1... | collective-permute-start | bytes 393224 | tf_op jit(solution)/shard_map/ppermute | solution.py:23
  21.3 0.6 %step.20 = (bf16[256,256]{1,0:T(8,128)(2,1)S(1)}, f32[256,256]{1,0:T(8,128)S(1)}) custom-call(bf16[256,5120]{1,0:T(8,128)(2,1)S(1)} %copy-done, s32[256,640]{1,0:T(8,128)S(1)} %copy-done.1, f32[256,256]{1,0:T(8,128)S(1)} %get-tuple-element.65.frames, bf16[256,256]{1,0:T(8,128)(2,1)S(1)} %collective-permute-done.12.refs_0_, ...), custom_call_target="tpu_custom_call", output_to_operand_aliasing={{1}: (4, {})} | custom-call | tf_op jit(solution)/shard_map/step/pallas_call | solution.py:40
  21.8 1.6 %collective-permute-start.16 = (bf16[256,256]{1,0:T(8,128)(2,1)S(1)}, bf16[256,256]{1,0:T(8,128)(2,1)S(1)}, u32[]{:S(2)}, u32[]{:S(2)}) collective-permute-start(bf16[256,256]{1,0:T(8,128)(2,1)S(1)} %get-tuple-element.76), channel_id=1, source_target_pairs={{0,1},{1,2},{2,3},{3,4},{4,5},{5,6},{6,7},{7,0},{8,9},{9,10},{10,1... | collective-permute-start | bytes 393224 | tf_op jit(solution)/shard_map/ppermute | solution.py:23
  23.4 0.6 %step.21 = (bf16[256,256]{1,0:T(8,128)(2,1)S(1)}, f32[256,256]{1,0:T(8,128)S(1)}) custom-call(bf16[256,5120]{1,0:T(8,128)(2,1)S(1)} %copy-done, s32[256,640]{1,0:T(8,128)S(1)} %copy-done.1, f32[256,256]{1,0:T(8,128)S(1)} %get-tuple-element.65.frames, bf16[256,256]{1,0:T(8,128)(2,1)S(1)} %collective-permute-done.11.refs_0_, ...), custom_call_target="tpu_custom_call", output_to_operand_aliasing={{1}: (4, {})} | custom-call | tf_op jit(solution)/shard_map/step/pallas_call | solution.py:40
  24.0 1.6 %collective-permute-start.15 = (bf16[256,256]{1,0:T(8,128)(2,1)S(1)}, bf16[256,256]{1,0:T(8,128)(2,1)S(1)}, u32[]{:S(2)}, u32[]{:S(2)}) collective-permute-start(bf16[256,256]{1,0:T(8,128)(2,1)S(1)} %get-tuple-element.75), channel_id=1, source_target_pairs={{0,1},{1,2},{2,3},{3,4},{4,5},{5,6},{6,7},{7,0},{8,9},{9,10},{10,1... | collective-permute-start | bytes 393224 | tf_op jit(solution)/shard_map/ppermute | solution.py:23
  25.5 0.6 %step.22 = (bf16[256,256]{1,0:T(8,128)(2,1)S(1)}, f32[256,256]{1,0:T(8,128)S(1)}) custom-call(bf16[256,5120]{1,0:T(8,128)(2,1)S(1)} %copy-done, s32[256,640]{1,0:T(8,128)S(1)} %copy-done.1, f32[256,256]{1,0:T(8,128)S(1)} %get-tuple-element.65.frames, bf16[256,256]{1,0:T(8,128)(2,1)S(1)} %collective-permute-done.10.refs_0_, ...), custom_call_target="tpu_custom_call", output_to_operand_aliasing={{1}: (4, {})} | custom-call | tf_op jit(solution)/shard_map/step/pallas_call | solution.py:40
  26.1 1.6 %collective-permute-start.14 = (bf16[256,256]{1,0:T(8,128)(2,1)S(1)}, bf16[256,256]{1,0:T(8,128)(2,1)S(1)}, u32[]{:S(2)}, u32[]{:S(2)}) collective-permute-start(bf16[256,256]{1,0:T(8,128)(2,1)S(1)} %get-tuple-element.73), channel_id=1, source_target_pairs={{0,1},{1,2},{2,3},{3,4},{4,5},{5,6},{6,7},{7,0},{8,9},{9,10},{10,1... | collective-permute-start | bytes 393224 | tf_op jit(solution)/shard_map/ppermute | solution.py:23
  27.7 0.9 %collective-permute-done.17.refs_0_ = bf16[256,256]{1,0:T(8,128)(2,1)S(1)} collective-permute-done((bf16[256,256]{1,0:T(8,128)(2,1)S(1)}, bf16[256,256]{1,0:T(8,128)(2,1)S(1)}, u32[]{:S(2)}, u32[]{:S(2)}) %collective-permute-start.17) | collective-permute-done | bytes 131104 | tf_op jit(solution)/shard_map/ppermute | solution.py:23
  29.1 2.3 %collective-permute-done.16.refs_0_ = bf16[256,256]{1,0:T(8,128)(2,1)S(1)} collective-permute-done((bf16[256,256]{1,0:T(8,128)(2,1)S(1)}, bf16[256,256]{1,0:T(8,128)(2,1)S(1)}, u32[]{:S(2)}, u32[]{:S(2)}) %collective-permute-start.16) | collective-permute-done | bytes 131104 | tf_op jit(solution)/shard_map/ppermute | solution.py:23
  31.4 0.6 %step.24 = (bf16[256,256]{1,0:T(8,128)(2,1)S(1)}, f32[256,256]{1,0:T(8,128)S(1)}) custom-call(bf16[256,5120]{1,0:T(8,128)(2,1)S(1)} %copy-done, s32[256,640]{1,0:T(8,128)S(1)} %copy-done.1, f32[256,256]{1,0:T(8,128)S(1)} %get-tuple-element.74.frames, bf16[256,256]{1,0:T(8,128)(2,1)S(1)} %collective-permute-done.16.refs_0_, ...), custom_call_target="tpu_custom_call", output_to_operand_aliasing={{1}: (4, {})} | custom-call | flops 200000000 | tf_op jit(solution)/shard_map/step/pallas_call | solution.py:40
  31.9 2.2 %collective-permute-done.15.refs_0_ = bf16[256,256]{1,0:T(8,128)(2,1)S(1)} collective-permute-done((bf16[256,256]{1,0:T(8,128)(2,1)S(1)}, bf16[256,256]{1,0:T(8,128)(2,1)S(1)}, u32[]{:S(2)}, u32[]{:S(2)}) %collective-permute-start.15) | collective-permute-done | bytes 131104 | tf_op jit(solution)/shard_map/ppermute | solution.py:23
  34.2 0.6 %step.25 = (bf16[256,256]{1,0:T(8,128)(2,1)S(1)}, f32[256,256]{1,0:T(8,128)S(1)}) custom-call(bf16[256,5120]{1,0:T(8,128)(2,1)S(1)} %copy-done, s32[256,640]{1,0:T(8,128)S(1)} %copy-done.1, f32[256,256]{1,0:T(8,128)S(1)} %get-tuple-element.74.frames, bf16[256,256]{1,0:T(8,128)(2,1)S(1)} %collective-permute-done.15.refs_0_, ...), custom_call_target="tpu_custom_call", output_to_operand_aliasing={{1}: (4, {})} | custom-call | flops 200000000 | tf_op jit(solution)/shard_map/step/pallas_call | solution.py:40
  34.8 1.5 %collective-permute-done.14.block = bf16[256,256]{1,0:T(8,128)(2,1)S(1)} collective-permute-done((bf16[256,256]{1,0:T(8,128)(2,1)S(1)}, bf16[256,256]{1,0:T(8,128)(2,1)S(1)}, u32[]{:S(2)}, u32[]{:S(2)}) %collective-permute-start.14) | collective-permute-done | bytes 131104 | tf_op jit(solution)/shard_map/ppermute | solution.py:23
  36.3 1.2 %last.1 = (f32[256,256]{1,0:T(8,128)}, bf16[1024,256]{1,0:T(8,128)(2,1)}) custom-call(bf16[256,5120]{1,0:T(8,128)(2,1)S(1)} %copy-done, s32[256,640]{1,0:T(8,128)S(1)} %copy-done.1, bf16[256,256]{1,0:T(8,128)(2,1)S(1)} %collective-permute-done.14.block, f32[256,256]{1,0:T(8,128)S(1)} %get-tuple-element.74.frames, f32[256,256]{1,0:T(8,128)S(1)} %get-tuple-element.80.done, ...), custom_call_target="tpu_custom_call" | custom-call | flops 200000000 | tf_op jit(solution)/shard_map/last/pallas_call | solution.py:40
  (33 shorter events, 4.4 us)
Async XLA Ops:
  0.6 2.6 %copy-start.1 = (s32[256,640]{1,0:T(8,128)S(1)}, s32[256,640]{1,0:T(8,128)}, u32[]{:S(2)}) copy-start(s32[256,640]{1,0:T(8,128)} %bits.35) | copy-start | bytes 1966084
  0.6 2.6 %copy-start.2 = (bf16[1024,256]{1,0:T(8,128)(2,1)S(1)}, bf16[1024,256]{1,0:T(8,128)(2,1)}, u32[]{:S(2)}) copy-start(bf16[1024,256]{1,0:T(8,128)(2,1)} %refs_0_.1) | copy-start | bytes 1572868
  0.7 2.6 %copy-start.3 = (f32[256,256]{1,0:T(8,128)S(1)}, f32[256,256]{1,0:T(8,128)}, u32[]{:S(2)}) copy-start(f32[256,256]{1,0:T(8,128)} %frames.3) | copy-start | bytes 786436
  0.7 2.5 %copy-start = (bf16[256,5120]{1,0:T(8,128)(2,1)S(1)}, bf16[256,5120]{1,0:T(8,128)(2,1)}, u32[]{:S(2)}) copy-start(bf16[256,5120]{1,0:T(8,128)(2,1)} %wanted.15) | copy-start | bytes 7864324
  0.7 8.4 %collective-permute-start.2 = (bf16[512,256]{1,0:T(8,128)(2,1)S(1)}, bf16[512,256]{1,0:T(8,128)(2,1)S(1)}, u32[]{:S(2)}, u32[]{:S(2)}) collective-permute-start(bf16[512,256]{1,0:T(8,128)(2,1)S(1)} %get-tuple-element.50), channel_id=1, source_target_pairs={{0,8},{8,16},{16,24},{24,0},{1,9},{9,17},{17,25},{25,1},{2,10},{10... | collective-permute-start | bytes 786440 | tf_op jit(solution)/shard_map/ppermute | solution.py:23
  4.0 3.7 %collective-permute-start.4 = (bf16[256,256]{1,0:T(8,128)(2,1)S(1)}, bf16[256,256]{1,0:T(8,128)(2,1)S(1)}, u32[]{:S(2)}, u32[]{:S(2)}) collective-permute-start(bf16[256,256]{1,0:T(8,128)(2,1)S(1)} %get-tuple-element.52), channel_id=1, source_target_pairs={{0,8},{8,0},{16,24},{24,16},{1,9},{9,1},{17,25},{25,17},{2,10},{10... | collective-permute-start | bytes 393224 | tf_op jit(solution)/shard_map/ppermute | solution.py:28
  4.5 3.8 %collective-permute-start.3 = (bf16[256,256]{1,0:T(8,128)(2,1)S(1)}, bf16[256,256]{1,0:T(8,128)(2,1)S(1)}, u32[]{:S(2)}, u32[]{:S(2)}) collective-permute-start(bf16[256,256]{1,0:T(8,128)(2,1)S(1)} %get-tuple-element.51), channel_id=1, source_target_pairs={{0,8},{8,0},{16,24},{24,16},{1,9},{9,1},{17,25},{25,17},{2,10},{10... | collective-permute-start | bytes 393224 | tf_op jit(solution)/shard_map/ppermute | solution.py:28
  4.6 6.0 %collective-permute-start.1 = (bf16[256,256]{1,0:T(8,128)(2,1)S(1)}, bf16[256,256]{1,0:T(8,128)(2,1)S(1)}, u32[]{:S(2)}, u32[]{:S(2)}) collective-permute-start(bf16[256,256]{1,0:T(8,128)(2,1)S(1)} %get-tuple-element.49), channel_id=1, source_target_pairs={{0,8},{8,16},{16,24},{24,0},{1,9},{9,17},{17,25},{25,1},{2,10},{10... | collective-permute-start | bytes 393224 | tf_op jit(solution)/shard_map/ppermute | solution.py:23
  5.6 6.4 %collective-permute-start = (bf16[256,256]{1,0:T(8,128)(2,1)S(1)}, bf16[256,256]{1,0:T(8,128)(2,1)S(1)}, u32[]{:S(2)}, u32[]{:S(2)}) collective-permute-start(bf16[256,256]{1,0:T(8,128)(2,1)S(1)} %get-tuple-element.48), channel_id=1, source_target_pairs={{0,8},{8,16},{16,24},{24,0},{1,9},{9,17},{17,25},{25,1},{2,10},{10... | collective-permute-start | bytes 393224 | tf_op jit(solution)/shard_map/ppermute | solution.py:23
  7.7 5.7 %collective-permute-start.8 = (bf16[256,256]{1,0:T(8,128)(2,1)S(1)}, bf16[256,256]{1,0:T(8,128)(2,1)S(1)}, u32[]{:S(2)}, u32[]{:S(2)}) collective-permute-start(bf16[256,256]{1,0:T(8,128)(2,1)S(1)} %get-tuple-element.60), channel_id=1, source_target_pairs={{0,8},{8,16},{16,24},{24,0},{1,9},{9,17},{17,25},{25,1},{2,10},{10... | collective-permute-start | bytes 393224 | tf_op jit(solution)/shard_map/ppermute | solution.py:23
  9.8 3.6 %collective-permute-start.9 = (bf16[256,256]{1,0:T(8,128)(2,1)S(1)}, bf16[256,256]{1,0:T(8,128)(2,1)S(1)}, u32[]{:S(2)}, u32[]{:S(2)}) collective-permute-start(bf16[256,256]{1,0:T(8,128)(2,1)S(1)} %get-tuple-element.61), channel_id=1, source_target_pairs={{0,8},{8,0},{16,24},{24,16},{1,9},{9,1},{17,25},{25,17},{2,10},{10... | collective-permute-start | bytes 393224 | tf_op jit(solution)/shard_map/ppermute | solution.py:28
  9.8 5.0 %collective-permute-start.7 = (bf16[256,256]{1,0:T(8,128)(2,1)S(1)}, bf16[256,256]{1,0:T(8,128)(2,1)S(1)}, u32[]{:S(2)}, u32[]{:S(2)}) collective-permute-start(bf16[256,256]{1,0:T(8,128)(2,1)S(1)} %get-tuple-element.59), channel_id=1, source_target_pairs={{0,8},{8,16},{16,24},{24,0},{1,9},{9,17},{17,25},{25,1},{2,10},{10... | collective-permute-start | bytes 393224 | tf_op jit(solution)/shard_map/ppermute | solution.py:23
  11.1 5.1 %collective-permute-start.6 = (bf16[256,256]{1,0:T(8,128)(2,1)S(1)}, bf16[256,256]{1,0:T(8,128)(2,1)S(1)}, u32[]{:S(2)}, u32[]{:S(2)}) collective-permute-start(bf16[256,256]{1,0:T(8,128)(2,1)S(1)} %get-tuple-element.58), channel_id=1, source_target_pairs={{0,8},{8,16},{16,24},{24,0},{1,9},{9,17},{17,25},{25,1},{2,10},{10... | collective-permute-start | bytes 393224 | tf_op jit(solution)/shard_map/ppermute | solution.py:23
  12.5 5.1 %collective-permute-start.5 = (bf16[256,256]{1,0:T(8,128)(2,1)S(1)}, bf16[256,256]{1,0:T(8,128)(2,1)S(1)}, u32[]{:S(2)}, u32[]{:S(2)}) collective-permute-start(bf16[256,256]{1,0:T(8,128)(2,1)S(1)} %get-tuple-element.57), channel_id=1, source_target_pairs={{0,8},{8,16},{16,24},{24,0},{1,9},{9,17},{17,25},{25,1},{2,10},{10... | collective-permute-start | bytes 393224 | tf_op jit(solution)/shard_map/ppermute | solution.py:23
  14.0 5.1 %collective-permute-start.13 = (bf16[256,256]{1,0:T(8,128)(2,1)S(1)}, bf16[256,256]{1,0:T(8,128)(2,1)S(1)}, u32[]{:S(2)}, u32[]{:S(2)}) collective-permute-start(bf16[256,256]{1,0:T(8,128)(2,1)S(1)} %get-tuple-element.69), channel_id=1, source_target_pairs={{0,8},{8,16},{16,24},{24,0},{1,9},{9,17},{17,25},{25,1},{2,10},{10... | collective-permute-start | bytes 393224 | tf_op jit(solution)/shard_map/ppermute | solution.py:23
  15.4 5.9 %collective-permute-start.12 = (bf16[256,256]{1,0:T(8,128)(2,1)S(1)}, bf16[256,256]{1,0:T(8,128)(2,1)S(1)}, u32[]{:S(2)}, u32[]{:S(2)}) collective-permute-start(bf16[256,256]{1,0:T(8,128)(2,1)S(1)} %get-tuple-element.68), channel_id=1, source_target_pairs={{0,8},{8,16},{16,24},{24,0},{1,9},{9,17},{17,25},{25,1},{2,10},{10... | collective-permute-start | bytes 393224 | tf_op jit(solution)/shard_map/ppermute | solution.py:23
  16.8 6.6 %collective-permute-start.11 = (bf16[256,256]{1,0:T(8,128)(2,1)S(1)}, bf16[256,256]{1,0:T(8,128)(2,1)S(1)}, u32[]{:S(2)}, u32[]{:S(2)}) collective-permute-start(bf16[256,256]{1,0:T(8,128)(2,1)S(1)} %get-tuple-element.67), channel_id=1, source_target_pairs={{0,8},{8,16},{16,24},{24,0},{1,9},{9,17},{17,25},{25,1},{2,10},{10... | collective-permute-start | bytes 393224 | tf_op jit(solution)/shard_map/ppermute | solution.py:23
  18.2 7.4 %collective-permute-start.10 = (bf16[256,256]{1,0:T(8,128)(2,1)S(1)}, bf16[256,256]{1,0:T(8,128)(2,1)S(1)}, u32[]{:S(2)}, u32[]{:S(2)}) collective-permute-start(bf16[256,256]{1,0:T(8,128)(2,1)S(1)} %get-tuple-element.66), channel_id=1, source_target_pairs={{0,8},{8,16},{16,24},{24,0},{1,9},{9,17},{17,25},{25,1},{2,10},{10... | collective-permute-start | bytes 393224 | tf_op jit(solution)/shard_map/ppermute | solution.py:23
  19.5 9.1 %collective-permute-start.17 = (bf16[256,256]{1,0:T(8,128)(2,1)S(1)}, bf16[256,256]{1,0:T(8,128)(2,1)S(1)}, u32[]{:S(2)}, u32[]{:S(2)}) collective-permute-start(bf16[256,256]{1,0:T(8,128)(2,1)S(1)} %get-tuple-element.77), channel_id=1, source_target_pairs={{0,1},{1,2},{2,3},{3,4},{4,5},{5,6},{6,7},{7,0},{8,9},{9,10},{10,1... | collective-permute-start | bytes 393224 | tf_op jit(solution)/shard_map/ppermute | solution.py:23
  21.8 9.6 %collective-permute-start.16 = (bf16[256,256]{1,0:T(8,128)(2,1)S(1)}, bf16[256,256]{1,0:T(8,128)(2,1)S(1)}, u32[]{:S(2)}, u32[]{:S(2)}) collective-permute-start(bf16[256,256]{1,0:T(8,128)(2,1)S(1)} %get-tuple-element.76), channel_id=1, source_target_pairs={{0,1},{1,2},{2,3},{3,4},{4,5},{5,6},{6,7},{7,0},{8,9},{9,10},{10,1... | collective-permute-start | bytes 393224 | tf_op jit(solution)/shard_map/ppermute | solution.py:23
  24.0 10.2 %collective-permute-start.15 = (bf16[256,256]{1,0:T(8,128)(2,1)S(1)}, bf16[256,256]{1,0:T(8,128)(2,1)S(1)}, u32[]{:S(2)}, u32[]{:S(2)}) collective-permute-start(bf16[256,256]{1,0:T(8,128)(2,1)S(1)} %get-tuple-element.75), channel_id=1, source_target_pairs={{0,1},{1,2},{2,3},{3,4},{4,5},{5,6},{6,7},{7,0},{8,9},{9,10},{10,1... | collective-permute-start | bytes 393224 | tf_op jit(solution)/shard_map/ppermute | solution.py:23
  26.1 10.2 %collective-permute-start.14 = (bf16[256,256]{1,0:T(8,128)(2,1)S(1)}, bf16[256,256]{1,0:T(8,128)(2,1)S(1)}, u32[]{:S(2)}, u32[]{:S(2)}) collective-permute-start(bf16[256,256]{1,0:T(8,128)(2,1)S(1)} %get-tuple-element.73), channel_id=1, source_target_pairs={{0,1},{1,2},{2,3},{3,4},{4,5},{5,6},{6,7},{7,0},{8,9},{9,10},{10,1... | collective-permute-start | bytes 393224 | tf_op jit(solution)/shard_map/ppermute | solution.py:23

commit v7 on v6

--- a/solution.py
+++ b/solution.py
@@ -70,10 +70,17 @@
     )
 
 
+def product(frames_low, block):
+    return lax.dot_general(
+        frames_low, block, (((1,), (1,)), ((), ())), preferred_element_type=jnp.float32
+    )
+
+
 def clipped_errors(frames_low, block, wanted, visible):
-    predicted = lax.dot_general(
-        frames_low, block, (((1,), (1,)), ((), ())), preferred_element_type=jnp.float32
-    )
+    return clipped_rest(product(frames_low, block), wanted, visible)
+
+
+def clipped_rest(predicted, wanted, visible):
     errors = wanted.astype(jnp.float32) - predicted
     clipped = jnp.clip(errors, -1.0, 1.0)
     return jnp.where(visible != 0, clipped, 0.0).astype(LOW)
@@ -103,21 +110,24 @@
     early = 2 * size
     early_words = min(early, mask_bits.shape[1])
 
-    def load_kernel(observed, mask_bits, frames_in, pixels_in, new, scaled, wanted, bits, frames, pixels, sems):
+    def load_kernel(observed, mask_bits, frames_in, pixels_in, new, scaled, wanted, bits, frames, pixels, predicted, sems):
         @pl.when(is_odd())
         def _():
             copies = [
-                pltpu.make_async_copy(mask_bits.at[:, :early_words], bits, sems.at[0]),
+                pltpu.make_async_copy(frames_in, frames, sems.at[0]),
                 pltpu.make_async_copy(pixels_in.at[:early], pixels, sems.at[1]),
-                pltpu.make_async_copy(observed.at[:, :early], wanted, sems.at[2]),
-                pltpu.make_async_copy(frames_in, frames, sems.at[3]),
+                pltpu.make_async_copy(mask_bits.at[:, :early_words], bits, sems.at[2]),
+                pltpu.make_async_copy(observed.at[:, :early], wanted, sems.at[3]),
             ]
             for copy in copies:
                 copy.start()
-            for copy in copies:
+            for copy in copies[:2]:
                 copy.wait()
             frames_low = frames[...].astype(LOW)
-            scaled[...] = clipped_errors(frames_low, pixels[...], wanted[...], flags(bits, 0, early))
+            predicted[...] = product(frames_low, pixels[...])
+            for copy in copies[2:]:
+                copy.wait()
+            scaled[...] = clipped_rest(predicted[...], wanted[...], flags(bits, 0, early))
             new[...] = updated(frames_low, pixels[...], scaled[...])
 
     new, scaled = call(
@@ -134,6 +144,7 @@
             pltpu.VMEM((rows, early_words), mask_bits.dtype),
             pltpu.VMEM((rows, rank), jnp.float32),
             pltpu.VMEM((early, rank), LOW),
+            pltpu.VMEM((rows, early), jnp.float32),
             DMA((4,)),
         ],
     )

time: 37.6 us -> 37.6 us (level)
  starting transfers between devices: 13.8 us -> 14.5 us
  waiting for transfers between devices: 12.3 us -> 11.7 us
    ppermute x15, waiting for transfers between devices: 12.3 us -> 11.7 us  [shifted(): lax.ppermute(value, axis, [(s, (s + 1) % count) for s in range(count)])]
    ppermute x15, starting transfers between devices: 13.2 us -> 13.7 us  [shifted(): lax.ppermute(value, axis, [(s, (s + 1) % count) for s in range(count)])]
where the time goes in v7:
time: 37.6 us; the launch traced here: 37.4 us
  starting transfers between devices  14.5 us (39%)
  waiting for transfers between devices  11.7 us (31%)
  Pallas kernels  10.3 us (27%)
  between operations  0.86 us (2%)
    ppermute x15, starting transfers between devices, shifted(): lax.ppermute(value, axis, [(s, (s + 1) % count) for s in range(count)])  13.7 us
    ppermute x15, waiting for transfers between devices, shifted(): lax.ppermute(value, axis, [(s, (s + 1) % count) for s in range(count)])  11.7 us
    pallas_call x20, Pallas kernels, call(): pl.pallas_call(kernel, name=name, out_shape=tuple(outs), in_specs=in_spec...  10.3 us
    ppermute x3, starting transfers between devices, swapped(): lax.ppermute(value, 'blk', [(s, s + 1 - 2 * (s % 2)) for s in range(count)])  0.78 us
  transfers between devices with their start and end apart: 18, of which 12 were waited for; matrix products, arithmetic and copies ran while one was open for 0% of the time, Pallas kernels for 24%

profile of v7, /device:TPU:0, one launch (start us, length us, event | category | flops | bytes accessed | tf_op | source)
XLA Modules:
  0.0 37.4 jit_solution(2538439894415806504)
XLA Ops:
  0.7 2.4 %collective-permute-start.2 = (bf16[512,256]{1,0:T(8,128)(2,1)S(1)}, bf16[512,256]{1,0:T(8,128)(2,1)S(1)}, u32[]{:S(2)}, u32[]{:S(2)}) collective-permute-start(bf16[512,256]{1,0:T(8,128)(2,1)S(1)} %get-tuple-element.50), channel_id=1, source_target_pairs={{0,8},{8,16},{16,24},{24,0},{1,9},{9,17},{17,25},{25,1},{2,10},{10... | collective-permute-start | bytes 786440 | tf_op jit(solution)/shard_map/ppermute | solution.py:23
  3.2 0.7 %middle.1 = (bf16[256,256]{1,0:T(8,128)(2,1)S(1)}, bf16[256,256]{1,0:T(8,128)(2,1)S(1)}, bf16[256,256]{1,0:T(8,128)(2,1)S(1)}, f32[256,256]{1,0:T(8,128)S(1)}) custom-call(bf16[256,1024]{1,0:T(8,128)(2,1)S(1)} %slice.3.observed0.wanted, s32[256,640]{1,0:T(8,128)S(1)} %copy-done.1, bf16[1024,256]{1,0:T(8,128)(2,1)S(1)} %copy-done.2, ...), custom_call_target="tpu_custom_call" | custom-call | tf_op jit(solution)/shard_map/middle/pallas_call | solution.py:40
  3.9 0.6 %collective-permute-start.4 = (bf16[256,256]{1,0:T(8,128)(2,1)S(1)}, bf16[256,256]{1,0:T(8,128)(2,1)S(1)}, u32[]{:S(2)}, u32[]{:S(2)}) collective-permute-start(bf16[256,256]{1,0:T(8,128)(2,1)S(1)} %get-tuple-element.52), channel_id=1, source_target_pairs={{0,8},{8,0},{16,24},{24,16},{1,9},{9,1},{17,25},{25,17},{2,10},{10... | collective-permute-start | bytes 393224 | tf_op jit(solution)/shard_map/ppermute | solution.py:28
  5.6 2.1 %collective-permute-start = (bf16[256,256]{1,0:T(8,128)(2,1)S(1)}, bf16[256,256]{1,0:T(8,128)(2,1)S(1)}, u32[]{:S(2)}, u32[]{:S(2)}) collective-permute-start(bf16[256,256]{1,0:T(8,128)(2,1)S(1)} %get-tuple-element.48), channel_id=1, source_target_pairs={{0,8},{8,16},{16,24},{24,0},{1,9},{9,17},{17,25},{25,1},{2,10},{10... | collective-permute-start | bytes 393224 | tf_op jit(solution)/shard_map/ppermute | solution.py:23
  7.7 0.7 %collective-permute-start.8 = (bf16[256,256]{1,0:T(8,128)(2,1)S(1)}, bf16[256,256]{1,0:T(8,128)(2,1)S(1)}, u32[]{:S(2)}, u32[]{:S(2)}) collective-permute-start(bf16[256,256]{1,0:T(8,128)(2,1)S(1)} %get-tuple-element.60), channel_id=1, source_target_pairs={{0,8},{8,16},{16,24},{24,0},{1,9},{9,17},{17,25},{25,1},{2,10},{10... | collective-permute-start | bytes 393224 | tf_op jit(solution)/shard_map/ppermute | solution.py:23
  8.4 0.7 %collective-permute-done.2.block = bf16[512,256]{1,0:T(8,128)(2,1)S(1)} collective-permute-done((bf16[512,256]{1,0:T(8,128)(2,1)S(1)}, bf16[512,256]{1,0:T(8,128)(2,1)S(1)}, u32[]{:S(2)}, u32[]{:S(2)}) %collective-permute-start.2) | collective-permute-done | bytes 262176 | tf_op jit(solution)/shard_map/ppermute | solution.py:23
  9.1 0.6 %both.1 = (bf16[256,256]{1,0:T(8,128)(2,1)S(1)}, bf16[256,256]{1,0:T(8,128)(2,1)S(1)}, f32[256,256]{1,0:T(8,128)S(1)}) custom-call(bf16[256,5120]{1,0:T(8,128)(2,1)S(1)} %copy-done, s32[256,640]{1,0:T(8,128)S(1)} %copy-done.1, f32[256,256]{1,0:T(8,128)S(1)} %get-tuple-element.47.frames, ...), custom_call_target="tpu_custom_call", output_to_operand_aliasing={{2}: (5, {})} | custom-call | tf_op jit(solution)/shard_map/both/pallas_call | solution.py:40
  10.5 0.6 %step.14 = (bf16[256,256]{1,0:T(8,128)(2,1)S(1)}, f32[256,256]{1,0:T(8,128)S(1)}) custom-call(bf16[256,5120]{1,0:T(8,128)(2,1)S(1)} %copy-done, s32[256,640]{1,0:T(8,128)S(1)} %copy-done.1, f32[256,256]{1,0:T(8,128)S(1)} %get-tuple-element.47.frames, bf16[256,256]{1,0:T(8,128)(2,1)S(1)} %collective-permute-done.1.refs_0_, ...), custom_call_target="tpu_custom_call", output_to_operand_aliasing={{1}: (4, {})} | custom-call | tf_op jit(solution)/shard_map/step/pallas_call | solution.py:40
  11.2 0.7 %collective-permute-done.refs_0_ = bf16[256,256]{1,0:T(8,128)(2,1)S(1)} collective-permute-done((bf16[256,256]{1,0:T(8,128)(2,1)S(1)}, bf16[256,256]{1,0:T(8,128)(2,1)S(1)}, u32[]{:S(2)}, u32[]{:S(2)}) %collective-permute-start) | collective-permute-done | bytes 131104 | tf_op jit(solution)/shard_map/ppermute | solution.py:23
  11.9 0.6 %step.15 = (bf16[256,256]{1,0:T(8,128)(2,1)S(1)}, f32[256,256]{1,0:T(8,128)S(1)}) custom-call(bf16[256,5120]{1,0:T(8,128)(2,1)S(1)} %copy-done, s32[256,640]{1,0:T(8,128)S(1)} %copy-done.1, f32[256,256]{1,0:T(8,128)S(1)} %get-tuple-element.47.frames, bf16[256,256]{1,0:T(8,128)(2,1)S(1)} %collective-permute-done.refs_0_, ...), custom_call_target="tpu_custom_call", output_to_operand_aliasing={{1}: (4, {})} | custom-call | tf_op jit(solution)/shard_map/step/pallas_call | solution.py:40
  12.7 0.6 %collective-permute-done.8.refs_0_ = bf16[256,256]{1,0:T(8,128)(2,1)S(1)} collective-permute-done((bf16[256,256]{1,0:T(8,128)(2,1)S(1)}, bf16[256,256]{1,0:T(8,128)(2,1)S(1)}, u32[]{:S(2)}, u32[]{:S(2)}) %collective-permute-start.8) | collective-permute-done | bytes 131104 | tf_op jit(solution)/shard_map/ppermute | solution.py:23
  13.3 0.6 %step.16 = (bf16[256,256]{1,0:T(8,128)(2,1)S(1)}, f32[256,256]{1,0:T(8,128)S(1)}) custom-call(bf16[256,5120]{1,0:T(8,128)(2,1)S(1)} %copy-done, s32[256,640]{1,0:T(8,128)S(1)} %copy-done.1, f32[256,256]{1,0:T(8,128)S(1)} %get-tuple-element.56.frames, bf16[256,256]{1,0:T(8,128)(2,1)S(1)} %collective-permute-done.8.refs_0_, ...), custom_call_target="tpu_custom_call" | custom-call | tf_op jit(solution)/shard_map/step/pallas_call | solution.py:40
  14.1 0.6 %collective-permute-done.7.refs_0_ = bf16[256,256]{1,0:T(8,128)(2,1)S(1)} collective-permute-done((bf16[256,256]{1,0:T(8,128)(2,1)S(1)}, bf16[256,256]{1,0:T(8,128)(2,1)S(1)}, u32[]{:S(2)}, u32[]{:S(2)}) %collective-permute-start.7) | collective-permute-done | bytes 131104 | tf_op jit(solution)/shard_map/ppermute | solution.py:23
  14.7 0.6 %step.17 = (bf16[256,256]{1,0:T(8,128)(2,1)S(1)}, f32[256,256]{1,0:T(8,128)S(1)}) custom-call(bf16[256,5120]{1,0:T(8,128)(2,1)S(1)} %copy-done, s32[256,640]{1,0:T(8,128)S(1)} %copy-done.1, f32[256,256]{1,0:T(8,128)S(1)} %get-tuple-element.56.frames, bf16[256,256]{1,0:T(8,128)(2,1)S(1)} %collective-permute-done.7.refs_0_, ...), custom_call_target="tpu_custom_call", output_to_operand_aliasing={{1}: (4, {})} | custom-call | tf_op jit(solution)/shard_map/step/pallas_call | solution.py:40
  15.5 0.6 %collective-permute-done.6.refs_0_ = bf16[256,256]{1,0:T(8,128)(2,1)S(1)} collective-permute-done((bf16[256,256]{1,0:T(8,128)(2,1)S(1)}, bf16[256,256]{1,0:T(8,128)(2,1)S(1)}, u32[]{:S(2)}, u32[]{:S(2)}) %collective-permute-start.6) | collective-permute-done | bytes 131104 | tf_op jit(solution)/shard_map/ppermute | solution.py:23
  16.1 0.6 %step.18 = (bf16[256,256]{1,0:T(8,128)(2,1)S(1)}, f32[256,256]{1,0:T(8,128)S(1)}) custom-call(bf16[256,5120]{1,0:T(8,128)(2,1)S(1)} %copy-done, s32[256,640]{1,0:T(8,128)S(1)} %copy-done.1, f32[256,256]{1,0:T(8,128)S(1)} %get-tuple-element.56.frames, bf16[256,256]{1,0:T(8,128)(2,1)S(1)} %collective-permute-done.6.refs_0_, ...), custom_call_target="tpu_custom_call", output_to_operand_aliasing={{1}: (4, {})} | custom-call | tf_op jit(solution)/shard_map/step/pallas_call | solution.py:40
  16.9 0.6 %collective-permute-done.5.refs_0_ = bf16[256,256]{1,0:T(8,128)(2,1)S(1)} collective-permute-done((bf16[256,256]{1,0:T(8,128)(2,1)S(1)}, bf16[256,256]{1,0:T(8,128)(2,1)S(1)}, u32[]{:S(2)}, u32[]{:S(2)}) %collective-permute-start.5) | collective-permute-done | bytes 131104 | tf_op jit(solution)/shard_map/ppermute | solution.py:23
  17.5 0.6 %step.19 = (bf16[256,256]{1,0:T(8,128)(2,1)S(1)}, f32[256,256]{1,0:T(8,128)S(1)}) custom-call(bf16[256,5120]{1,0:T(8,128)(2,1)S(1)} %copy-done, s32[256,640]{1,0:T(8,128)S(1)} %copy-done.1, f32[256,256]{1,0:T(8,128)S(1)} %get-tuple-element.56.frames, bf16[256,256]{1,0:T(8,128)(2,1)S(1)} %collective-permute-done.5.refs_0_, ...), custom_call_target="tpu_custom_call", output_to_operand_aliasing={{1}: (4, {})} | custom-call | tf_op jit(solution)/shard_map/step/pallas_call | solution.py:40
  18.3 0.6 %collective-permute-done.13.block = bf16[256,256]{1,0:T(8,128)(2,1)S(1)} collective-permute-done((bf16[256,256]{1,0:T(8,128)(2,1)S(1)}, bf16[256,256]{1,0:T(8,128)(2,1)S(1)}, u32[]{:S(2)}, u32[]{:S(2)}) %collective-permute-start.13) | collective-permute-done | bytes 131104 | tf_op jit(solution)/shard_map/ppermute | solution.py:23
  19.4 1.6 %collective-permute-start.17 = (bf16[256,256]{1,0:T(8,128)(2,1)S(1)}, bf16[256,256]{1,0:T(8,128)(2,1)S(1)}, u32[]{:S(2)}, u32[]{:S(2)}) collective-permute-start(bf16[256,256]{1,0:T(8,128)(2,1)S(1)} %get-tuple-element.77), channel_id=1, source_target_pairs={{0,1},{1,2},{2,3},{3,4},{4,5},{5,6},{6,7},{7,0},{8,9},{9,10},{10,1... | collective-permute-start | bytes 393224 | tf_op jit(solution)/shard_map/ppermute | solution.py:23
  21.2 0.6 %step.20 = (bf16[256,256]{1,0:T(8,128)(2,1)S(1)}, f32[256,256]{1,0:T(8,128)S(1)}) custom-call(bf16[256,5120]{1,0:T(8,128)(2,1)S(1)} %copy-done, s32[256,640]{1,0:T(8,128)S(1)} %copy-done.1, f32[256,256]{1,0:T(8,128)S(1)} %get-tuple-element.65.frames, bf16[256,256]{1,0:T(8,128)(2,1)S(1)} %collective-permute-done.12.refs_0_, ...), custom_call_target="tpu_custom_call", output_to_operand_aliasing={{1}: (4, {})} | custom-call | tf_op jit(solution)/shard_map/step/pallas_call | solution.py:40
  21.7 1.6 %collective-permute-start.16 = (bf16[256,256]{1,0:T(8,128)(2,1)S(1)}, bf16[256,256]{1,0:T(8,128)(2,1)S(1)}, u32[]{:S(2)}, u32[]{:S(2)}) collective-permute-start(bf16[256,256]{1,0:T(8,128)(2,1)S(1)} %get-tuple-element.76), channel_id=1, source_target_pairs={{0,1},{1,2},{2,3},{3,4},{4,5},{5,6},{6,7},{7,0},{8,9},{9,10},{10,1... | collective-permute-start | bytes 393224 | tf_op jit(solution)/shard_map/ppermute | solution.py:23
  23.3 0.6 %step.21 = (bf16[256,256]{1,0:T(8,128)(2,1)S(1)}, f32[256,256]{1,0:T(8,128)S(1)}) custom-call(bf16[256,5120]{1,0:T(8,128)(2,1)S(1)} %copy-done, s32[256,640]{1,0:T(8,128)S(1)} %copy-done.1, f32[256,256]{1,0:T(8,128)S(1)} %get-tuple-element.65.frames, bf16[256,256]{1,0:T(8,128)(2,1)S(1)} %collective-permute-done.11.refs_0_, ...), custom_call_target="tpu_custom_call", output_to_operand_aliasing={{1}: (4, {})} | custom-call | tf_op jit(solution)/shard_map/step/pallas_call | solution.py:40
  23.9 1.6 %collective-permute-start.15 = (bf16[256,256]{1,0:T(8,128)(2,1)S(1)}, bf16[256,256]{1,0:T(8,128)(2,1)S(1)}, u32[]{:S(2)}, u32[]{:S(2)}) collective-permute-start(bf16[256,256]{1,0:T(8,128)(2,1)S(1)} %get-tuple-element.75), channel_id=1, source_target_pairs={{0,1},{1,2},{2,3},{3,4},{4,5},{5,6},{6,7},{7,0},{8,9},{9,10},{10,1... | collective-permute-start | bytes 393224 | tf_op jit(solution)/shard_map/ppermute | solution.py:23
  25.4 0.6 %step.22 = (bf16[256,256]{1,0:T(8,128)(2,1)S(1)}, f32[256,256]{1,0:T(8,128)S(1)}) custom-call(bf16[256,5120]{1,0:T(8,128)(2,1)S(1)} %copy-done, s32[256,640]{1,0:T(8,128)S(1)} %copy-done.1, f32[256,256]{1,0:T(8,128)S(1)} %get-tuple-element.65.frames, bf16[256,256]{1,0:T(8,128)(2,1)S(1)} %collective-permute-done.10.refs_0_, ...), custom_call_target="tpu_custom_call", output_to_operand_aliasing={{1}: (4, {})} | custom-call | tf_op jit(solution)/shard_map/step/pallas_call | solution.py:40
  26.0 1.6 %collective-permute-start.14 = (bf16[256,256]{1,0:T(8,128)(2,1)S(1)}, bf16[256,256]{1,0:T(8,128)(2,1)S(1)}, u32[]{:S(2)}, u32[]{:S(2)}) collective-permute-start(bf16[256,256]{1,0:T(8,128)(2,1)S(1)} %get-tuple-element.73), channel_id=1, source_target_pairs={{0,1},{1,2},{2,3},{3,4},{4,5},{5,6},{6,7},{7,0},{8,9},{9,10},{10,1... | collective-permute-start | bytes 393224 | tf_op jit(solution)/shard_map/ppermute | solution.py:23
  27.6 0.9 %collective-permute-done.17.refs_0_ = bf16[256,256]{1,0:T(8,128)(2,1)S(1)} collective-permute-done((bf16[256,256]{1,0:T(8,128)(2,1)S(1)}, bf16[256,256]{1,0:T(8,128)(2,1)S(1)}, u32[]{:S(2)}, u32[]{:S(2)}) %collective-permute-start.17) | collective-permute-done | bytes 131104 | tf_op jit(solution)/shard_map/ppermute | solution.py:23
  29.0 2.3 %collective-permute-done.16.refs_0_ = bf16[256,256]{1,0:T(8,128)(2,1)S(1)} collective-permute-done((bf16[256,256]{1,0:T(8,128)(2,1)S(1)}, bf16[256,256]{1,0:T(8,128)(2,1)S(1)}, u32[]{:S(2)}, u32[]{:S(2)}) %collective-permute-start.16) | collective-permute-done | bytes 131104 | tf_op jit(solution)/shard_map/ppermute | solution.py:23
  31.3 0.6 %step.24 = (bf16[256,256]{1,0:T(8,128)(2,1)S(1)}, f32[256,256]{1,0:T(8,128)S(1)}) custom-call(bf16[256,5120]{1,0:T(8,128)(2,1)S(1)} %copy-done, s32[256,640]{1,0:T(8,128)S(1)} %copy-done.1, f32[256,256]{1,0:T(8,128)S(1)} %get-tuple-element.74.frames, bf16[256,256]{1,0:T(8,128)(2,1)S(1)} %collective-permute-done.16.refs_0_, ...), custom_call_target="tpu_custom_call", output_to_operand_aliasing={{1}: (4, {})} | custom-call | flops 200000000 | tf_op jit(solution)/shard_map/step/pallas_call | solution.py:40
  31.8 2.2 %collective-permute-done.15.refs_0_ = bf16[256,256]{1,0:T(8,128)(2,1)S(1)} collective-permute-done((bf16[256,256]{1,0:T(8,128)(2,1)S(1)}, bf16[256,256]{1,0:T(8,128)(2,1)S(1)}, u32[]{:S(2)}, u32[]{:S(2)}) %collective-permute-start.15) | collective-permute-done | bytes 131104 | tf_op jit(solution)/shard_map/ppermute | solution.py:23
  34.6 1.6 %collective-permute-done.14.block = bf16[256,256]{1,0:T(8,128)(2,1)S(1)} collective-permute-done((bf16[256,256]{1,0:T(8,128)(2,1)S(1)}, bf16[256,256]{1,0:T(8,128)(2,1)S(1)}, u32[]{:S(2)}, u32[]{:S(2)}) %collective-permute-start.14) | collective-permute-done | bytes 131104 | tf_op jit(solution)/shard_map/ppermute | solution.py:23
  36.3 1.2 %last.1 = (f32[256,256]{1,0:T(8,128)}, bf16[1024,256]{1,0:T(8,128)(2,1)}) custom-call(bf16[256,5120]{1,0:T(8,128)(2,1)S(1)} %copy-done, s32[256,640]{1,0:T(8,128)S(1)} %copy-done.1, bf16[256,256]{1,0:T(8,128)(2,1)S(1)} %collective-permute-done.14.block, f32[256,256]{1,0:T(8,128)S(1)} %get-tuple-element.74.frames, f32[256,256]{1,0:T(8,128)S(1)} %get-tuple-element.80.done, ...), custom_call_target="tpu_custom_call" | custom-call | flops 200000000 | tf_op jit(solution)/shard_map/last/pallas_call | solution.py:40
  (33 shorter events, 5.1 us)
Async XLA Ops:
  0.6 2.5 %copy-start.1 = (s32[256,640]{1,0:T(8,128)S(1)}, s32[256,640]{1,0:T(8,128)}, u32[]{:S(2)}) copy-start(s32[256,640]{1,0:T(8,128)} %bits.35) | copy-start | bytes 1966084
  0.6 2.5 %copy-start.2 = (bf16[1024,256]{1,0:T(8,128)(2,1)S(1)}, bf16[1024,256]{1,0:T(8,128)(2,1)}, u32[]{:S(2)}) copy-start(bf16[1024,256]{1,0:T(8,128)(2,1)} %refs_0_.1) | copy-start | bytes 1572868
  0.7 2.5 %copy-start.3 = (f32[256,256]{1,0:T(8,128)S(1)}, f32[256,256]{1,0:T(8,128)}, u32[]{:S(2)}) copy-start(f32[256,256]{1,0:T(8,128)} %frames.3) | copy-start | bytes 786436
  0.7 2.4 %copy-start = (bf16[256,5120]{1,0:T(8,128)(2,1)S(1)}, bf16[256,5120]{1,0:T(8,128)(2,1)}, u32[]{:S(2)}) copy-start(bf16[256,5120]{1,0:T(8,128)(2,1)} %wanted.15) | copy-start | bytes 7864324
  0.7 8.3 %collective-permute-start.2 = (bf16[512,256]{1,0:T(8,128)(2,1)S(1)}, bf16[512,256]{1,0:T(8,128)(2,1)S(1)}, u32[]{:S(2)}, u32[]{:S(2)}) collective-permute-start(bf16[512,256]{1,0:T(8,128)(2,1)S(1)} %get-tuple-element.50), channel_id=1, source_target_pairs={{0,8},{8,16},{16,24},{24,0},{1,9},{9,17},{17,25},{25,1},{2,10},{10... | collective-permute-start | bytes 786440 | tf_op jit(solution)/shard_map/ppermute | solution.py:23
  3.9 3.8 %collective-permute-start.4 = (bf16[256,256]{1,0:T(8,128)(2,1)S(1)}, bf16[256,256]{1,0:T(8,128)(2,1)S(1)}, u32[]{:S(2)}, u32[]{:S(2)}) collective-permute-start(bf16[256,256]{1,0:T(8,128)(2,1)S(1)} %get-tuple-element.52), channel_id=1, source_target_pairs={{0,8},{8,0},{16,24},{24,16},{1,9},{9,1},{17,25},{25,17},{2,10},{10... | collective-permute-start | bytes 393224 | tf_op jit(solution)/shard_map/ppermute | solution.py:28
  4.5 3.8 %collective-permute-start.3 = (bf16[256,256]{1,0:T(8,128)(2,1)S(1)}, bf16[256,256]{1,0:T(8,128)(2,1)S(1)}, u32[]{:S(2)}, u32[]{:S(2)}) collective-permute-start(bf16[256,256]{1,0:T(8,128)(2,1)S(1)} %get-tuple-element.51), channel_id=1, source_target_pairs={{0,8},{8,0},{16,24},{24,16},{1,9},{9,1},{17,25},{25,17},{2,10},{10... | collective-permute-start | bytes 393224 | tf_op jit(solution)/shard_map/ppermute | solution.py:28
  4.6 5.9 %collective-permute-start.1 = (bf16[256,256]{1,0:T(8,128)(2,1)S(1)}, bf16[256,256]{1,0:T(8,128)(2,1)S(1)}, u32[]{:S(2)}, u32[]{:S(2)}) collective-permute-start(bf16[256,256]{1,0:T(8,128)(2,1)S(1)} %get-tuple-element.49), channel_id=1, source_target_pairs={{0,8},{8,16},{16,24},{24,0},{1,9},{9,17},{17,25},{25,1},{2,10},{10... | collective-permute-start | bytes 393224 | tf_op jit(solution)/shard_map/ppermute | solution.py:23
  5.6 6.3 %collective-permute-start = (bf16[256,256]{1,0:T(8,128)(2,1)S(1)}, bf16[256,256]{1,0:T(8,128)(2,1)S(1)}, u32[]{:S(2)}, u32[]{:S(2)}) collective-permute-start(bf16[256,256]{1,0:T(8,128)(2,1)S(1)} %get-tuple-element.48), channel_id=1, source_target_pairs={{0,8},{8,16},{16,24},{24,0},{1,9},{9,17},{17,25},{25,1},{2,10},{10... | collective-permute-start | bytes 393224 | tf_op jit(solution)/shard_map/ppermute | solution.py:23
  7.7 5.6 %collective-permute-start.8 = (bf16[256,256]{1,0:T(8,128)(2,1)S(1)}, bf16[256,256]{1,0:T(8,128)(2,1)S(1)}, u32[]{:S(2)}, u32[]{:S(2)}) collective-permute-start(bf16[256,256]{1,0:T(8,128)(2,1)S(1)} %get-tuple-element.60), channel_id=1, source_target_pairs={{0,8},{8,16},{16,24},{24,0},{1,9},{9,17},{17,25},{25,1},{2,10},{10... | collective-permute-start | bytes 393224 | tf_op jit(solution)/shard_map/ppermute | solution.py:23
  9.7 3.6 %collective-permute-start.9 = (bf16[256,256]{1,0:T(8,128)(2,1)S(1)}, bf16[256,256]{1,0:T(8,128)(2,1)S(1)}, u32[]{:S(2)}, u32[]{:S(2)}) collective-permute-start(bf16[256,256]{1,0:T(8,128)(2,1)S(1)} %get-tuple-element.61), channel_id=1, source_target_pairs={{0,8},{8,0},{16,24},{24,16},{1,9},{9,1},{17,25},{25,17},{2,10},{10... | collective-permute-start | bytes 393224 | tf_op jit(solution)/shard_map/ppermute | solution.py:28
  9.7 5.0 %collective-permute-start.7 = (bf16[256,256]{1,0:T(8,128)(2,1)S(1)}, bf16[256,256]{1,0:T(8,128)(2,1)S(1)}, u32[]{:S(2)}, u32[]{:S(2)}) collective-permute-start(bf16[256,256]{1,0:T(8,128)(2,1)S(1)} %get-tuple-element.59), channel_id=1, source_target_pairs={{0,8},{8,16},{16,24},{24,0},{1,9},{9,17},{17,25},{25,1},{2,10},{10... | collective-permute-start | bytes 393224 | tf_op jit(solution)/shard_map/ppermute | solution.py:23
  11.0 5.1 %collective-permute-start.6 = (bf16[256,256]{1,0:T(8,128)(2,1)S(1)}, bf16[256,256]{1,0:T(8,128)(2,1)S(1)}, u32[]{:S(2)}, u32[]{:S(2)}) collective-permute-start(bf16[256,256]{1,0:T(8,128)(2,1)S(1)} %get-tuple-element.58), channel_id=1, source_target_pairs={{0,8},{8,16},{16,24},{24,0},{1,9},{9,17},{17,25},{25,1},{2,10},{10... | collective-permute-start | bytes 393224 | tf_op jit(solution)/shard_map/ppermute | solution.py:23
  12.4 5.1 %collective-permute-start.5 = (bf16[256,256]{1,0:T(8,128)(2,1)S(1)}, bf16[256,256]{1,0:T(8,128)(2,1)S(1)}, u32[]{:S(2)}, u32[]{:S(2)}) collective-permute-start(bf16[256,256]{1,0:T(8,128)(2,1)S(1)} %get-tuple-element.57), channel_id=1, source_target_pairs={{0,8},{8,16},{16,24},{24,0},{1,9},{9,17},{17,25},{25,1},{2,10},{10... | collective-permute-start | bytes 393224 | tf_op jit(solution)/shard_map/ppermute | solution.py:23
  13.8 5.1 %collective-permute-start.13 = (bf16[256,256]{1,0:T(8,128)(2,1)S(1)}, bf16[256,256]{1,0:T(8,128)(2,1)S(1)}, u32[]{:S(2)}, u32[]{:S(2)}) collective-permute-start(bf16[256,256]{1,0:T(8,128)(2,1)S(1)} %get-tuple-element.69), channel_id=1, source_target_pairs={{0,8},{8,16},{16,24},{24,0},{1,9},{9,17},{17,25},{25,1},{2,10},{10... | collective-permute-start | bytes 393224 | tf_op jit(solution)/shard_map/ppermute | solution.py:23
  15.2 5.9 %collective-permute-start.12 = (bf16[256,256]{1,0:T(8,128)(2,1)S(1)}, bf16[256,256]{1,0:T(8,128)(2,1)S(1)}, u32[]{:S(2)}, u32[]{:S(2)}) collective-permute-start(bf16[256,256]{1,0:T(8,128)(2,1)S(1)} %get-tuple-element.68), channel_id=1, source_target_pairs={{0,8},{8,16},{16,24},{24,0},{1,9},{9,17},{17,25},{25,1},{2,10},{10... | collective-permute-start | bytes 393224 | tf_op jit(solution)/shard_map/ppermute | solution.py:23
  16.6 6.6 %collective-permute-start.11 = (bf16[256,256]{1,0:T(8,128)(2,1)S(1)}, bf16[256,256]{1,0:T(8,128)(2,1)S(1)}, u32[]{:S(2)}, u32[]{:S(2)}) collective-permute-start(bf16[256,256]{1,0:T(8,128)(2,1)S(1)} %get-tuple-element.67), channel_id=1, source_target_pairs={{0,8},{8,16},{16,24},{24,0},{1,9},{9,17},{17,25},{25,1},{2,10},{10... | collective-permute-start | bytes 393224 | tf_op jit(solution)/shard_map/ppermute | solution.py:23
  18.1 7.4 %collective-permute-start.10 = (bf16[256,256]{1,0:T(8,128)(2,1)S(1)}, bf16[256,256]{1,0:T(8,128)(2,1)S(1)}, u32[]{:S(2)}, u32[]{:S(2)}) collective-permute-start(bf16[256,256]{1,0:T(8,128)(2,1)S(1)} %get-tuple-element.66), channel_id=1, source_target_pairs={{0,8},{8,16},{16,24},{24,0},{1,9},{9,17},{17,25},{25,1},{2,10},{10... | collective-permute-start | bytes 393224 | tf_op jit(solution)/shard_map/ppermute | solution.py:23
  19.4 9.1 %collective-permute-start.17 = (bf16[256,256]{1,0:T(8,128)(2,1)S(1)}, bf16[256,256]{1,0:T(8,128)(2,1)S(1)}, u32[]{:S(2)}, u32[]{:S(2)}) collective-permute-start(bf16[256,256]{1,0:T(8,128)(2,1)S(1)} %get-tuple-element.77), channel_id=1, source_target_pairs={{0,1},{1,2},{2,3},{3,4},{4,5},{5,6},{6,7},{7,0},{8,9},{9,10},{10,1... | collective-permute-start | bytes 393224 | tf_op jit(solution)/shard_map/ppermute | solution.py:23
  21.7 9.5 %collective-permute-start.16 = (bf16[256,256]{1,0:T(8,128)(2,1)S(1)}, bf16[256,256]{1,0:T(8,128)(2,1)S(1)}, u32[]{:S(2)}, u32[]{:S(2)}) collective-permute-start(bf16[256,256]{1,0:T(8,128)(2,1)S(1)} %get-tuple-element.76), channel_id=1, source_target_pairs={{0,1},{1,2},{2,3},{3,4},{4,5},{5,6},{6,7},{7,0},{8,9},{9,10},{10,1... | collective-permute-start | bytes 393224 | tf_op jit(solution)/shard_map/ppermute | solution.py:23
  23.9 10.2 %collective-permute-start.15 = (bf16[256,256]{1,0:T(8,128)(2,1)S(1)}, bf16[256,256]{1,0:T(8,128)(2,1)S(1)}, u32[]{:S(2)}, u32[]{:S(2)}) collective-permute-start(bf16[256,256]{1,0:T(8,128)(2,1)S(1)} %get-tuple-element.75), channel_id=1, source_target_pairs={{0,1},{1,2},{2,3},{3,4},{4,5},{5,6},{6,7},{7,0},{8,9},{9,10},{10,1... | collective-permute-start | bytes 393224 | tf_op jit(solution)/shard_map/ppermute | solution.py:23
  26.0 10.3 %collective-permute-start.14 = (bf16[256,256]{1,0:T(8,128)(2,1)S(1)}, bf16[256,256]{1,0:T(8,128)(2,1)S(1)}, u32[]{:S(2)}, u32[]{:S(2)}) collective-permute-start(bf16[256,256]{1,0:T(8,128)(2,1)S(1)} %get-tuple-element.73), channel_id=1, source_target_pairs={{0,1},{1,2},{2,3},{3,4},{4,5},{5,6},{6,7},{7,0},{8,9},{9,10},{10,1... | collective-permute-start | bytes 393224 | tf_op jit(solution)/shard_map/ppermute | solution.py:23

commit v8 on v7

--- a/solution.py
+++ b/solution.py
@@ -120,7 +120,7 @@
                 pltpu.make_async_copy(observed.at[:, :early], wanted, sems.at[3]),
             ]
             for copy in copies:
-                copy.start()
+                copy.start(priority=1)
             for copy in copies[:2]:
                 copy.wait()
             frames_low = frames[...].astype(LOW)
@@ -298,22 +298,36 @@
 
     frames, done = done, None
     visit = visits - 1
-    made = []
+    written = None
     for c in range(CHUNKS - 1):
         new, done = step(visit, c, coming[c], frames, done, later)
-        made.append(new)
-
-    def last_kernel(wanted, bits, block, frames, done, *refs):
-        made, (frames_out, pixels_out, new, sum_v, sems) = refs[: CHUNKS - 1], refs[CHUNKS - 1 :]
+
+        def write_kernel(new, *refs, at=c * size):
+            pixels_out, sem = refs[-2:]
+            copy = pltpu.make_async_copy(new, pixels_out.at[at : at + size], sem)
+            copy.start()
+            copy.wait()
+
+        first = written is None
+        written = call(
+            "write",
+            write_kernel,
+            [new] if first else [new, written],
+            [struct((width, rank))],
+            in_specs=[VMEM] if first else [VMEM, HBM],
+            out_specs=[HBM],
+            scratch=[DMA],
+            aliases={} if first else {1: 0},
+            flops=LAST_FLOPS,
+        )[0]
+
+    def last_kernel(wanted, bits, block, frames, done, written, frames_out, pixels_out, new, sum_v, sems):
+        del written
+        at = width - size
         copies = [
-            pltpu.make_async_copy(ref, pixels_out.at[c * size : (c + 1) * size], sems.at[c])
-            for c, ref in enumerate(made)
+            pltpu.make_async_copy(new, pixels_out.at[at:], sems.at[0]),
+            pltpu.make_async_copy(sum_v, frames_out, sems.at[1]),
         ]
-        at = width - size
-        copies.append(pltpu.make_async_copy(new, pixels_out.at[at:], sems.at[CHUNKS - 1]))
-        copies.append(pltpu.make_async_copy(sum_v, frames_out, sems.at[CHUNKS]))
-        for copy in copies[: CHUNKS - 1]:
-            copy.start()
         columns = visit * width + at
         frames_low = frames[...].astype(LOW)
         scaled = clipped_errors(
@@ -324,19 +338,21 @@
         )
         grad = jnp.dot(scaled, block[...], preferred_element_type=jnp.float32)
         sum_v[...] = added(frames[...], done[...], grad)
-        copies[-1].start()
+        copies[-1].start(priority=1)
         new[...] = updated(frames_low, block[...], scaled)
-        copies[-2].start()
+        copies[0].start()
         for copy in copies:
             copy.wait()
 
     return call(
         "last",
         last_kernel,
-        [later, bits, coming[-1], frames, done, *made],
+        [later, bits, coming[-1], frames, done, written],
         [frames_t, struct((width, rank))],
+        in_specs=[VMEM] * 5 + [HBM],
         out_specs=[HBM] * 2,
-        scratch=[pltpu.VMEM((size, rank), LOW), pltpu.VMEM((rows, rank), jnp.float32), DMA((CHUNKS + 1,))],
+        aliases={5: 1},
+        scratch=[pltpu.VMEM((size, rank), LOW), pltpu.VMEM((rows, rank), jnp.float32), DMA((2,))],
         flops=LAST_FLOPS,
     )
 

time: 37.6 us -> 37.6 us (level)
  waiting for transfers between devices: 11.7 us -> 9.69 us
  Pallas kernels: 10.3 us -> 12.3 us
    ppermute x15, waiting for transfers between devices: 11.7 us -> 9.69 us  [shifted(): lax.ppermute(value, axis, [(s, (s + 1) % count) for s in range(count)])]
    pallas_call x20 -> x23, Pallas kernels: 10.3 us -> 12.3 us  [call(): pl.pallas_call(kernel, name=name, out_shape=tuple(outs), in_specs=in_spec...]
  transfers between devices with their start and end apart: 18 -> 18, of which waited for: 12 -> 12; matrix products, arithmetic and copies ran while one was open for 0% -> 0% of each run, Pallas kernels for 24% -> 30%
where the time goes in v8:
time: 37.6 us; the launch traced here: 37.4 us
  starting transfers between devices  14.5 us (39%)
  Pallas kernels  12.3 us (33%)
  waiting for transfers between devices  9.69 us (26%)
  between operations  0.89 us (2%)
    ppermute x15, starting transfers between devices, shifted(): lax.ppermute(value, axis, [(s, (s + 1) % count) for s in range(count)])  13.7 us
    pallas_call x23, Pallas kernels, call(): pl.pallas_call(kernel, name=name, out_shape=tuple(outs), in_specs=in_spec...  12.3 us
    ppermute x15, waiting for transfers between devices, shifted(): lax.ppermute(value, axis, [(s, (s + 1) % count) for s in range(count)])  9.69 us
    ppermute x3, starting transfers between devices, swapped(): lax.ppermute(value, 'blk', [(s, s + 1 - 2 * (s % 2)) for s in range(count)])  0.78 us
  transfers between devices with their start and end apart: 18, of which 12 were waited for; matrix products, arithmetic and copies ran while one was open for 0% of the time, Pallas kernels for 30%

profile of v8, /device:TPU:0, one launch (start us, length us, event | category | flops | bytes accessed | tf_op | source)
XLA Modules:
  0.0 37.4 jit_solution(15209447570859036884)
XLA Ops:
  0.7 2.4 %collective-permute-start.2 = (bf16[512,256]{1,0:T(8,128)(2,1)S(1)}, bf16[512,256]{1,0:T(8,128)(2,1)S(1)}, u32[]{:S(2)}, u32[]{:S(2)}) collective-permute-start(bf16[512,256]{1,0:T(8,128)(2,1)S(1)} %get-tuple-element.50), channel_id=1, source_target_pairs={{0,8},{8,16},{16,24},{24,0},{1,9},{9,17},{17,25},{25,1},{2,10},{10... | collective-permute-start | bytes 786440 | tf_op jit(solution)/shard_map/ppermute | solution.py:23
  3.2 0.7 %middle.1 = (bf16[256,256]{1,0:T(8,128)(2,1)S(1)}, bf16[256,256]{1,0:T(8,128)(2,1)S(1)}, bf16[256,256]{1,0:T(8,128)(2,1)S(1)}, f32[256,256]{1,0:T(8,128)S(1)}) custom-call(bf16[256,1024]{1,0:T(8,128)(2,1)S(1)} %slice.3.observed0.wanted, s32[256,640]{1,0:T(8,128)S(1)} %copy-done.1, bf16[1024,256]{1,0:T(8,128)(2,1)S(1)} %copy-done.2, ...), custom_call_target="tpu_custom_call" | custom-call | tf_op jit(solution)/shard_map/middle/pallas_call | solution.py:40
  3.9 0.6 %collective-permute-start.4 = (bf16[256,256]{1,0:T(8,128)(2,1)S(1)}, bf16[256,256]{1,0:T(8,128)(2,1)S(1)}, u32[]{:S(2)}, u32[]{:S(2)}) collective-permute-start(bf16[256,256]{1,0:T(8,128)(2,1)S(1)} %get-tuple-element.52), channel_id=1, source_target_pairs={{0,8},{8,0},{16,24},{24,16},{1,9},{9,1},{17,25},{25,17},{2,10},{10... | collective-permute-start | bytes 393224 | tf_op jit(solution)/shard_map/ppermute | solution.py:28
  5.6 2.1 %collective-permute-start = (bf16[256,256]{1,0:T(8,128)(2,1)S(1)}, bf16[256,256]{1,0:T(8,128)(2,1)S(1)}, u32[]{:S(2)}, u32[]{:S(2)}) collective-permute-start(bf16[256,256]{1,0:T(8,128)(2,1)S(1)} %get-tuple-element.48), channel_id=1, source_target_pairs={{0,8},{8,16},{16,24},{24,0},{1,9},{9,17},{17,25},{25,1},{2,10},{10... | collective-permute-start | bytes 393224 | tf_op jit(solution)/shard_map/ppermute | solution.py:23
  7.7 0.7 %collective-permute-start.8 = (bf16[256,256]{1,0:T(8,128)(2,1)S(1)}, bf16[256,256]{1,0:T(8,128)(2,1)S(1)}, u32[]{:S(2)}, u32[]{:S(2)}) collective-permute-start(bf16[256,256]{1,0:T(8,128)(2,1)S(1)} %get-tuple-element.60), channel_id=1, source_target_pairs={{0,8},{8,16},{16,24},{24,0},{1,9},{9,17},{17,25},{25,1},{2,10},{10... | collective-permute-start | bytes 393224 | tf_op jit(solution)/shard_map/ppermute | solution.py:23
  8.4 0.7 %collective-permute-done.2.block = bf16[512,256]{1,0:T(8,128)(2,1)S(1)} collective-permute-done((bf16[512,256]{1,0:T(8,128)(2,1)S(1)}, bf16[512,256]{1,0:T(8,128)(2,1)S(1)}, u32[]{:S(2)}, u32[]{:S(2)}) %collective-permute-start.2) | collective-permute-done | bytes 262176 | tf_op jit(solution)/shard_map/ppermute | solution.py:23
  9.1 0.6 %both.1 = (bf16[256,256]{1,0:T(8,128)(2,1)S(1)}, bf16[256,256]{1,0:T(8,128)(2,1)S(1)}, f32[256,256]{1,0:T(8,128)S(1)}) custom-call(bf16[256,5120]{1,0:T(8,128)(2,1)S(1)} %copy-done, s32[256,640]{1,0:T(8,128)S(1)} %copy-done.1, f32[256,256]{1,0:T(8,128)S(1)} %get-tuple-element.47.frames, ...), custom_call_target="tpu_custom_call", output_to_operand_aliasing={{2}: (5, {})} | custom-call | tf_op jit(solution)/shard_map/both/pallas_call | solution.py:40
  10.5 0.6 %step.14 = (bf16[256,256]{1,0:T(8,128)(2,1)S(1)}, f32[256,256]{1,0:T(8,128)S(1)}) custom-call(bf16[256,5120]{1,0:T(8,128)(2,1)S(1)} %copy-done, s32[256,640]{1,0:T(8,128)S(1)} %copy-done.1, f32[256,256]{1,0:T(8,128)S(1)} %get-tuple-element.47.frames, bf16[256,256]{1,0:T(8,128)(2,1)S(1)} %collective-permute-done.1.refs_0_, ...), custom_call_target="tpu_custom_call", output_to_operand_aliasing={{1}: (4, {})} | custom-call | tf_op jit(solution)/shard_map/step/pallas_call | solution.py:40
  11.2 0.7 %collective-permute-done.refs_0_ = bf16[256,256]{1,0:T(8,128)(2,1)S(1)} collective-permute-done((bf16[256,256]{1,0:T(8,128)(2,1)S(1)}, bf16[256,256]{1,0:T(8,128)(2,1)S(1)}, u32[]{:S(2)}, u32[]{:S(2)}) %collective-permute-start) | collective-permute-done | bytes 131104 | tf_op jit(solution)/shard_map/ppermute | solution.py:23
  12.7 0.6 %collective-permute-done.8.refs_0_ = bf16[256,256]{1,0:T(8,128)(2,1)S(1)} collective-permute-done((bf16[256,256]{1,0:T(8,128)(2,1)S(1)}, bf16[256,256]{1,0:T(8,128)(2,1)S(1)}, u32[]{:S(2)}, u32[]{:S(2)}) %collective-permute-start.8) | collective-permute-done | bytes 131104 | tf_op jit(solution)/shard_map/ppermute | solution.py:23
  13.3 0.6 %step.16 = (bf16[256,256]{1,0:T(8,128)(2,1)S(1)}, f32[256,256]{1,0:T(8,128)S(1)}) custom-call(bf16[256,5120]{1,0:T(8,128)(2,1)S(1)} %copy-done, s32[256,640]{1,0:T(8,128)S(1)} %copy-done.1, f32[256,256]{1,0:T(8,128)S(1)} %get-tuple-element.56.frames, bf16[256,256]{1,0:T(8,128)(2,1)S(1)} %collective-permute-done.8.refs_0_, ...), custom_call_target="tpu_custom_call" | custom-call | tf_op jit(solution)/shard_map/step/pallas_call | solution.py:40
  14.1 0.6 %collective-permute-done.7.refs_0_ = bf16[256,256]{1,0:T(8,128)(2,1)S(1)} collective-permute-done((bf16[256,256]{1,0:T(8,128)(2,1)S(1)}, bf16[256,256]{1,0:T(8,128)(2,1)S(1)}, u32[]{:S(2)}, u32[]{:S(2)}) %collective-permute-start.7) | collective-permute-done | bytes 131104 | tf_op jit(solution)/shard_map/ppermute | solution.py:23
  14.7 0.6 %step.17 = (bf16[256,256]{1,0:T(8,128)(2,1)S(1)}, f32[256,256]{1,0:T(8,128)S(1)}) custom-call(bf16[256,5120]{1,0:T(8,128)(2,1)S(1)} %copy-done, s32[256,640]{1,0:T(8,128)S(1)} %copy-done.1, f32[256,256]{1,0:T(8,128)S(1)} %get-tuple-element.56.frames, bf16[256,256]{1,0:T(8,128)(2,1)S(1)} %collective-permute-done.7.refs_0_, ...), custom_call_target="tpu_custom_call", output_to_operand_aliasing={{1}: (4, {})} | custom-call | tf_op jit(solution)/shard_map/step/pallas_call | solution.py:40
  15.5 0.6 %collective-permute-done.6.refs_0_ = bf16[256,256]{1,0:T(8,128)(2,1)S(1)} collective-permute-done((bf16[256,256]{1,0:T(8,128)(2,1)S(1)}, bf16[256,256]{1,0:T(8,128)(2,1)S(1)}, u32[]{:S(2)}, u32[]{:S(2)}) %collective-permute-start.6) | collective-permute-done | bytes 131104 | tf_op jit(solution)/shard_map/ppermute | solution.py:23
  16.1 0.6 %step.18 = (bf16[256,256]{1,0:T(8,128)(2,1)S(1)}, f32[256,256]{1,0:T(8,128)S(1)}) custom-call(bf16[256,5120]{1,0:T(8,128)(2,1)S(1)} %copy-done, s32[256,640]{1,0:T(8,128)S(1)} %copy-done.1, f32[256,256]{1,0:T(8,128)S(1)} %get-tuple-element.56.frames, bf16[256,256]{1,0:T(8,128)(2,1)S(1)} %collective-permute-done.6.refs_0_, ...), custom_call_target="tpu_custom_call", output_to_operand_aliasing={{1}: (4, {})} | custom-call | tf_op jit(solution)/shard_map/step/pallas_call | solution.py:40
  16.9 0.6 %collective-permute-done.5.refs_0_ = bf16[256,256]{1,0:T(8,128)(2,1)S(1)} collective-permute-done((bf16[256,256]{1,0:T(8,128)(2,1)S(1)}, bf16[256,256]{1,0:T(8,128)(2,1)S(1)}, u32[]{:S(2)}, u32[]{:S(2)}) %collective-permute-start.5) | collective-permute-done | bytes 131104 | tf_op jit(solution)/shard_map/ppermute | solution.py:23
  18.3 0.6 %collective-permute-done.13.block = bf16[256,256]{1,0:T(8,128)(2,1)S(1)} collective-permute-done((bf16[256,256]{1,0:T(8,128)(2,1)S(1)}, bf16[256,256]{1,0:T(8,128)(2,1)S(1)}, u32[]{:S(2)}, u32[]{:S(2)}) %collective-permute-start.13) | collective-permute-done | bytes 131104 | tf_op jit(solution)/shard_map/ppermute | solution.py:23
  19.4 1.6 %collective-permute-start.17 = (bf16[256,256]{1,0:T(8,128)(2,1)S(1)}, bf16[256,256]{1,0:T(8,128)(2,1)S(1)}, u32[]{:S(2)}, u32[]{:S(2)}) collective-permute-start(bf16[256,256]{1,0:T(8,128)(2,1)S(1)} %get-tuple-element.77), channel_id=1, source_target_pairs={{0,1},{1,2},{2,3},{3,4},{4,5},{5,6},{6,7},{7,0},{8,9},{9,10},{10,1... | collective-permute-start | bytes 393224 | tf_op jit(solution)/shard_map/ppermute | solution.py:23
  21.2 0.6 %step.20 = (bf16[256,256]{1,0:T(8,128)(2,1)S(1)}, f32[256,256]{1,0:T(8,128)S(1)}) custom-call(bf16[256,5120]{1,0:T(8,128)(2,1)S(1)} %copy-done, s32[256,640]{1,0:T(8,128)S(1)} %copy-done.1, f32[256,256]{1,0:T(8,128)S(1)} %get-tuple-element.65.frames, bf16[256,256]{1,0:T(8,128)(2,1)S(1)} %collective-permute-done.12.refs_0_, ...), custom_call_target="tpu_custom_call", output_to_operand_aliasing={{1}: (4, {})} | custom-call | tf_op jit(solution)/shard_map/step/pallas_call | solution.py:40
  21.7 1.6 %collective-permute-start.16 = (bf16[256,256]{1,0:T(8,128)(2,1)S(1)}, bf16[256,256]{1,0:T(8,128)(2,1)S(1)}, u32[]{:S(2)}, u32[]{:S(2)}) collective-permute-start(bf16[256,256]{1,0:T(8,128)(2,1)S(1)} %get-tuple-element.76), channel_id=1, source_target_pairs={{0,1},{1,2},{2,3},{3,4},{4,5},{5,6},{6,7},{7,0},{8,9},{9,10},{10,1... | collective-permute-start | bytes 393224 | tf_op jit(solution)/shard_map/ppermute | solution.py:23
  23.3 0.6 %step.21 = (bf16[256,256]{1,0:T(8,128)(2,1)S(1)}, f32[256,256]{1,0:T(8,128)S(1)}) custom-call(bf16[256,5120]{1,0:T(8,128)(2,1)S(1)} %copy-done, s32[256,640]{1,0:T(8,128)S(1)} %copy-done.1, f32[256,256]{1,0:T(8,128)S(1)} %get-tuple-element.65.frames, bf16[256,256]{1,0:T(8,128)(2,1)S(1)} %collective-permute-done.11.refs_0_, ...), custom_call_target="tpu_custom_call", output_to_operand_aliasing={{1}: (4, {})} | custom-call | tf_op jit(solution)/shard_map/step/pallas_call | solution.py:40
  23.9 1.6 %collective-permute-start.15 = (bf16[256,256]{1,0:T(8,128)(2,1)S(1)}, bf16[256,256]{1,0:T(8,128)(2,1)S(1)}, u32[]{:S(2)}, u32[]{:S(2)}) collective-permute-start(bf16[256,256]{1,0:T(8,128)(2,1)S(1)} %get-tuple-element.75), channel_id=1, source_target_pairs={{0,1},{1,2},{2,3},{3,4},{4,5},{5,6},{6,7},{7,0},{8,9},{9,10},{10,1... | collective-permute-start | bytes 393224 | tf_op jit(solution)/shard_map/ppermute | solution.py:23
  26.0 1.6 %collective-permute-start.14 = (bf16[256,256]{1,0:T(8,128)(2,1)S(1)}, bf16[256,256]{1,0:T(8,128)(2,1)S(1)}, u32[]{:S(2)}, u32[]{:S(2)}) collective-permute-start(bf16[256,256]{1,0:T(8,128)(2,1)S(1)} %get-tuple-element.73), channel_id=1, source_target_pairs={{0,1},{1,2},{2,3},{3,4},{4,5},{5,6},{6,7},{7,0},{8,9},{9,10},{10,1... | collective-permute-start | bytes 393224 | tf_op jit(solution)/shard_map/ppermute | solution.py:23
  27.6 0.9 %collective-permute-done.17.refs_0_ = bf16[256,256]{1,0:T(8,128)(2,1)S(1)} collective-permute-done((bf16[256,256]{1,0:T(8,128)(2,1)S(1)}, bf16[256,256]{1,0:T(8,128)(2,1)S(1)}, u32[]{:S(2)}, u32[]{:S(2)}) %collective-permute-start.17) | collective-permute-done | bytes 131104 | tf_op jit(solution)/shard_map/ppermute | solution.py:23
  29.0 0.7 %write.3.refs_0_ = bf16[1024,256]{1,0:T(8,128)(2,1)} custom-call(bf16[256,256]{1,0:T(8,128)(2,1)S(1)} %get-tuple-element.83.new), custom_call_target="tpu_custom_call" | custom-call | flops 200000000 | tf_op jit(solution)/shard_map/write/pallas_call | solution.py:40
  29.7 1.6 %collective-permute-done.16.refs_0_ = bf16[256,256]{1,0:T(8,128)(2,1)S(1)} collective-permute-done((bf16[256,256]{1,0:T(8,128)(2,1)S(1)}, bf16[256,256]{1,0:T(8,128)(2,1)S(1)}, u32[]{:S(2)}, u32[]{:S(2)}) %collective-permute-start.16) | collective-permute-done | bytes 131104 | tf_op jit(solution)/shard_map/ppermute | solution.py:23
  31.3 0.6 %step.24 = (bf16[256,256]{1,0:T(8,128)(2,1)S(1)}, f32[256,256]{1,0:T(8,128)S(1)}) custom-call(bf16[256,5120]{1,0:T(8,128)(2,1)S(1)} %copy-done, s32[256,640]{1,0:T(8,128)S(1)} %copy-done.1, f32[256,256]{1,0:T(8,128)S(1)} %get-tuple-element.74.frames, bf16[256,256]{1,0:T(8,128)(2,1)S(1)} %collective-permute-done.16.refs_0_, ...), custom_call_target="tpu_custom_call", output_to_operand_aliasing={{1}: (4, {})} | custom-call | flops 200000000 | tf_op jit(solution)/shard_map/step/pallas_call | solution.py:40
  31.8 0.7 %write.4.refs_0_ = bf16[1024,256]{1,0:T(8,128)(2,1)} custom-call(bf16[256,256]{1,0:T(8,128)(2,1)S(1)} %get-tuple-element.82.new, bf16[1024,256]{1,0:T(8,128)(2,1)} %write.3.refs_0_), custom_call_target="tpu_custom_call", output_to_operand_aliasing={{}: (1, {})} | custom-call | flops 200000000 | tf_op jit(solution)/shard_map/write/pallas_call | solution.py:40
  32.5 1.6 %collective-permute-done.15.refs_0_ = bf16[256,256]{1,0:T(8,128)(2,1)S(1)} collective-permute-done((bf16[256,256]{1,0:T(8,128)(2,1)S(1)}, bf16[256,256]{1,0:T(8,128)(2,1)S(1)}, u32[]{:S(2)}, u32[]{:S(2)}) %collective-permute-start.15) | collective-permute-done | bytes 131104 | tf_op jit(solution)/shard_map/ppermute | solution.py:23
  34.6 0.7 %write.5.written = bf16[1024,256]{1,0:T(8,128)(2,1)} custom-call(bf16[256,256]{1,0:T(8,128)(2,1)S(1)} %get-tuple-element.81.new, bf16[1024,256]{1,0:T(8,128)(2,1)} %write.4.refs_0_), custom_call_target="tpu_custom_call", output_to_operand_aliasing={{}: (1, {})} | custom-call | flops 200000000 | tf_op jit(solution)/shard_map/write/pallas_call | solution.py:40
  35.3 1.0 %collective-permute-done.14.block = bf16[256,256]{1,0:T(8,128)(2,1)S(1)} collective-permute-done((bf16[256,256]{1,0:T(8,128)(2,1)S(1)}, bf16[256,256]{1,0:T(8,128)(2,1)S(1)}, u32[]{:S(2)}, u32[]{:S(2)}) %collective-permute-start.14) | collective-permute-done | bytes 131104 | tf_op jit(solution)/shard_map/ppermute | solution.py:23
  36.3 1.2 %last.1 = (f32[256,256]{1,0:T(8,128)}, bf16[1024,256]{1,0:T(8,128)(2,1)}) custom-call(bf16[256,5120]{1,0:T(8,128)(2,1)S(1)} %copy-done, s32[256,640]{1,0:T(8,128)S(1)} %copy-done.1, bf16[256,256]{1,0:T(8,128)(2,1)S(1)} %collective-permute-done.14.block, f32[256,256]{1,0:T(8,128)S(1)} %get-tuple-element.74.frames, ...), custom_call_target="tpu_custom_call", output_to_operand_aliasing={{1}: (5, {})} | custom-call | flops 200000000 | tf_op jit(solution)/shard_map/last/pallas_call | solution.py:40
  (36 shorter events, 6.7 us)
Async XLA Ops:
  0.6 2.5 %copy-start.1 = (s32[256,640]{1,0:T(8,128)S(1)}, s32[256,640]{1,0:T(8,128)}, u32[]{:S(2)}) copy-start(s32[256,640]{1,0:T(8,128)} %bits.35) | copy-start | bytes 1966084
  0.6 2.5 %copy-start.2 = (bf16[1024,256]{1,0:T(8,128)(2,1)S(1)}, bf16[1024,256]{1,0:T(8,128)(2,1)}, u32[]{:S(2)}) copy-start(bf16[1024,256]{1,0:T(8,128)(2,1)} %refs_0_.1) | copy-start | bytes 1572868
  0.7 2.5 %copy-start.3 = (f32[256,256]{1,0:T(8,128)S(1)}, f32[256,256]{1,0:T(8,128)}, u32[]{:S(2)}) copy-start(f32[256,256]{1,0:T(8,128)} %frames.3) | copy-start | bytes 786436
  0.7 2.4 %copy-start = (bf16[256,5120]{1,0:T(8,128)(2,1)S(1)}, bf16[256,5120]{1,0:T(8,128)(2,1)}, u32[]{:S(2)}) copy-start(bf16[256,5120]{1,0:T(8,128)(2,1)} %wanted.15) | copy-start | bytes 7864324
  0.7 8.3 %collective-permute-start.2 = (bf16[512,256]{1,0:T(8,128)(2,1)S(1)}, bf16[512,256]{1,0:T(8,128)(2,1)S(1)}, u32[]{:S(2)}, u32[]{:S(2)}) collective-permute-start(bf16[512,256]{1,0:T(8,128)(2,1)S(1)} %get-tuple-element.50), channel_id=1, source_target_pairs={{0,8},{8,16},{16,24},{24,0},{1,9},{9,17},{17,25},{25,1},{2,10},{10... | collective-permute-start | bytes 786440 | tf_op jit(solution)/shard_map/ppermute | solution.py:23
  3.9 3.8 %collective-permute-start.4 = (bf16[256,256]{1,0:T(8,128)(2,1)S(1)}, bf16[256,256]{1,0:T(8,128)(2,1)S(1)}, u32[]{:S(2)}, u32[]{:S(2)}) collective-permute-start(bf16[256,256]{1,0:T(8,128)(2,1)S(1)} %get-tuple-element.52), channel_id=1, source_target_pairs={{0,8},{8,0},{16,24},{24,16},{1,9},{9,1},{17,25},{25,17},{2,10},{10... | collective-permute-start | bytes 393224 | tf_op jit(solution)/shard_map/ppermute | solution.py:28
  4.5 3.8 %collective-permute-start.3 = (bf16[256,256]{1,0:T(8,128)(2,1)S(1)}, bf16[256,256]{1,0:T(8,128)(2,1)S(1)}, u32[]{:S(2)}, u32[]{:S(2)}) collective-permute-start(bf16[256,256]{1,0:T(8,128)(2,1)S(1)} %get-tuple-element.51), channel_id=1, source_target_pairs={{0,8},{8,0},{16,24},{24,16},{1,9},{9,1},{17,25},{25,17},{2,10},{10... | collective-permute-start | bytes 393224 | tf_op jit(solution)/shard_map/ppermute | solution.py:28
  4.6 5.9 %collective-permute-start.1 = (bf16[256,256]{1,0:T(8,128)(2,1)S(1)}, bf16[256,256]{1,0:T(8,128)(2,1)S(1)}, u32[]{:S(2)}, u32[]{:S(2)}) collective-permute-start(bf16[256,256]{1,0:T(8,128)(2,1)S(1)} %get-tuple-element.49), channel_id=1, source_target_pairs={{0,8},{8,16},{16,24},{24,0},{1,9},{9,17},{17,25},{25,1},{2,10},{10... | collective-permute-start | bytes 393224 | tf_op jit(solution)/shard_map/ppermute | solution.py:23
  5.6 6.3 %collective-permute-start = (bf16[256,256]{1,0:T(8,128)(2,1)S(1)}, bf16[256,256]{1,0:T(8,128)(2,1)S(1)}, u32[]{:S(2)}, u32[]{:S(2)}) collective-permute-start(bf16[256,256]{1,0:T(8,128)(2,1)S(1)} %get-tuple-element.48), channel_id=1, source_target_pairs={{0,8},{8,16},{16,24},{24,0},{1,9},{9,17},{17,25},{25,1},{2,10},{10... | collective-permute-start | bytes 393224 | tf_op jit(solution)/shard_map/ppermute | solution.py:23
  7.7 5.6 %collective-permute-start.8 = (bf16[256,256]{1,0:T(8,128)(2,1)S(1)}, bf16[256,256]{1,0:T(8,128)(2,1)S(1)}, u32[]{:S(2)}, u32[]{:S(2)}) collective-permute-start(bf16[256,256]{1,0:T(8,128)(2,1)S(1)} %get-tuple-element.60), channel_id=1, source_target_pairs={{0,8},{8,16},{16,24},{24,0},{1,9},{9,17},{17,25},{25,1},{2,10},{10... | collective-permute-start | bytes 393224 | tf_op jit(solution)/shard_map/ppermute | solution.py:23
  9.7 3.6 %collective-permute-start.9 = (bf16[256,256]{1,0:T(8,128)(2,1)S(1)}, bf16[256,256]{1,0:T(8,128)(2,1)S(1)}, u32[]{:S(2)}, u32[]{:S(2)}) collective-permute-start(bf16[256,256]{1,0:T(8,128)(2,1)S(1)} %get-tuple-element.61), channel_id=1, source_target_pairs={{0,8},{8,0},{16,24},{24,16},{1,9},{9,1},{17,25},{25,17},{2,10},{10... | collective-permute-start | bytes 393224 | tf_op jit(solution)/shard_map/ppermute | solution.py:28
  9.7 5.0 %collective-permute-start.7 = (bf16[256,256]{1,0:T(8,128)(2,1)S(1)}, bf16[256,256]{1,0:T(8,128)(2,1)S(1)}, u32[]{:S(2)}, u32[]{:S(2)}) collective-permute-start(bf16[256,256]{1,0:T(8,128)(2,1)S(1)} %get-tuple-element.59), channel_id=1, source_target_pairs={{0,8},{8,16},{16,24},{24,0},{1,9},{9,17},{17,25},{25,1},{2,10},{10... | collective-permute-start | bytes 393224 | tf_op jit(solution)/shard_map/ppermute | solution.py:23
  11.0 5.1 %collective-permute-start.6 = (bf16[256,256]{1,0:T(8,128)(2,1)S(1)}, bf16[256,256]{1,0:T(8,128)(2,1)S(1)}, u32[]{:S(2)}, u32[]{:S(2)}) collective-permute-start(bf16[256,256]{1,0:T(8,128)(2,1)S(1)} %get-tuple-element.58), channel_id=1, source_target_pairs={{0,8},{8,16},{16,24},{24,0},{1,9},{9,17},{17,25},{25,1},{2,10},{10... | collective-permute-start | bytes 393224 | tf_op jit(solution)/shard_map/ppermute | solution.py:23
  12.4 5.1 %collective-permute-start.5 = (bf16[256,256]{1,0:T(8,128)(2,1)S(1)}, bf16[256,256]{1,0:T(8,128)(2,1)S(1)}, u32[]{:S(2)}, u32[]{:S(2)}) collective-permute-start(bf16[256,256]{1,0:T(8,128)(2,1)S(1)} %get-tuple-element.57), channel_id=1, source_target_pairs={{0,8},{8,16},{16,24},{24,0},{1,9},{9,17},{17,25},{25,1},{2,10},{10... | collective-permute-start | bytes 393224 | tf_op jit(solution)/shard_map/ppermute | solution.py:23
  13.8 5.1 %collective-permute-start.13 = (bf16[256,256]{1,0:T(8,128)(2,1)S(1)}, bf16[256,256]{1,0:T(8,128)(2,1)S(1)}, u32[]{:S(2)}, u32[]{:S(2)}) collective-permute-start(bf16[256,256]{1,0:T(8,128)(2,1)S(1)} %get-tuple-element.69), channel_id=1, source_target_pairs={{0,8},{8,16},{16,24},{24,0},{1,9},{9,17},{17,25},{25,1},{2,10},{10... | collective-permute-start | bytes 393224 | tf_op jit(solution)/shard_map/ppermute | solution.py:23
  15.2 5.9 %collective-permute-start.12 = (bf16[256,256]{1,0:T(8,128)(2,1)S(1)}, bf16[256,256]{1,0:T(8,128)(2,1)S(1)}, u32[]{:S(2)}, u32[]{:S(2)}) collective-permute-start(bf16[256,256]{1,0:T(8,128)(2,1)S(1)} %get-tuple-element.68), channel_id=1, source_target_pairs={{0,8},{8,16},{16,24},{24,0},{1,9},{9,17},{17,25},{25,1},{2,10},{10... | collective-permute-start | bytes 393224 | tf_op jit(solution)/shard_map/ppermute | solution.py:23
  16.6 6.6 %collective-permute-start.11 = (bf16[256,256]{1,0:T(8,128)(2,1)S(1)}, bf16[256,256]{1,0:T(8,128)(2,1)S(1)}, u32[]{:S(2)}, u32[]{:S(2)}) collective-permute-start(bf16[256,256]{1,0:T(8,128)(2,1)S(1)} %get-tuple-element.67), channel_id=1, source_target_pairs={{0,8},{8,16},{16,24},{24,0},{1,9},{9,17},{17,25},{25,1},{2,10},{10... | collective-permute-start | bytes 393224 | tf_op jit(solution)/shard_map/ppermute | solution.py:23
  18.1 7.4 %collective-permute-start.10 = (bf16[256,256]{1,0:T(8,128)(2,1)S(1)}, bf16[256,256]{1,0:T(8,128)(2,1)S(1)}, u32[]{:S(2)}, u32[]{:S(2)}) collective-permute-start(bf16[256,256]{1,0:T(8,128)(2,1)S(1)} %get-tuple-element.66), channel_id=1, source_target_pairs={{0,8},{8,16},{16,24},{24,0},{1,9},{9,17},{17,25},{25,1},{2,10},{10... | collective-permute-start | bytes 393224 | tf_op jit(solution)/shard_map/ppermute | solution.py:23
  19.4 9.1 %collective-permute-start.17 = (bf16[256,256]{1,0:T(8,128)(2,1)S(1)}, bf16[256,256]{1,0:T(8,128)(2,1)S(1)}, u32[]{:S(2)}, u32[]{:S(2)}) collective-permute-start(bf16[256,256]{1,0:T(8,128)(2,1)S(1)} %get-tuple-element.77), channel_id=1, source_target_pairs={{0,1},{1,2},{2,3},{3,4},{4,5},{5,6},{6,7},{7,0},{8,9},{9,10},{10,1... | collective-permute-start | bytes 393224 | tf_op jit(solution)/shard_map/ppermute | solution.py:23
  21.7 9.5 %collective-permute-start.16 = (bf16[256,256]{1,0:T(8,128)(2,1)S(1)}, bf16[256,256]{1,0:T(8,128)(2,1)S(1)}, u32[]{:S(2)}, u32[]{:S(2)}) collective-permute-start(bf16[256,256]{1,0:T(8,128)(2,1)S(1)} %get-tuple-element.76), channel_id=1, source_target_pairs={{0,1},{1,2},{2,3},{3,4},{4,5},{5,6},{6,7},{7,0},{8,9},{9,10},{10,1... | collective-permute-start | bytes 393224 | tf_op jit(solution)/shard_map/ppermute | solution.py:23
  23.9 10.2 %collective-permute-start.15 = (bf16[256,256]{1,0:T(8,128)(2,1)S(1)}, bf16[256,256]{1,0:T(8,128)(2,1)S(1)}, u32[]{:S(2)}, u32[]{:S(2)}) collective-permute-start(bf16[256,256]{1,0:T(8,128)(2,1)S(1)} %get-tuple-element.75), channel_id=1, source_target_pairs={{0,1},{1,2},{2,3},{3,4},{4,5},{5,6},{6,7},{7,0},{8,9},{9,10},{10,1... | collective-permute-start | bytes 393224 | tf_op jit(solution)/shard_map/ppermute | solution.py:23
  26.0 10.3 %collective-permute-start.14 = (bf16[256,256]{1,0:T(8,128)(2,1)S(1)}, bf16[256,256]{1,0:T(8,128)(2,1)S(1)}, u32[]{:S(2)}, u32[]{:S(2)}) collective-permute-start(bf16[256,256]{1,0:T(8,128)(2,1)S(1)} %get-tuple-element.73), channel_id=1, source_target_pairs={{0,1},{1,2},{2,3},{3,4},{4,5},{5,6},{6,7},{7,0},{8,9},{9,10},{10,1... | collective-permute-start | bytes 393224 | tf_op jit(solution)/shard_map/ppermute | solution.py:23

commit v9 on v8

--- a/solution.py
+++ b/solution.py
@@ -128,7 +128,7 @@
             for copy in copies[2:]:
                 copy.wait()
             scaled[...] = clipped_rest(predicted[...], wanted[...], flags(bits, 0, early))
-            new[...] = updated(frames_low, pixels[...], scaled[...])
+            new[:early] = updated(frames_low, pixels[...], scaled[...])
 
     new, scaled = call(
         "load",
@@ -137,7 +137,7 @@
             pltpu.with_memory_space_constraint(a, pltpu.HBM)
             for a in (observed, mask_bits, frame_factors, pixel_factors)
         ],
-        [struct((early, rank)), struct((rows, early))],
+        [struct((early + 16, rank)), struct((rows, early))],
         in_specs=[HBM] * 4,
         scratch=[
             pltpu.VMEM((rows, early), LOW),
@@ -152,7 +152,7 @@
     arrived = shifted(new, "blk")
     observed0, bits, pixels, frames = observed[:, :width], mask_bits, pixel_factors, frame_factors
 
-    def middle_kernel(observed0, bits, pixels, frames, scaled, new0, new1, new, done):
+    def middle_kernel(observed0, bits, pixels, frames, scaled, new0, new, done):
         end = early + size
 
         @pl.when(is_odd())
@@ -166,19 +166,19 @@
         @pl.when(jnp.logical_not(is_odd()))
         def _():
             made, grad = tile(frames[...], pixels[:end], observed0[:, :end], flags(bits, 0, end))
-            new0[...] = made[:size]
-            new1[...] = made[size:early]
+            new0[...] = made[:early]
             new[...] = made[early:]
             done[...] = added(frames[...], None, grad)
 
-    new0, new1, new, done = call(
+    new0, new, done = call(
         "middle",
         middle_kernel,
         [observed0, bits, pixels, frames, scaled],
-        [chunk_t, chunk_t, chunk_t, frames_t],
+        [struct((early, rank)), chunk_t, frames_t],
     )
     third = shifted(new, "blk")
-    coming = [(arrived, swapped(new0), 0), (arrived, swapped(new1), size), third]
+    handed = swapped(new0)
+    coming = [None, None, third]
 
     def step(visit, chunk, block, frames, done, wanted):
         at = chunk * size
@@ -221,7 +221,7 @@
         @pl.when(is_odd())
         def _():
             new[...], grad = tile(
-                frames[...], block[...], wanted[:, width : width + size], flags(bits, width, size)
+                frames[...], block[:size], wanted[:, width : width + size], flags(bits, width, size)
             )
             done[...] = added(frames[...], None, grad)
 
@@ -230,14 +230,14 @@
         def _():
             at = width + size
             new[...], grad = tile(
-                frames[...], own[...], wanted[:, at : at + size], flags(bits, at, size)
+                frames[...], own[size:], wanted[:, at : at + size], flags(bits, at, size)
             )
             done_out[...] = added(frames[...], done[...], grad)
 
         @pl.when(jnp.logical_not(is_odd()))
         def _():
             made, grad = tile(
-                frames[...], block[...], wanted[:, width : width + early], flags(bits, width, early)
+                frames[...], block[:early], wanted[:, width : width + early], flags(bits, width, early)
             )
             new0[...] = made[:size]
             new[...] = made[size:]
@@ -266,13 +266,13 @@
 
     frames = done
     new, done = call(
-        "odd", odd_kernel, [later, bits, frames, coming[0][1]], [chunk_t, frames_t]
+        "odd", odd_kernel, [later, bits, frames, handed], [chunk_t, frames_t]
     )
     passed = shifted(new, "blk")
     new0, new, done = call(
         "both",
         both_kernel,
-        [later, bits, frames, arrived, coming[1][1], done],
+        [later, bits, frames, arrived, handed, done],
         [chunk_t, chunk_t, frames_t],
         aliases={5: 2},
     )

time: 37.6 us -> 37.4 us (level)
  starting transfers between devices: 14.5 us -> 13.4 us
  waiting for transfers between devices: 9.69 us -> 10.5 us
    ppermute x15, starting transfers between devices: 13.7 us -> 12.7 us  [shifted(): lax.ppermute(value, axis, [(s, (s + 1) % count) for s in range(count)])]
    ppermute x15, waiting for transfers between devices: 9.69 us -> 10.5 us  [shifted(): lax.ppermute(value, axis, [(s, (s + 1) % count) for s in range(count)])]
    ppermute x3 -> x2, starting transfers between devices: 0.78 us -> 0.69 us  [swapped(): lax.ppermute(value, 'blk', [(s, s + 1 - 2 * (s % 2)) for s in range(count)])]
  transfers between devices with their start and end apart: 18 -> 17, of which waited for: 12 -> 12; matrix products, arithmetic and copies ran while one was open for 0% -> 0% of each run, Pallas kernels for 30% -> 30%
where the time goes in v9:
time: 37.4 us; the launch traced here: 37.2 us
  starting transfers between devices  13.4 us (36%)
  Pallas kernels  12.4 us (33%)
  waiting for transfers between devices  10.5 us (28%)
  between operations  0.93 us (2%)
    ppermute x15, starting transfers between devices, shifted(): lax.ppermute(value, axis, [(s, (s + 1) % count) for s in range(count)])  12.7 us
    pallas_call x23, Pallas kernels, call(): pl.pallas_call(kernel, name=name, out_shape=tuple(outs), in_specs=in_spec...  12.4 us
    ppermute x15, waiting for transfers between devices, shifted(): lax.ppermute(value, axis, [(s, (s + 1) % count) for s in range(count)])  10.5 us
  transfers between devices with their start and end apart: 17, of which 12 were waited for; matrix products, arithmetic and copies ran while one was open for 0% of the time, Pallas kernels for 30%

profile of v9, /device:TPU:0, one launch (start us, length us, event | category | flops | bytes accessed | tf_op | source)
XLA Modules:
  0.0 37.2 jit_solution(14934954779746903193)
XLA Ops:
  0.7 2.4 %collective-permute-start.2 = (bf16[528,256]{1,0:T(8,128)(2,1)S(1)}, bf16[528,256]{1,0:T(8,128)(2,1)S(1)}, u32[]{:S(2)}, u32[]{:S(2)}) collective-permute-start(bf16[528,256]{1,0:T(8,128)(2,1)S(1)} %get-tuple-element.49), channel_id=1, source_target_pairs={{0,8},{8,16},{16,24},{24,0},{1,9},{9,17},{17,25},{25,1},{2,10},{10... | collective-permute-start | bytes 811016 | tf_op jit(solution)/shard_map/ppermute | solution.py:23
  3.2 0.7 %middle.1 = (bf16[512,256]{1,0:T(8,128)(2,1)S(1)}, bf16[256,256]{1,0:T(8,128)(2,1)S(1)}, f32[256,256]{1,0:T(8,128)S(1)}) custom-call(bf16[256,1024]{1,0:T(8,128)(2,1)S(1)} %slice.3.observed0.wanted, s32[256,640]{1,0:T(8,128)S(1)} %copy-done.1, bf16[1024,256]{1,0:T(8,128)(2,1)S(1)} %copy-done.2, f32[256,256]{1,0:T(8,128)S(1)} %copy-done.3, ...), custom_call_target="tpu_custom_call" | custom-call | tf_op jit(solution)/shard_map/middle/pallas_call | solution.py:40
  3.9 0.6 %collective-permute-start.3 = (bf16[512,256]{1,0:T(8,128)(2,1)S(1)}, bf16[512,256]{1,0:T(8,128)(2,1)S(1)}, u32[]{:S(2)}, u32[]{:S(2)}) collective-permute-start(bf16[512,256]{1,0:T(8,128)(2,1)S(1)} %get-tuple-element.50), channel_id=1, source_target_pairs={{0,8},{8,0},{16,24},{24,16},{1,9},{9,1},{17,25},{25,17},{2,10},{10... | collective-permute-start | bytes 786440 | tf_op jit(solution)/shard_map/ppermute | solution.py:28
  5.1 2.1 %collective-permute-start = (bf16[256,256]{1,0:T(8,128)(2,1)S(1)}, bf16[256,256]{1,0:T(8,128)(2,1)S(1)}, u32[]{:S(2)}, u32[]{:S(2)}) collective-permute-start(bf16[256,256]{1,0:T(8,128)(2,1)S(1)} %get-tuple-element.47), channel_id=1, source_target_pairs={{0,8},{8,16},{16,24},{24,0},{1,9},{9,17},{17,25},{25,1},{2,10},{10... | collective-permute-start | bytes 393224 | tf_op jit(solution)/shard_map/ppermute | solution.py:23
  7.2 1.0 %collective-permute-start.7 = (bf16[256,256]{1,0:T(8,128)(2,1)S(1)}, bf16[256,256]{1,0:T(8,128)(2,1)S(1)}, u32[]{:S(2)}, u32[]{:S(2)}) collective-permute-start(bf16[256,256]{1,0:T(8,128)(2,1)S(1)} %get-tuple-element.58), channel_id=1, source_target_pairs={{0,8},{8,16},{16,24},{24,0},{1,9},{9,17},{17,25},{25,1},{2,10},{10... | collective-permute-start | bytes 393224 | tf_op jit(solution)/shard_map/ppermute | solution.py:23
  8.3 0.9 %collective-permute-done.2.block = bf16[528,256]{1,0:T(8,128)(2,1)S(1)} collective-permute-done((bf16[528,256]{1,0:T(8,128)(2,1)S(1)}, bf16[528,256]{1,0:T(8,128)(2,1)S(1)}, u32[]{:S(2)}, u32[]{:S(2)}) %collective-permute-start.2) | collective-permute-done | bytes 270368 | tf_op jit(solution)/shard_map/ppermute | solution.py:23
  9.2 0.6 %both.1 = (bf16[256,256]{1,0:T(8,128)(2,1)S(1)}, bf16[256,256]{1,0:T(8,128)(2,1)S(1)}, f32[256,256]{1,0:T(8,128)S(1)}) custom-call(bf16[256,5120]{1,0:T(8,128)(2,1)S(1)} %copy-done, s32[256,640]{1,0:T(8,128)S(1)} %copy-done.1, f32[256,256]{1,0:T(8,128)S(1)} %get-tuple-element.46.frames, ...), custom_call_target="tpu_custom_call", output_to_operand_aliasing={{2}: (5, {})} | custom-call | tf_op jit(solution)/shard_map/both/pallas_call | solution.py:40
  11.2 0.8 %collective-permute-done.refs_0_ = bf16[256,256]{1,0:T(8,128)(2,1)S(1)} collective-permute-done((bf16[256,256]{1,0:T(8,128)(2,1)S(1)}, bf16[256,256]{1,0:T(8,128)(2,1)S(1)}, u32[]{:S(2)}, u32[]{:S(2)}) %collective-permute-start) | collective-permute-done | bytes 131104 | tf_op jit(solution)/shard_map/ppermute | solution.py:23
  12.0 0.6 %step.15 = (bf16[256,256]{1,0:T(8,128)(2,1)S(1)}, f32[256,256]{1,0:T(8,128)S(1)}) custom-call(bf16[256,5120]{1,0:T(8,128)(2,1)S(1)} %copy-done, s32[256,640]{1,0:T(8,128)S(1)} %copy-done.1, f32[256,256]{1,0:T(8,128)S(1)} %get-tuple-element.46.frames, bf16[256,256]{1,0:T(8,128)(2,1)S(1)} %collective-permute-done.refs_0_, ...), custom_call_target="tpu_custom_call", output_to_operand_aliasing={{1}: (4, {})} | custom-call | tf_op jit(solution)/shard_map/step/pallas_call | solution.py:40
  12.6 0.8 %collective-permute-done.7.refs_0_ = bf16[256,256]{1,0:T(8,128)(2,1)S(1)} collective-permute-done((bf16[256,256]{1,0:T(8,128)(2,1)S(1)}, bf16[256,256]{1,0:T(8,128)(2,1)S(1)}, u32[]{:S(2)}, u32[]{:S(2)}) %collective-permute-start.7) | collective-permute-done | bytes 131104 | tf_op jit(solution)/shard_map/ppermute | solution.py:23
  13.4 0.6 %step.16 = (bf16[256,256]{1,0:T(8,128)(2,1)S(1)}, f32[256,256]{1,0:T(8,128)S(1)}) custom-call(bf16[256,5120]{1,0:T(8,128)(2,1)S(1)} %copy-done, s32[256,640]{1,0:T(8,128)S(1)} %copy-done.1, f32[256,256]{1,0:T(8,128)S(1)} %get-tuple-element.54.frames, bf16[256,256]{1,0:T(8,128)(2,1)S(1)} %collective-permute-done.7.refs_0_, ...), custom_call_target="tpu_custom_call" | custom-call | tf_op jit(solution)/shard_map/step/pallas_call | solution.py:40
  14.0 0.8 %collective-permute-done.6.refs_0_ = bf16[256,256]{1,0:T(8,128)(2,1)S(1)} collective-permute-done((bf16[256,256]{1,0:T(8,128)(2,1)S(1)}, bf16[256,256]{1,0:T(8,128)(2,1)S(1)}, u32[]{:S(2)}, u32[]{:S(2)}) %collective-permute-start.6) | collective-permute-done | bytes 131104 | tf_op jit(solution)/shard_map/ppermute | solution.py:23
  15.4 0.8 %collective-permute-done.5.refs_0_ = bf16[256,256]{1,0:T(8,128)(2,1)S(1)} collective-permute-done((bf16[256,256]{1,0:T(8,128)(2,1)S(1)}, bf16[256,256]{1,0:T(8,128)(2,1)S(1)}, u32[]{:S(2)}, u32[]{:S(2)}) %collective-permute-start.5) | collective-permute-done | bytes 131104 | tf_op jit(solution)/shard_map/ppermute | solution.py:23
  16.8 0.8 %collective-permute-done.4.refs_0_ = bf16[256,256]{1,0:T(8,128)(2,1)S(1)} collective-permute-done((bf16[256,256]{1,0:T(8,128)(2,1)S(1)}, bf16[256,256]{1,0:T(8,128)(2,1)S(1)}, u32[]{:S(2)}, u32[]{:S(2)}) %collective-permute-start.4) | collective-permute-done | bytes 131104 | tf_op jit(solution)/shard_map/ppermute | solution.py:23
  17.6 0.6 %step.19 = (bf16[256,256]{1,0:T(8,128)(2,1)S(1)}, f32[256,256]{1,0:T(8,128)S(1)}) custom-call(bf16[256,5120]{1,0:T(8,128)(2,1)S(1)} %copy-done, s32[256,640]{1,0:T(8,128)S(1)} %copy-done.1, f32[256,256]{1,0:T(8,128)S(1)} %get-tuple-element.54.frames, bf16[256,256]{1,0:T(8,128)(2,1)S(1)} %collective-permute-done.4.refs_0_, ...), custom_call_target="tpu_custom_call", output_to_operand_aliasing={{1}: (4, {})} | custom-call | tf_op jit(solution)/shard_map/step/pallas_call | solution.py:40
  18.2 0.8 %collective-permute-done.12.block = bf16[256,256]{1,0:T(8,128)(2,1)S(1)} collective-permute-done((bf16[256,256]{1,0:T(8,128)(2,1)S(1)}, bf16[256,256]{1,0:T(8,128)(2,1)S(1)}, u32[]{:S(2)}, u32[]{:S(2)}) %collective-permute-start.12) | collective-permute-done | bytes 131104 | tf_op jit(solution)/shard_map/ppermute | solution.py:23
  19.5 1.6 %collective-permute-start.16 = (bf16[256,256]{1,0:T(8,128)(2,1)S(1)}, bf16[256,256]{1,0:T(8,128)(2,1)S(1)}, u32[]{:S(2)}, u32[]{:S(2)}) collective-permute-start(bf16[256,256]{1,0:T(8,128)(2,1)S(1)} %get-tuple-element.75), channel_id=1, source_target_pairs={{0,1},{1,2},{2,3},{3,4},{4,5},{5,6},{6,7},{7,0},{8,9},{9,10},{10,1... | collective-permute-start | bytes 393224 | tf_op jit(solution)/shard_map/ppermute | solution.py:23
  21.2 0.6 %step.20 = (bf16[256,256]{1,0:T(8,128)(2,1)S(1)}, f32[256,256]{1,0:T(8,128)S(1)}) custom-call(bf16[256,5120]{1,0:T(8,128)(2,1)S(1)} %copy-done, s32[256,640]{1,0:T(8,128)S(1)} %copy-done.1, f32[256,256]{1,0:T(8,128)S(1)} %get-tuple-element.63.frames, bf16[256,256]{1,0:T(8,128)(2,1)S(1)} %collective-permute-done.11.refs_0_, ...), custom_call_target="tpu_custom_call", output_to_operand_aliasing={{1}: (4, {})} | custom-call | tf_op jit(solution)/shard_map/step/pallas_call | solution.py:40
  21.8 1.6 %collective-permute-start.15 = (bf16[256,256]{1,0:T(8,128)(2,1)S(1)}, bf16[256,256]{1,0:T(8,128)(2,1)S(1)}, u32[]{:S(2)}, u32[]{:S(2)}) collective-permute-start(bf16[256,256]{1,0:T(8,128)(2,1)S(1)} %get-tuple-element.74), channel_id=1, source_target_pairs={{0,1},{1,2},{2,3},{3,4},{4,5},{5,6},{6,7},{7,0},{8,9},{9,10},{10,1... | collective-permute-start | bytes 393224 | tf_op jit(solution)/shard_map/ppermute | solution.py:23
  23.4 0.6 %step.21 = (bf16[256,256]{1,0:T(8,128)(2,1)S(1)}, f32[256,256]{1,0:T(8,128)S(1)}) custom-call(bf16[256,5120]{1,0:T(8,128)(2,1)S(1)} %copy-done, s32[256,640]{1,0:T(8,128)S(1)} %copy-done.1, f32[256,256]{1,0:T(8,128)S(1)} %get-tuple-element.63.frames, bf16[256,256]{1,0:T(8,128)(2,1)S(1)} %collective-permute-done.10.refs_0_, ...), custom_call_target="tpu_custom_call", output_to_operand_aliasing={{1}: (4, {})} | custom-call | tf_op jit(solution)/shard_map/step/pallas_call | solution.py:40
  23.9 1.6 %collective-permute-start.14 = (bf16[256,256]{1,0:T(8,128)(2,1)S(1)}, bf16[256,256]{1,0:T(8,128)(2,1)S(1)}, u32[]{:S(2)}, u32[]{:S(2)}) collective-permute-start(bf16[256,256]{1,0:T(8,128)(2,1)S(1)} %get-tuple-element.73), channel_id=1, source_target_pairs={{0,1},{1,2},{2,3},{3,4},{4,5},{5,6},{6,7},{7,0},{8,9},{9,10},{10,1... | collective-permute-start | bytes 393224 | tf_op jit(solution)/shard_map/ppermute | solution.py:23
  25.5 0.6 %step.22 = (bf16[256,256]{1,0:T(8,128)(2,1)S(1)}, f32[256,256]{1,0:T(8,128)S(1)}) custom-call(bf16[256,5120]{1,0:T(8,128)(2,1)S(1)} %copy-done, s32[256,640]{1,0:T(8,128)S(1)} %copy-done.1, f32[256,256]{1,0:T(8,128)S(1)} %get-tuple-element.63.frames, bf16[256,256]{1,0:T(8,128)(2,1)S(1)} %collective-permute-done.9.refs_0_, ...), custom_call_target="tpu_custom_call", output_to_operand_aliasing={{1}: (4, {})} | custom-call | tf_op jit(solution)/shard_map/step/pallas_call | solution.py:40
  26.1 1.6 %collective-permute-start.13 = (bf16[256,256]{1,0:T(8,128)(2,1)S(1)}, bf16[256,256]{1,0:T(8,128)(2,1)S(1)}, u32[]{:S(2)}, u32[]{:S(2)}) collective-permute-start(bf16[256,256]{1,0:T(8,128)(2,1)S(1)} %get-tuple-element.71), channel_id=1, source_target_pairs={{0,1},{1,2},{2,3},{3,4},{4,5},{5,6},{6,7},{7,0},{8,9},{9,10},{10,1... | collective-permute-start | bytes 393224 | tf_op jit(solution)/shard_map/ppermute | solution.py:23
  27.7 0.9 %collective-permute-done.16.refs_0_ = bf16[256,256]{1,0:T(8,128)(2,1)S(1)} collective-permute-done((bf16[256,256]{1,0:T(8,128)(2,1)S(1)}, bf16[256,256]{1,0:T(8,128)(2,1)S(1)}, u32[]{:S(2)}, u32[]{:S(2)}) %collective-permute-start.16) | collective-permute-done | bytes 131104 | tf_op jit(solution)/shard_map/ppermute | solution.py:23
  29.1 0.7 %write.3.refs_0_ = bf16[1024,256]{1,0:T(8,128)(2,1)} custom-call(bf16[256,256]{1,0:T(8,128)(2,1)S(1)} %get-tuple-element.81.new), custom_call_target="tpu_custom_call" | custom-call | flops 200000000 | tf_op jit(solution)/shard_map/write/pallas_call | solution.py:40
  29.7 1.6 %collective-permute-done.15.refs_0_ = bf16[256,256]{1,0:T(8,128)(2,1)S(1)} collective-permute-done((bf16[256,256]{1,0:T(8,128)(2,1)S(1)}, bf16[256,256]{1,0:T(8,128)(2,1)S(1)}, u32[]{:S(2)}, u32[]{:S(2)}) %collective-permute-start.15) | collective-permute-done | bytes 131104 | tf_op jit(solution)/shard_map/ppermute | solution.py:23
  31.3 0.6 %step.24 = (bf16[256,256]{1,0:T(8,128)(2,1)S(1)}, f32[256,256]{1,0:T(8,128)S(1)}) custom-call(bf16[256,5120]{1,0:T(8,128)(2,1)S(1)} %copy-done, s32[256,640]{1,0:T(8,128)S(1)} %copy-done.1, f32[256,256]{1,0:T(8,128)S(1)} %get-tuple-element.72.frames, bf16[256,256]{1,0:T(8,128)(2,1)S(1)} %collective-permute-done.15.refs_0_, ...), custom_call_target="tpu_custom_call", output_to_operand_aliasing={{1}: (4, {})} | custom-call | flops 200000000 | tf_op jit(solution)/shard_map/step/pallas_call | solution.py:40
  31.9 0.7 %write.4.refs_0_ = bf16[1024,256]{1,0:T(8,128)(2,1)} custom-call(bf16[256,256]{1,0:T(8,128)(2,1)S(1)} %get-tuple-element.80.new, bf16[1024,256]{1,0:T(8,128)(2,1)} %write.3.refs_0_), custom_call_target="tpu_custom_call", output_to_operand_aliasing={{}: (1, {})} | custom-call | flops 200000000 | tf_op jit(solution)/shard_map/write/pallas_call | solution.py:40
  32.6 1.6 %collective-permute-done.14.refs_0_ = bf16[256,256]{1,0:T(8,128)(2,1)S(1)} collective-permute-done((bf16[256,256]{1,0:T(8,128)(2,1)S(1)}, bf16[256,256]{1,0:T(8,128)(2,1)S(1)}, u32[]{:S(2)}, u32[]{:S(2)}) %collective-permute-start.14) | collective-permute-done | bytes 131104 | tf_op jit(solution)/shard_map/ppermute | solution.py:23
  34.7 0.7 %write.5.written = bf16[1024,256]{1,0:T(8,128)(2,1)} custom-call(bf16[256,256]{1,0:T(8,128)(2,1)S(1)} %get-tuple-element.79.new, bf16[1024,256]{1,0:T(8,128)(2,1)} %write.4.refs_0_), custom_call_target="tpu_custom_call", output_to_operand_aliasing={{}: (1, {})} | custom-call | flops 200000000 | tf_op jit(solution)/shard_map/write/pallas_call | solution.py:40
  35.4 0.7 %collective-permute-done.13.block = bf16[256,256]{1,0:T(8,128)(2,1)S(1)} collective-permute-done((bf16[256,256]{1,0:T(8,128)(2,1)S(1)}, bf16[256,256]{1,0:T(8,128)(2,1)S(1)}, u32[]{:S(2)}, u32[]{:S(2)}) %collective-permute-start.13) | collective-permute-done | bytes 131104 | tf_op jit(solution)/shard_map/ppermute | solution.py:23
  36.1 1.2 %last.1 = (f32[256,256]{1,0:T(8,128)}, bf16[1024,256]{1,0:T(8,128)(2,1)}) custom-call(bf16[256,5120]{1,0:T(8,128)(2,1)S(1)} %copy-done, s32[256,640]{1,0:T(8,128)S(1)} %copy-done.1, bf16[256,256]{1,0:T(8,128)(2,1)S(1)} %collective-permute-done.13.block, f32[256,256]{1,0:T(8,128)S(1)} %get-tuple-element.72.frames, ...), custom_call_target="tpu_custom_call", output_to_operand_aliasing={{1}: (5, {})} | custom-call | flops 200000000 | tf_op jit(solution)/shard_map/last/pallas_call | solution.py:40
  (34 shorter events, 5.3 us)
Async XLA Ops:
  0.6 2.5 %copy-start.1 = (s32[256,640]{1,0:T(8,128)S(1)}, s32[256,640]{1,0:T(8,128)}, u32[]{:S(2)}) copy-start(s32[256,640]{1,0:T(8,128)} %bits.35) | copy-start | bytes 1966084
  0.6 2.5 %copy-start.2 = (bf16[1024,256]{1,0:T(8,128)(2,1)S(1)}, bf16[1024,256]{1,0:T(8,128)(2,1)}, u32[]{:S(2)}) copy-start(bf16[1024,256]{1,0:T(8,128)(2,1)} %refs_0_.1) | copy-start | bytes 1572868
  0.7 2.5 %copy-start.3 = (f32[256,256]{1,0:T(8,128)S(1)}, f32[256,256]{1,0:T(8,128)}, u32[]{:S(2)}) copy-start(f32[256,256]{1,0:T(8,128)} %frames.3) | copy-start | bytes 786436
  0.7 2.4 %copy-start = (bf16[256,5120]{1,0:T(8,128)(2,1)S(1)}, bf16[256,5120]{1,0:T(8,128)(2,1)}, u32[]{:S(2)}) copy-start(bf16[256,5120]{1,0:T(8,128)(2,1)} %wanted.15) | copy-start | bytes 7864324
  0.7 8.4 %collective-permute-start.2 = (bf16[528,256]{1,0:T(8,128)(2,1)S(1)}, bf16[528,256]{1,0:T(8,128)(2,1)S(1)}, u32[]{:S(2)}, u32[]{:S(2)}) collective-permute-start(bf16[528,256]{1,0:T(8,128)(2,1)S(1)} %get-tuple-element.49), channel_id=1, source_target_pairs={{0,8},{8,16},{16,24},{24,0},{1,9},{9,17},{17,25},{25,1},{2,10},{10... | collective-permute-start | bytes 811016 | tf_op jit(solution)/shard_map/ppermute | solution.py:23
  3.9 3.3 %collective-permute-start.3 = (bf16[512,256]{1,0:T(8,128)(2,1)S(1)}, bf16[512,256]{1,0:T(8,128)(2,1)S(1)}, u32[]{:S(2)}, u32[]{:S(2)}) collective-permute-start(bf16[512,256]{1,0:T(8,128)(2,1)S(1)} %get-tuple-element.50), channel_id=1, source_target_pairs={{0,8},{8,0},{16,24},{24,16},{1,9},{9,1},{17,25},{25,17},{2,10},{10... | collective-permute-start | bytes 786440 | tf_op jit(solution)/shard_map/ppermute | solution.py:28
  4.5 6.0 %collective-permute-start.1 = (bf16[256,256]{1,0:T(8,128)(2,1)S(1)}, bf16[256,256]{1,0:T(8,128)(2,1)S(1)}, u32[]{:S(2)}, u32[]{:S(2)}) collective-permute-start(bf16[256,256]{1,0:T(8,128)(2,1)S(1)} %get-tuple-element.48), channel_id=1, source_target_pairs={{0,8},{8,16},{16,24},{24,0},{1,9},{9,17},{17,25},{25,1},{2,10},{10... | collective-permute-start | bytes 393224 | tf_op jit(solution)/shard_map/ppermute | solution.py:23
  5.1 6.8 %collective-permute-start = (bf16[256,256]{1,0:T(8,128)(2,1)S(1)}, bf16[256,256]{1,0:T(8,128)(2,1)S(1)}, u32[]{:S(2)}, u32[]{:S(2)}) collective-permute-start(bf16[256,256]{1,0:T(8,128)(2,1)S(1)} %get-tuple-element.47), channel_id=1, source_target_pairs={{0,8},{8,16},{16,24},{24,0},{1,9},{9,17},{17,25},{25,1},{2,10},{10... | collective-permute-start | bytes 393224 | tf_op jit(solution)/shard_map/ppermute | solution.py:23
  7.2 6.1 %collective-permute-start.7 = (bf16[256,256]{1,0:T(8,128)(2,1)S(1)}, bf16[256,256]{1,0:T(8,128)(2,1)S(1)}, u32[]{:S(2)}, u32[]{:S(2)}) collective-permute-start(bf16[256,256]{1,0:T(8,128)(2,1)S(1)} %get-tuple-element.58), channel_id=1, source_target_pairs={{0,8},{8,16},{16,24},{24,0},{1,9},{9,17},{17,25},{25,1},{2,10},{10... | collective-permute-start | bytes 393224 | tf_op jit(solution)/shard_map/ppermute | solution.py:23
  9.7 3.6 %collective-permute-start.8 = (bf16[256,256]{1,0:T(8,128)(2,1)S(1)}, bf16[256,256]{1,0:T(8,128)(2,1)S(1)}, u32[]{:S(2)}, u32[]{:S(2)}) collective-permute-start(bf16[256,256]{1,0:T(8,128)(2,1)S(1)} %get-tuple-element.59), channel_id=1, source_target_pairs={{0,8},{8,0},{16,24},{24,16},{1,9},{9,1},{17,25},{25,17},{2,10},{10... | collective-permute-start | bytes 393224 | tf_op jit(solution)/shard_map/ppermute | solution.py:28
  9.8 5.0 %collective-permute-start.6 = (bf16[256,256]{1,0:T(8,128)(2,1)S(1)}, bf16[256,256]{1,0:T(8,128)(2,1)S(1)}, u32[]{:S(2)}, u32[]{:S(2)}) collective-permute-start(bf16[256,256]{1,0:T(8,128)(2,1)S(1)} %get-tuple-element.57), channel_id=1, source_target_pairs={{0,8},{8,16},{16,24},{24,0},{1,9},{9,17},{17,25},{25,1},{2,10},{10... | collective-permute-start | bytes 393224 | tf_op jit(solution)/shard_map/ppermute | solution.py:23
  11.1 5.1 %collective-permute-start.5 = (bf16[256,256]{1,0:T(8,128)(2,1)S(1)}, bf16[256,256]{1,0:T(8,128)(2,1)S(1)}, u32[]{:S(2)}, u32[]{:S(2)}) collective-permute-start(bf16[256,256]{1,0:T(8,128)(2,1)S(1)} %get-tuple-element.56), channel_id=1, source_target_pairs={{0,8},{8,16},{16,24},{24,0},{1,9},{9,17},{17,25},{25,1},{2,10},{10... | collective-permute-start | bytes 393224 | tf_op jit(solution)/shard_map/ppermute | solution.py:23
  12.5 5.1 %collective-permute-start.4 = (bf16[256,256]{1,0:T(8,128)(2,1)S(1)}, bf16[256,256]{1,0:T(8,128)(2,1)S(1)}, u32[]{:S(2)}, u32[]{:S(2)}) collective-permute-start(bf16[256,256]{1,0:T(8,128)(2,1)S(1)} %get-tuple-element.55), channel_id=1, source_target_pairs={{0,8},{8,16},{16,24},{24,0},{1,9},{9,17},{17,25},{25,1},{2,10},{10... | collective-permute-start | bytes 393224 | tf_op jit(solution)/shard_map/ppermute | solution.py:23
  13.9 5.0 %collective-permute-start.12 = (bf16[256,256]{1,0:T(8,128)(2,1)S(1)}, bf16[256,256]{1,0:T(8,128)(2,1)S(1)}, u32[]{:S(2)}, u32[]{:S(2)}) collective-permute-start(bf16[256,256]{1,0:T(8,128)(2,1)S(1)} %get-tuple-element.67), channel_id=1, source_target_pairs={{0,8},{8,16},{16,24},{24,0},{1,9},{9,17},{17,25},{25,1},{2,10},{10... | collective-permute-start | bytes 393224 | tf_op jit(solution)/shard_map/ppermute | solution.py:23
  15.3 5.9 %collective-permute-start.11 = (bf16[256,256]{1,0:T(8,128)(2,1)S(1)}, bf16[256,256]{1,0:T(8,128)(2,1)S(1)}, u32[]{:S(2)}, u32[]{:S(2)}) collective-permute-start(bf16[256,256]{1,0:T(8,128)(2,1)S(1)} %get-tuple-element.66), channel_id=1, source_target_pairs={{0,8},{8,16},{16,24},{24,0},{1,9},{9,17},{17,25},{25,1},{2,10},{10... | collective-permute-start | bytes 393224 | tf_op jit(solution)/shard_map/ppermute | solution.py:23
  16.7 6.6 %collective-permute-start.10 = (bf16[256,256]{1,0:T(8,128)(2,1)S(1)}, bf16[256,256]{1,0:T(8,128)(2,1)S(1)}, u32[]{:S(2)}, u32[]{:S(2)}) collective-permute-start(bf16[256,256]{1,0:T(8,128)(2,1)S(1)} %get-tuple-element.65), channel_id=1, source_target_pairs={{0,8},{8,16},{16,24},{24,0},{1,9},{9,17},{17,25},{25,1},{2,10},{10... | collective-permute-start | bytes 393224 | tf_op jit(solution)/shard_map/ppermute | solution.py:23
  18.1 7.4 %collective-permute-start.9 = (bf16[256,256]{1,0:T(8,128)(2,1)S(1)}, bf16[256,256]{1,0:T(8,128)(2,1)S(1)}, u32[]{:S(2)}, u32[]{:S(2)}) collective-permute-start(bf16[256,256]{1,0:T(8,128)(2,1)S(1)} %get-tuple-element.64), channel_id=1, source_target_pairs={{0,8},{8,16},{16,24},{24,0},{1,9},{9,17},{17,25},{25,1},{2,10},{10... | collective-permute-start | bytes 393224 | tf_op jit(solution)/shard_map/ppermute | solution.py:23
  19.5 9.0 %collective-permute-start.16 = (bf16[256,256]{1,0:T(8,128)(2,1)S(1)}, bf16[256,256]{1,0:T(8,128)(2,1)S(1)}, u32[]{:S(2)}, u32[]{:S(2)}) collective-permute-start(bf16[256,256]{1,0:T(8,128)(2,1)S(1)} %get-tuple-element.75), channel_id=1, source_target_pairs={{0,1},{1,2},{2,3},{3,4},{4,5},{5,6},{6,7},{7,0},{8,9},{9,10},{10,1... | collective-permute-start | bytes 393224 | tf_op jit(solution)/shard_map/ppermute | solution.py:23
  21.8 9.5 %collective-permute-start.15 = (bf16[256,256]{1,0:T(8,128)(2,1)S(1)}, bf16[256,256]{1,0:T(8,128)(2,1)S(1)}, u32[]{:S(2)}, u32[]{:S(2)}) collective-permute-start(bf16[256,256]{1,0:T(8,128)(2,1)S(1)} %get-tuple-element.74), channel_id=1, source_target_pairs={{0,1},{1,2},{2,3},{3,4},{4,5},{5,6},{6,7},{7,0},{8,9},{9,10},{10,1... | collective-permute-start | bytes 393224 | tf_op jit(solution)/shard_map/ppermute | solution.py:23
  23.9 10.2 %collective-permute-start.14 = (bf16[256,256]{1,0:T(8,128)(2,1)S(1)}, bf16[256,256]{1,0:T(8,128)(2,1)S(1)}, u32[]{:S(2)}, u32[]{:S(2)}) collective-permute-start(bf16[256,256]{1,0:T(8,128)(2,1)S(1)} %get-tuple-element.73), channel_id=1, source_target_pairs={{0,1},{1,2},{2,3},{3,4},{4,5},{5,6},{6,7},{7,0},{8,9},{9,10},{10,1... | collective-permute-start | bytes 393224 | tf_op jit(solution)/shard_map/ppermute | solution.py:23
  26.1 10.0 %collective-permute-start.13 = (bf16[256,256]{1,0:T(8,128)(2,1)S(1)}, bf16[256,256]{1,0:T(8,128)(2,1)S(1)}, u32[]{:S(2)}, u32[]{:S(2)}) collective-permute-start(bf16[256,256]{1,0:T(8,128)(2,1)S(1)} %get-tuple-element.71), channel_id=1, source_target_pairs={{0,1},{1,2},{2,3},{3,4},{4,5},{5,6},{6,7},{7,0},{8,9},{9,10},{10,1... | collective-permute-start | bytes 393224 | tf_op jit(solution)/shard_map/ppermute | solution.py:23
